TPU v7x, 32 devices: a whole 2x2x4 slice. The times are simulated.
32 devices in a mesh: patch: 16 (over z, y, x), depth: 2 (over core).
Axes of the slice: x: 2, y: 2, z: 4, core: 2. Of those that a mesh axis runs over, the one named last changes fastest.
Arguments:
- skip_features: bfloat16 [64, 64, 8, 1024], P('patch', None, 'depth'), may hold values from -12 to 12
- volume_ids: int32 [64, 8, 1024], P('patch', 'depth'), may hold values from 1 to 3, as said below
- output_grad: bfloat16 [64, 64, 8, 1024], P('patch', None, 'depth'), may hold values from -6 to 6
- widening: float32 [27, 64, 128], replicated, may hold values from -0.15625 to 0.15625
- widening_velocity: float32 [27, 64, 128], replicated, may hold values from -1536 to 1536
- widening_average: float32 [27, 64, 128], replicated, may hold values from -0.15625 to 0.15625
- bottom: float32 [27, 128, 128], replicated, may hold values from -0.109375 to 0.109375
- bottom_velocity: float32 [27, 128, 128], replicated, may hold values from -1536 to 1536
- bottom_average: float32 [27, 128, 128], replicated, may hold values from -0.109375 to 0.109375
- merging: float32 [27, 192, 64], replicated, may hold values from -0.078125 to 0.078125
- merging_velocity: float32 [27, 192, 64], replicated, may hold values from -4096 to 4096
- merging_average: float32 [27, 192, 64], replicated, may hold values from -0.078125 to 0.078125
- closing: float32 [27, 64, 64], replicated, may hold values from -0.15625 to 0.15625
- closing_velocity: float32 [27, 64, 64], replicated, may hold values from -4096 to 4096
- closing_average: float32 [27, 64, 64], replicated, may hold values from -0.15625 to 0.15625
- gating: float32 [194, 32], replicated, may hold values from -3 to 3
- gating_velocity: float32 [194, 32], replicated, may hold values from -1280 to 1280
- gating_average: float32 [194, 32], replicated, may hold values from -0.4375 to 0.4375
- scales: float32 [2, 384], replicated, may hold values from -1 to 1.5
- scales_velocity: float32 [2, 384], replicated, may hold values from -4096 to 4096
- scales_average: float32 [2, 384], replicated, may hold values from -1 to 1.5
Outputs:
- decoded: bfloat16 [64, 64, 8, 1024], P('patch', None, 'depth')
- skip_grad: float32 [64, 64, 8, 1024], P('patch', None, 'depth')
- widening_next: float32 [27, 64, 128], replicated
- bottom_next: float32 [27, 128, 128], replicated
- merging_next: float32 [27, 192, 64], replicated
- closing_next: float32 [27, 64, 64], replicated
- gating_next: float32 [194, 32], replicated
- scales_next: float32 [2, 384], replicated
- widening_momentum: float32 [27, 64, 128], replicated
- bottom_momentum: float32 [27, 128, 128], replicated
- merging_momentum: float32 [27, 192, 64], replicated
- closing_momentum: float32 [27, 64, 64], replicated
- gating_momentum: float32 [194, 32], replicated
- scales_momentum: float32 [2, 384], replicated
- widening_smoothed: float32 [27, 64, 128], replicated
- bottom_smoothed: float32 [27, 128, 128], replicated
- merging_smoothed: float32 [27, 192, 64], replicated
- closing_smoothed: float32 [27, 64, 64], replicated
- gating_smoothed: float32 [194, 32], replicated
- scales_smoothed: float32 [2, 384], replicated
- widening_copy: bfloat16 [27, 64, 128], replicated
- bottom_copy: bfloat16 [27, 128, 128], replicated
- merging_copy: bfloat16 [27, 192, 64], replicated
- closing_copy: bfloat16 [27, 64, 64], replicated
- gating_copy: bfloat16 [194, 32], replicated
- scales_copy: bfloat16 [2, 384], replicated
Inputs may be any that keep to these rules, and one draw needn't show every extreme that they name: `volume_ids`: each voxel's volume id; ids are constant on aligned 2x2x2 blocks of voxels.
All inputs are finite; a program needn't handle non-finite values.
Results may differ from a plain program's by a relative error of at most 0.012.
Values may be sent and summed in bfloat16 or wider, within the bound.
A program may use at most 640 MiB of HBM per device.

v0:
```python
import jax
import jax.numpy as jnp
from jax import lax
from jax.sharding import PartitionSpec as P

HEIGHT = 32
WIDTH = 32


epsilon = 1e-05
momentum_decay = 0.9
learning_rate = 1e-05
scale_rate = 0.0002
weight_decay = 0.0001
average_decay = 0.75
tap_offsets = [
    (depth_step, row_step, col_step)
    for depth_step in (-1, 0, 1)
    for row_step in (-1, 0, 1)
    for col_step in (-1, 0, 1)
]


def extended(array, sides, width):
    for axis, dim in sides:
        peers, length = (lax.axis_size(axis), array.shape[dim])
        up = [(i, (i + 1) % peers) for i in range(peers - 1)]
        down = [(j, i) for i, j in up]
        last = lax.slice_in_dim(array, length - width, length, axis=dim)
        first = lax.slice_in_dim(array, 0, width, axis=dim)
        before = lax.ppermute(last, axis, up)
        after = lax.ppermute(first, axis, down)
        array = jnp.concatenate([before, array, after], axis=dim)
    return array


def depth_halo(values):
    return extended(values, (("depth", 2),), 1)


def build_masks(padded_ids, height, width):
    planes = padded_ids.shape[1] - 2
    cells = height * width
    spread = jnp.pad(padded_ids, ((0, 0), (0, 0), (width + 1, width + 1)))
    center = padded_ids[:, 1 : planes + 1, :]
    column = jnp.arange(cells, dtype=jnp.int32) % width
    result = []
    for depth_step, row_step, col_step in tap_offsets:
        begin = width + 1 + row_step * width + col_step
        beside = spread[:, 1 + depth_step : 1 + depth_step + planes, begin : begin + cells]
        inside = (column + col_step >= 0) & (column + col_step < width)
        result.append((beside == center) & inside[None, None, :])
    return jnp.stack(result).astype(jnp.bfloat16)


def gathered_taps(spread, masks, layer, planes, cells, width):
    pieces = []
    for index in range(9 * layer, 9 * layer + 9):
        depth_step, row_step, col_step = tap_offsets[index]
        begin = width + 1 + row_step * width + col_step
        shifted = spread[:, :, 1 + depth_step : 1 + depth_step + planes, begin : begin + cells]
        pieces.append(shifted * masks[index][:, None])
    return jnp.concatenate(pieces, axis=1)


def convolve(padded, kernel, masks, width):
    channels = padded.shape[1]
    planes = padded.shape[2] - 2
    cells = padded.shape[3]
    spread = jnp.pad(padded, ((0, 0), (0, 0), (0, 0), (width + 1, width + 1)))
    total = None
    for layer in range(3):
        stacked = gathered_taps(spread, masks, layer, planes, cells, width)
        weights = kernel[9 * layer : 9 * layer + 9].reshape(9 * channels, kernel.shape[2])
        term = jnp.einsum("pkdv,ko->podv", stacked, weights, preferred_element_type=jnp.float32)
        total = term if total is None else total + term
    return total


def kernel_grad(padded, grad_low, masks, width):
    channels = padded.shape[1]
    planes = padded.shape[2] - 2
    cells = padded.shape[3]
    spread = jnp.pad(padded, ((0, 0), (0, 0), (0, 0), (width + 1, width + 1)))
    parts = []
    for layer in range(3):
        stacked = gathered_taps(spread, masks, layer, planes, cells, width)
        part = jnp.einsum("pkdv,podv->ko", stacked, grad_low, preferred_element_type=jnp.float32)
        parts.append(part.reshape(9, channels, grad_low.shape[1]))
    return jnp.concatenate(parts, axis=0)


def flipped(kernel):
    return jnp.transpose(kernel[::-1], (0, 2, 1))


def norm_forward(values, gain, shift, count):
    totals = lax.psum(jnp.sum(values, axis=(0, 2, 3)), ("patch", "depth"))
    mean = totals / count
    centred = values - mean[None, :, None, None]
    squares = lax.psum(jnp.sum(centred * centred, axis=(0, 2, 3)), ("patch", "depth"))
    variance = squares / count
    factor = lax.rsqrt(variance + epsilon)
    normed = centred * factor[None, :, None, None]
    return (normed, factor, normed * gain[None, :, None, None] + shift[None, :, None, None])


def norm_backward(grad_out, normed, factor, gain, count):
    shift_grad, gain_grad = lax.psum(
        (jnp.sum(grad_out, axis=(0, 2, 3)), jnp.sum(grad_out * normed, axis=(0, 2, 3))),
        ("patch", "depth"),
    )
    inner = (
        grad_out
        - (shift_grad / count)[None, :, None, None]
        - normed * (gain_grad / count)[None, :, None, None]
    )
    return (
        (inner * (gain * factor)[None, :, None, None]).astype(jnp.bfloat16),
        gain_grad,
        shift_grad,
    )


def silu_slope(values):
    sigma = jax.nn.sigmoid(values)
    return sigma * (1.0 + values * (1.0 - sigma))


def alternate(even, odd, axis):
    joined = jnp.stack([even, odd], axis=axis + 1)
    shape = list(even.shape)
    shape[axis] = shape[axis] * 2
    return joined.reshape(shape)


def widen_axis(values, axis):
    count = values.shape[axis]
    first = lax.slice_in_dim(values, 0, 1, axis=axis)
    last = lax.slice_in_dim(values, count - 1, count, axis=axis)
    before = jnp.concatenate([first, lax.slice_in_dim(values, 0, count - 1, axis=axis)], axis=axis)
    after = jnp.concatenate([lax.slice_in_dim(values, 1, count, axis=axis), last], axis=axis)
    return alternate(0.75 * values + 0.25 * before, 0.75 * values + 0.25 * after, axis)


def split_pairs(grads, axis):
    shape = list(grads.shape)
    shape[axis] = shape[axis] // 2
    shape.insert(axis + 1, 2)
    paired = grads.reshape(shape)
    return (
        lax.index_in_dim(paired, 0, axis + 1, False),
        lax.index_in_dim(paired, 1, axis + 1, False),
    )


def narrow_axis(grads, axis):
    even, odd = split_pairs(grads, axis)
    count = even.shape[axis]
    later = jnp.concatenate(
        [
            lax.slice_in_dim(even, 1, count, axis=axis),
            lax.slice_in_dim(odd, count - 1, count, axis=axis),
        ],
        axis=axis,
    )
    earlier = jnp.concatenate(
        [lax.slice_in_dim(even, 0, 1, axis=axis), lax.slice_in_dim(odd, 0, count - 1, axis=axis)],
        axis=axis,
    )
    return 0.75 * (even + odd) + 0.25 * (later + earlier)


def upsample(coarse, height, width):
    patches, channels, planes, cells = coarse.shape
    padded = extended(coarse, (("depth", 2),), 1).astype(jnp.float32)
    values = coarse.astype(jnp.float32)
    first_device = lax.axis_index("depth") == 0
    last_device = lax.axis_index("depth") == lax.axis_size("depth") - 1
    below = jnp.where(first_device, values[:, :, :1], padded[:, :, :1])
    above = jnp.where(last_device, values[:, :, planes - 1 :], padded[:, :, planes + 1 :])
    before = jnp.concatenate([below, values[:, :, : planes - 1]], axis=2)
    after = jnp.concatenate([values[:, :, 1:], above], axis=2)
    deeper = alternate(0.75 * values + 0.25 * before, 0.75 * values + 0.25 * after, 2)
    grid = deeper.reshape(patches, channels, 2 * planes, height // 2, width // 2)
    grid = widen_axis(widen_axis(grid, 3), 4)
    return (grid.reshape(patches, channels, 2 * planes, height * width), padded, values)


def upsample_adjoint(grads, height, width):
    patches, channels, planes, cells = grads.shape
    grid = grads.reshape(patches, channels, planes, height, width)
    grid = narrow_axis(narrow_axis(grid, 4), 3)
    flat = grid.reshape(patches, channels, planes, cells // 4)
    padded = extended(flat.astype(jnp.bfloat16), (("depth", 2),), 1).astype(flat.dtype)
    even, odd = split_pairs(flat, 2)
    count = even.shape[2]
    first_device = lax.axis_index("depth") == 0
    last_device = lax.axis_index("depth") == lax.axis_size("depth") - 1
    above = jnp.where(last_device, odd[:, :, count - 1 :], padded[:, :, planes + 1 :])
    below = jnp.where(first_device, even[:, :, :1], padded[:, :, :1])
    later = jnp.concatenate([even[:, :, 1:], above], axis=2)
    earlier = jnp.concatenate([below, odd[:, :, : count - 1]], axis=2)
    return 0.75 * (even + odd) + 0.25 * (later + earlier)


def pool_blocks(values, height, width):
    patches, channels, planes, cells = values.shape
    blocks = values.astype(jnp.float32).reshape(
        patches, channels, planes // 2, 2, height // 2, 2, width // 2, 2
    )
    return jnp.mean(blocks, axis=(3, 5, 7)).reshape(patches, channels, planes // 2, cells // 4)


def unpool_blocks(grads, height, width):
    patches, channels, planes, cells = grads.shape
    blocks = grads.reshape(patches, channels, planes, 1, height // 2, 1, width // 2, 1) / 8.0
    blocks = jnp.broadcast_to(blocks, (patches, channels, planes, 2, height // 2, 2, width // 2, 2))
    return blocks.reshape(patches, channels, 2 * planes, 4 * cells)


def update_state(weight, grad, velocity, average, decay, rate):
    step = grad + decay * weight
    momentum = momentum_decay * velocity + step
    weight_next = weight - rate * (step + momentum_decay * momentum)
    smoothed = average_decay * average + (1.0 - average_decay) * weight_next
    return (weight_next, momentum, smoothed, weight_next.astype(jnp.bfloat16))


def local(
    skip_features,
    volume_ids,
    output_grad,
    widening,
    widening_velocity,
    widening_average,
    bottom,
    bottom_velocity,
    bottom_average,
    merging,
    merging_velocity,
    merging_average,
    closing,
    closing_velocity,
    closing_average,
    gating,
    gating_velocity,
    gating_average,
    scales,
    scales_velocity,
    scales_average,
):
    patches, in_channels, planes, cells = skip_features.shape
    encoder_width = bottom.shape[2]
    decoder_width = closing.shape[2]
    merged_width = gating.shape[0] - 2
    half_width = WIDTH // 2
    devices = lax.axis_size("patch") * lax.axis_size("depth")
    fine_count = float(devices * patches * planes * cells)
    coarse_count = fine_count / 8.0
    edges = [
        0,
        encoder_width,
        2 * encoder_width,
        2 * encoder_width + decoder_width,
        2 * encoder_width + 2 * decoder_width,
    ]
    segment_gains = [scales[0, edges[index] : edges[index + 1]] for index in range(4)]
    segment_shifts = [scales[1, edges[index] : edges[index + 1]] for index in range(4)]
    id_rims = extended(volume_ids, (("depth", 1),), 2)
    fine_masks = build_masks(id_rims[:, 1 : planes + 3], HEIGHT, WIDTH)
    coarse_plane = id_rims[:, 0 : planes + 3 : 2].reshape(
        patches, planes // 2 + 2, HEIGHT // 2, 2, half_width, 2
    )
    coarse_masks = build_masks(
        coarse_plane[:, :, :, 0, :, 0].reshape(patches, planes // 2 + 2, cells // 4),
        HEIGHT // 2,
        half_width,
    )
    widening_low = widening.astype(jnp.bfloat16)
    bottom_low = bottom.astype(jnp.bfloat16)
    merging_low = merging.astype(jnp.bfloat16)
    closing_low = closing.astype(jnp.bfloat16)
    projection = gating[:merged_width].astype(jnp.bfloat16)
    gate_bias = gating[merged_width]
    psi_weights = gating[merged_width + 1]
    pooled = pool_blocks(skip_features, HEIGHT, WIDTH).astype(jnp.bfloat16)
    pooled_pad = depth_halo(pooled)
    first_pre = convolve(pooled_pad, widening_low, coarse_masks, half_width)
    first_norm, first_factor, first_act = norm_forward(
        first_pre, segment_gains[0], segment_shifts[0], coarse_count
    )
    first_out = jax.nn.silu(first_act).astype(jnp.bfloat16)
    first_pad = depth_halo(first_out)
    second_pre = convolve(first_pad, bottom_low, coarse_masks, half_width)
    second_norm, second_factor, second_act = norm_forward(
        second_pre, segment_gains[1], segment_shifts[1], coarse_count
    )
    coarse = jax.nn.silu(second_act).astype(jnp.bfloat16)
    fine_up, coarse_pad, coarse_values = upsample(coarse, HEIGHT, WIDTH)
    upsampled = fine_up.astype(jnp.bfloat16)
    query = jnp.einsum(
        "pcdv,ca->padv", skip_features, projection[:in_channels], preferred_element_type=jnp.float32
    )
    query = query + jnp.einsum(
        "pcdv,ca->padv", upsampled, projection[in_channels:], preferred_element_type=jnp.float32
    )
    query = query + gate_bias[None, :, None, None]
    active = jax.nn.silu(query)
    attention = jax.nn.sigmoid(jnp.sum(active * psi_weights[None, :, None, None], axis=1))
    skip_float = skip_features.astype(jnp.float32)
    attended = (skip_float * attention[:, None]).astype(jnp.bfloat16)
    merged = jnp.concatenate([attended, upsampled], axis=1)
    merged_pad = extended(merged, (("depth", 2),), 1)
    third_pre = convolve(merged_pad, merging_low, fine_masks, WIDTH)
    third_norm, third_factor, third_act = norm_forward(
        third_pre, segment_gains[2], segment_shifts[2], fine_count
    )
    third_out = jax.nn.silu(third_act).astype(jnp.bfloat16)
    third_pad = depth_halo(third_out)
    fourth_pre = convolve(third_pad, closing_low, fine_masks, WIDTH)
    fourth_norm, fourth_factor, fourth_act = norm_forward(
        fourth_pre, segment_gains[3], segment_shifts[3], fine_count
    )
    decoded = jax.nn.silu(fourth_act)
    upstream = output_grad.astype(jnp.float32) * silu_slope(fourth_act)
    grad_low, gain_four, shift_four = norm_backward(
        upstream, fourth_norm, fourth_factor, segment_gains[3], fine_count
    )
    closing_grad = kernel_grad(third_pad, grad_low, fine_masks, WIDTH)
    third_back = convolve(depth_halo(grad_low), flipped(closing_low), fine_masks, WIDTH)
    grad_low, gain_three, shift_three = norm_backward(
        third_back * silu_slope(third_act), third_norm, third_factor, segment_gains[2], fine_count
    )
    merging_grad = kernel_grad(merged_pad, grad_low, fine_masks, WIDTH)
    merged_back = convolve(depth_halo(grad_low), flipped(merging_low), fine_masks, WIDTH)
    attended_back = merged_back[:, :in_channels]
    upsampled_back = merged_back[:, in_channels:]
    attention_back = jnp.sum(attended_back * skip_float, axis=1)
    logit_back = attention_back * attention * (1.0 - attention)
    psi_grad = jnp.sum(logit_back[:, None] * active, axis=(0, 2, 3))
    query_back = (
        logit_back[:, None] * psi_weights[None, :, None, None] * silu_slope(query)
    ).astype(jnp.bfloat16)
    bias_grad = jnp.sum(query_back.astype(jnp.float32), axis=(0, 2, 3))
    skip_rows = jnp.einsum(
        "pcdv,padv->ca", skip_features, query_back, preferred_element_type=jnp.float32
    )
    upsampled_rows = jnp.einsum(
        "pcdv,padv->ca", upsampled, query_back, preferred_element_type=jnp.float32
    )
    gating_grad = jnp.concatenate(
        [skip_rows, upsampled_rows, bias_grad[None], psi_grad[None]], axis=0
    )
    skip_back = attended_back * attention[:, None] + jnp.einsum(
        "padv,ca->pcdv", query_back, projection[:in_channels], preferred_element_type=jnp.float32
    )
    upsampled_back = upsampled_back + jnp.einsum(
        "padv,ca->pcdv", query_back, projection[in_channels:], preferred_element_type=jnp.float32
    )
    merging_grad, closing_grad, gating_grad = lax.psum(
        (merging_grad, closing_grad, gating_grad), ("patch", "depth")
    )
    coarse_back = upsample_adjoint(upsampled_back, HEIGHT, WIDTH)
    grad_low, gain_two, shift_two = norm_backward(
        coarse_back * silu_slope(second_act),
        second_norm,
        second_factor,
        segment_gains[1],
        coarse_count,
    )
    bottom_grad = kernel_grad(first_pad, grad_low, coarse_masks, half_width)
    first_back = convolve(depth_halo(grad_low), flipped(bottom_low), coarse_masks, half_width)
    grad_low, gain_one, shift_one = norm_backward(
        first_back * silu_slope(first_act), first_norm, first_factor, segment_gains[0], coarse_count
    )
    widening_grad = kernel_grad(pooled_pad, grad_low, coarse_masks, half_width)
    pooled_back = convolve(depth_halo(grad_low), flipped(widening_low), coarse_masks, half_width)
    skip_grad = skip_back + unpool_blocks(pooled_back, HEIGHT, WIDTH)
    widening_grad, bottom_grad = lax.psum((widening_grad, bottom_grad), ("patch", "depth"))
    scales_grad = jnp.stack(
        [
            jnp.concatenate([gain_one, gain_two, gain_three, gain_four]),
            jnp.concatenate([shift_one, shift_two, shift_three, shift_four]),
        ]
    )
    widening_state = update_state(
        widening, widening_grad, widening_velocity, widening_average, weight_decay, learning_rate
    )
    bottom_state = update_state(
        bottom, bottom_grad, bottom_velocity, bottom_average, weight_decay, learning_rate
    )
    merging_state = update_state(
        merging, merging_grad, merging_velocity, merging_average, weight_decay, learning_rate
    )
    closing_state = update_state(
        closing, closing_grad, closing_velocity, closing_average, weight_decay, learning_rate
    )
    gating_state = update_state(
        gating, gating_grad, gating_velocity, gating_average, weight_decay, learning_rate
    )
    scales_state = update_state(
        scales, scales_grad, scales_velocity, scales_average, 0.0, scale_rate
    )
    return (
        decoded.astype(jnp.bfloat16),
        skip_grad,
        widening_state[0],
        bottom_state[0],
        merging_state[0],
        closing_state[0],
        gating_state[0],
        scales_state[0],
        widening_state[1],
        bottom_state[1],
        merging_state[1],
        closing_state[1],
        gating_state[1],
        scales_state[1],
        widening_state[2],
        bottom_state[2],
        merging_state[2],
        closing_state[2],
        gating_state[2],
        scales_state[2],
        widening_state[3],
        bottom_state[3],
        merging_state[3],
        closing_state[3],
        gating_state[3],
        scales_state[3],
    )


def solution(mesh):
    return jax.shard_map(
        local,
        mesh=mesh,
        in_specs=(
            P("patch", None, "depth", None),
            P("patch", "depth", None),
            P("patch", None, "depth", None),
            P(),
            P(),
            P(),
            P(),
            P(),
            P(),
            P(),
            P(),
            P(),
            P(),
            P(),
            P(),
            P(),
            P(),
            P(),
            P(),
            P(),
            P(),
        ),
        out_specs=(
            P("patch", None, "depth", None),
            P("patch", None, "depth", None),
            P(),
            P(),
            P(),
            P(),
            P(),
            P(),
            P(),
            P(),
            P(),
            P(),
            P(),
            P(),
            P(),
            P(),
            P(),
            P(),
            P(),
            P(),
            P(),
            P(),
            P(),
            P(),
            P(),
            P(),
        ),
        check_vma=False,
    )
```

profile of v0, /device:TPU:0, one launch (start us, length us, event | category | flops | bytes accessed | tf_op | source)
XLA Modules:
  0.0 1605.3 jit_solution(8978516307511546518)
XLA Ops:
  17.4 7.0 copy.226
  24.4 9.6 reduce_sum.189
  83.2 41.9 %psum.147 = f32[128]{0:T(128)S(1)} all-reduce(f32[128]{0:T(128)} %get-tuple-element.516), channel_id=1, replica_groups=mesh['patch'=16,'depth'=2] {'patch','depth'}, use_global_device_ids=true, to_apply=%region_2.3 | all-reduce | flops 128 | bytes 1024 | tf_op jit(solution)/shard_map/psum | solution.py:98
  125.5 41.0 %psum.148 = f32[128]{0:T(128)S(1)} all-reduce(f32[128]{0:T(128)S(1)} %multiply_reduce_fusion.6), channel_id=1, replica_groups=mesh['patch'=16,'depth'=2] {'patch','depth'}, use_global_device_ids=true, to_apply=%region_4.5 | all-reduce | flops 128 | bytes 1024 | tf_op jit(solution)/shard_map/psum | solution.py:101
  190.6 39.5 %psum.149 = f32[128]{0:T(128)S(1)} all-reduce(f32[128]{0:T(128)S(1)} %get-tuple-element.518), channel_id=1, replica_groups=mesh['patch'=16,'depth'=2] {'patch','depth'}, use_global_device_ids=true, to_apply=%region_6.7 | all-reduce | flops 128 | bytes 1024 | tf_op jit(solution)/shard_map/psum | solution.py:98
  230.4 40.6 %psum.150 = f32[128]{0:T(128)S(1)} all-reduce(f32[128]{0:T(128)S(1)} %multiply_reduce_fusion.5), channel_id=1, replica_groups=mesh['patch'=16,'depth'=2] {'patch','depth'}, use_global_device_ids=true, to_apply=%region_8.9 | all-reduce | flops 128 | bytes 1024 | tf_op jit(solution)/shard_map/psum | solution.py:101
  290.5 8.5 copy.246
  321.6 13.1 select_maximum_fusion
  334.7 9.0 fusion.28
  343.7 18.1 %fusion.27 = (bf16[4,1728,4,1024]{3,1,2,0:T(8,128)(2,1)}, bf16[4,1728,4,1024]{3,1,2,0:T(8,128)(2,1)}, bf16[4,1728,4,1024]{3,1,2,0:T(8,128)(2,1)}) fusion(bf16[4,1728,4,1024]{3,1,2,0:T(8,128)(2,1)} %get-tuple-element.171, bf16[4,192,6,1090]{3,1,2,0:T(8,128)(2,1)S(1)} %select_maximum_fusion, bf16[4,4,1024]{2,1,0:T(4,128)(2,1)S(1)} %get-tuple-element.388, ...), kind=kLoop, calls=%fused_computation.49 | loop fusion | flops 37748736 | bytes 37847040
  361.8 18.5 %fusion.26 = (bf16[4,1728,4,1024]{3,1,2,0:T(8,128)(2,1)}, bf16[4,1728,4,1024]{3,1,2,0:T(8,128)(2,1)}, bf16[4,1728,4,1024]{3,1,2,0:T(8,128)(2,1)}) fusion(bf16[4,1728,4,1024]{3,1,2,0:T(8,128)(2,1)} %get-tuple-element.168, bf16[4,192,6,1090]{3,1,2,0:T(8,128)(2,1)S(1)} %select_maximum_fusion, bf16[4,4,1024]{2,1,0:T(4,128)(2,1)S(1)} %get-tuple-element.387, ...), kind=kLoop, calls=%fused_computation.47 | loop fusion | flops 37748736 | bytes 37847040
  380.4 18.1 %fusion.25 = (bf16[4,1728,4,1024]{3,1,2,0:T(8,128)(2,1)}, bf16[4,1728,4,1024]{3,1,2,0:T(8,128)(2,1)}, bf16[4,1728,4,1024]{3,1,2,0:T(8,128)(2,1)}) fusion(bf16[4,1728,4,1024]{3,1,2,0:T(8,128)(2,1)} %get-tuple-element.165, bf16[4,192,6,1090]{3,1,2,0:T(8,128)(2,1)S(1)} %select_maximum_fusion, bf16[4,4,1024]{2,1,0:T(4,128)(2,1)S(1)} %get-tuple-element.386, ...), kind=kLoop, calls=%fused_computation.45 | loop fusion | flops 37748736 | bytes 37847040
  398.5 8.8 fusion.24
  407.3 18.3 %fusion.22 = (bf16[4,1728,4,1024]{3,1,2,0:T(8,128)(2,1)}, bf16[4,1728,4,1024]{3,1,2,0:T(8,128)(2,1)}, bf16[4,1728,4,1024]{3,1,2,0:T(8,128)(2,1)}) fusion(bf16[4,1728,4,1024]{3,1,2,0:T(8,128)(2,1)} %get-tuple-element.177, bf16[4,192,6,1090]{3,1,2,0:T(8,128)(2,1)S(1)} %select_maximum_fusion, bf16[4,4,1024]{2,1,0:T(4,128)(2,1)S(1)} %get-tuple-element.384, ...), kind=kLoop, calls=%fused_computation.39 | loop fusion | flops 37748736 | bytes 37847040
  425.6 18.1 %fusion.21 = (bf16[4,1728,4,1024]{3,1,2,0:T(8,128)(2,1)}, bf16[4,1728,4,1024]{3,1,2,0:T(8,128)(2,1)}, bf16[4,1728,4,1024]{3,1,2,0:T(8,128)(2,1)}) fusion(bf16[4,1728,4,1024]{3,1,2,0:T(8,128)(2,1)} %get-tuple-element.159, bf16[4,192,6,1090]{3,1,2,0:T(8,128)(2,1)S(1)} %select_maximum_fusion, bf16[4,4,1024]{2,1,0:T(4,128)(2,1)S(1)} %get-tuple-element.383, ...), kind=kLoop, calls=%fused_computation.37 | loop fusion | flops 37748736 | bytes 37847040
  443.8 18.3 %fusion.20 = (bf16[4,1728,4,1024]{3,1,2,0:T(8,128)(2,1)}, bf16[4,1728,4,1024]{3,1,2,0:T(8,128)(2,1)}, bf16[4,1728,4,1024]{3,1,2,0:T(8,128)(2,1)}) fusion(bf16[4,1728,4,1024]{3,1,2,0:T(8,128)(2,1)} %get-tuple-element.156, bf16[4,192,6,1090]{3,1,2,0:T(8,128)(2,1)S(1)} %select_maximum_fusion, bf16[4,4,1024]{2,1,0:T(4,128)(2,1)S(1)} %get-tuple-element.382, ...), kind=kLoop, calls=%fused_computation.35 | loop fusion | flops 37748736 | bytes 37847040
  462.1 18.1 %fusion.19 = (bf16[4,1728,4,1024]{3,1,2,0:T(8,128)(2,1)}, bf16[4,1728,4,1024]{3,1,2,0:T(8,128)(2,1)}, bf16[4,1728,4,1024]{3,1,2,0:T(8,128)(2,1)}) fusion(bf16[4,1728,4,1024]{3,1,2,0:T(8,128)(2,1)} %get-tuple-element.153, bf16[4,192,6,1090]{3,1,2,0:T(8,128)(2,1)S(1)} %select_maximum_fusion, bf16[4,4,1024]{2,1,0:T(4,128)(2,1)S(1)} %get-tuple-element.381, ...), kind=kLoop, calls=%fused_computation.33 | loop fusion | flops 37748736 | bytes 37847040 | tf_op jit(solution)/shard_map/concatenate | solution.py:63
  480.2 20.1 %fusion.244 = f32[4,4,1024,64]{2,3,1,0:T(8,128)S(1)} fusion(bf16[4,1728,4,1024]{3,1,2,0:T(8,128)(2,1)} %get-tuple-element.151, bf16[1728,64,1,1]{0,1,2,3:T(8,128)(2,1)S(1)} %copy-done.54), kind=kOutput, calls=%fused_computation.749 | convolution fusion | flops 3623878656 | bytes 61038592 | tf_op jit(solution)/shard_map/pkdv,ko->podv/dot_general | solution.py:75
  500.3 20.4 %fusion.246 = f32[4,4,1024,64]{2,3,1,0:T(8,128)S(1)} fusion(bf16[4,1728,4,1024]{3,1,2,0:T(8,128)(2,1)} %get-tuple-element.152, bf16[1728,64,1,1]{0,1,2,3:T(8,128)(2,1)S(1)} %copy-done.55), kind=kOutput, calls=%fused_computation.751 | convolution fusion | flops 3623878656 | bytes 61038592 | tf_op jit(solution)/shard_map/pkdv,ko->podv/dot_general | solution.py:75
  520.8 22.9 %fusion.329 = (f32[64]{0:T(128)S(1)}, f32[4,4,1024,64]{2,3,1,0:T(8,128)}) fusion(bf16[4,1728,4,1024]{3,1,2,0:T(8,128)(2,1)} %get-tuple-element.150, bf16[1728,64,1,1]{0,1,2,3:T(8,128)(2,1)S(1)} %copy-done.56, f32[4,4,1024,64]{2,3,1,0:T(8,128)S(1)} %fusion.246, f32[4,4,1024,64]{2,3,1,0:T(8,128)S(1)} %fusion.244), kind=kOutput, calls=%fused_computation.987 | convolution fusion | flops 3627024384 | bytes 69427456 | tf_op jit(solution)/shard_map/pkdv,ko->podv/dot_general | solution.py:75
  543.7 39.5 %psum.151 = f32[64]{0:T(128)S(1)} all-reduce(f32[64]{0:T(128)S(1)} %get-tuple-element.522), channel_id=1, replica_groups=mesh['patch'=16,'depth'=2] {'patch','depth'}, use_global_device_ids=true, to_apply=%region_11.12 | all-reduce | flops 64 | bytes 512 | tf_op jit(solution)/shard_map/psum | solution.py:98
  586.0 40.6 %psum.152 = f32[64]{0:T(128)S(1)} all-reduce(f32[64]{0:T(128)S(1)} %multiply_reduce_fusion.2), channel_id=1, replica_groups=mesh['patch'=16,'depth'=2] {'patch','depth'}, use_global_device_ids=true, to_apply=%region_13.14 | all-reduce | flops 64 | bytes 512 | tf_op jit(solution)/shard_map/psum | solution.py:101
  712.1 15.6 fusion.333
  733.9 15.4 fusion.330
  749.3 40.4 %psum.153 = f32[64]{0:T(128)S(1)} all-reduce(f32[64]{0:T(128)S(1)} %get-tuple-element.524), channel_id=1, replica_groups=mesh['patch'=16,'depth'=2] {'patch','depth'}, use_global_device_ids=true, to_apply=%region_15.16 | all-reduce | flops 64 | bytes 512 | tf_op jit(solution)/shard_map/psum | solution.py:98
  792.6 41.0 %psum.154 = f32[64]{0:T(128)S(1)} all-reduce(f32[64]{0:T(128)S(1)} %multiply_reduce_fusion.1), channel_id=1, replica_groups=mesh['patch'=16,'depth'=2] {'patch','depth'}, use_global_device_ids=true, to_apply=%region_17.18 | all-reduce | flops 64 | bytes 512 | tf_op jit(solution)/shard_map/psum | solution.py:101
  840.8 39.1 %all-reduce.13 = (f32[64]{0:T(128)S(1)}, f32[64]{0:T(128)S(1)}) all-reduce(f32[64]{0:T(128)S(1)} %get-tuple-element.107, f32[64]{0:T(128)S(1)} %get-tuple-element.106), channel_id=1, replica_groups=mesh['patch'=16,'depth'=2] {'patch','depth'}, use_global_device_ids=true, to_apply=%region_21.22 | all-reduce | flops 128 | bytes 1024 | tf_op jit(solution)/shard_map/psum | solution.py:109
  885.8 10.2 fusion.11
  905.9 9.0 fusion.7
  936.5 6.6 fusion.123
  971.1 7.1 fusion.336
  978.4 8.6 fusion.335
  987.2 11.3 fusion.296
  998.5 41.0 %all-reduce.12 = (f32[64]{0:T(128)S(1)}, f32[64]{0:T(128)S(1)}) all-reduce(f32[64]{0:T(128)S(1)} %get-tuple-element.105, f32[64]{0:T(128)S(1)} %get-tuple-element.104), channel_id=1, replica_groups=mesh['patch'=16,'depth'=2] {'patch','depth'}, use_global_device_ids=true, to_apply=%region_25.26 | all-reduce | flops 128 | bytes 1024 | tf_op jit(solution)/shard_map/psum | solution.py:109
  1045.8 24.0 %fusion.79 = f32[1728,64]{0,1:T(8,128)} fusion(bf16[4,1728,4,1024]{3,1,2,0:T(8,128)(2,1)} %get-tuple-element.152, bf16[4,64,4,1024]{3,1,2,0:T(8,128)(2,1)S(1)} %fusion.71), kind=kOutput, calls=%fused_computation.159 | convolution fusion | flops 3623878656 | bytes 59162624 | tf_op jit(solution)/shard_map/pkdv,podv->ko/dot_general | solution.py:88
  1069.8 24.2 %fusion.82 = f32[1728,64]{0,1:T(8,128)} fusion(bf16[4,1728,4,1024]{3,1,2,0:T(8,128)(2,1)} %get-tuple-element.151, bf16[4,64,4,1024]{3,1,2,0:T(8,128)(2,1)S(1)} %fusion.71), kind=kOutput, calls=%fused_computation.160 | convolution fusion | flops 3623878656 | bytes 59162624 | tf_op jit(solution)/shard_map/pkdv,podv->ko/dot_general | solution.py:88
  1097.3 24.7 %fusion.85 = f32[1728,64]{0,1:T(8,128)} fusion(bf16[4,1728,4,1024]{3,1,2,0:T(8,128)(2,1)} %get-tuple-element.150, bf16[4,64,4,1024]{3,1,2,0:T(8,128)(2,1)S(1)} %fusion.71), kind=kOutput, calls=%fused_computation.161 | convolution fusion | flops 3623878656 | bytes 59162624 | tf_op jit(solution)/shard_map/pkdv,podv->ko/dot_general | solution.py:88
  1149.7 6.5 fusion.95
  1191.5 13.4 fusion.338
  1207.8 11.1 fusion.337
  1219.0 22.3 %add_bitcast_fusion = f32[4,192,4,1024]{3,1,2,0:T(8,128)} fusion(f32[4,4,1024,192]{2,3,1,0:T(8,128)} %fusion.337, f32[4,4,1024,192]{2,3,1,0:T(8,128)} %fusion.338, bf16[4,576,4,1024]{3,1,2,0:T(8,128)(2,1)} %copy-done.8, bf16[576,192,1,1]{1,0,3,2:T(8,128)(2,1)S(1)} %bitcast.686), kind=kOutput, calls=%fused_computation.15 | convolution fusion | flops 3630170112 | bytes 56844288 | tf_op jit(solution)/shard_map/pkdv,ko->podv/dot_general | solution.py:75
  1255.2 8.7 copy.266
  1263.9 12.6 fusion.308
  1295.0 39.2 %all-reduce.11 = (f32[128]{0:T(128)S(1)}, f32[128]{0:T(128)S(1)}) all-reduce(f32[128]{0:T(128)S(1)} %get-tuple-element.111, f32[128]{0:T(128)S(1)} %get-tuple-element.110), channel_id=1, replica_groups=mesh['patch'=16,'depth'=2] {'patch','depth'}, use_global_device_ids=true, to_apply=%region_30.31 | all-reduce | flops 256 | bytes 2048 | tf_op jit(solution)/shard_map/psum | solution.py:109
  1367.6 41.4 %all-reduce.10 = (f32[128]{0:T(128)S(1)}, f32[128]{0:T(128)S(1)}, f32[194,32]{0,1:T(8,128)S(1)}) all-reduce(f32[128]{0:T(128)S(1)} %get-tuple-element.109, f32[128]{0:T(128)S(1)} %get-tuple-element.108, f32[194,32]{0,1:T(8,128)S(1)} %pad_maximum_fusion.30), channel_id=1, replica_groups=mesh['patch'=16,'depth'=2] {'patch','depth'}, use_global_device_ids=true, to_apply=%region_34.35 | all-reduce | flops 6464 | bytes 51712 | tf_op jit(solution)/shard_map/psum | solution.py:109
  1439.3 7.7 broadcast_in_dim.6
  1446.9 7.1 copy.287
  1464.0 110.1 %all-reduce.17.cloned.1.call-done = (f32[27,64,128]{2,1,0:T(8,128)}, f32[27,128,128]{2,1,0:T(8,128)}, f32[27,192,64]{1,0,2:T(8,128)}, f32[27,64,64]{2,1,0:T(8,128)}) async-done(((f32[27,64,128]{2,1,0:T(8,128)}, f32[27,128,128]{2,1,0:T(8,128)}, f32[27,192,64]{1,0,2:T(8,128)}, f32[27,64,64]{2,1,0:T(8,128)}), (f32[27,64,128]{2,1,0:T(8,128)}, f32[27,128,128]{2,1,0:T(8,128)}, f32[27,192,64]{1,0,2:T(8,128)}, ...) | async-done | bytes 4423696 | tf_op jit(solution)/shard_map/psum | solution.py:380
  (928 shorter events, 498.0 us)
Async XLA Ops:
  7.2 1567.0 %all-reduce.17.cloned.1.call-start = ((), (), s32[]{:S(2)}) async-start(), calls=%async_computation | async-start | bytes 11272192 | tf_op jit(solution)/shard_map/psum | solution.py:380
  8.8 51.9 %collective-permute-start.2 = (s32[4,2,1024]{2,1,0:T(2,128)}, s32[4,2,1024]{2,1,0:T(2,128)}, u32[]{:S(2)}, u32[]{:S(2)}) collective-permute-start(s32[4,2,1024]{2,1,0:T(2,128)} %get-tuple-element.500), channel_id=1, source_target_pairs={{0,1},{2,3},{4,5},{6,7},{8,9},{10,11},{12,13},{14,15},{16,17},{18,... | collective-permute-start | bytes 98312 | tf_op jit(solution)/shard_map/ppermute | solution.py:31
  11.8 48.9 %collective-permute-start.3 = (s32[4,2,1024]{2,1,0:T(2,128)}, s32[4,2,1024]{2,1,0:T(2,128)}, u32[]{:S(2)}, u32[]{:S(2)}) collective-permute-start(s32[4,2,1024]{2,1,0:T(2,128)} %get-tuple-element.501), channel_id=1, source_target_pairs={{1,0},{3,2},{5,4},{7,6},{9,8},{11,10},{13,12},{15,14},{17,16},{19,... | collective-permute-start | bytes 98312 | tf_op jit(solution)/shard_map/ppermute | solution.py:32
  35.0 38.5 %collective-permute-start = (bf16[4,64,1,256]{3,1,2,0:T(8,128)(2,1)}, bf16[4,64,1,256]{3,1,2,0:T(8,128)(2,1)}, u32[]{:S(2)}, u32[]{:S(2)}) collective-permute-start(bf16[4,64,1,256]{3,1,2,0:T(8,128)(2,1)} %get-tuple-element.471), channel_id=1, source_target_pairs={{0,1},{2,3},{4,5},{6,7},{8,9},{10,11},{12,13},{14,15},{16,17},{18,... | collective-permute-start | bytes 393224 | tf_op jit(solution)/shard_map/ppermute | solution.py:31
  39.3 34.3 %collective-permute-start.1 = (bf16[4,64,1,256]{3,1,2,0:T(8,128)(2,1)}, bf16[4,64,1,256]{3,1,2,0:T(8,128)(2,1)}, u32[]{:S(2)}, u32[]{:S(2)}) collective-permute-start(bf16[4,64,1,256]{3,1,2,0:T(8,128)(2,1)} %get-tuple-element.472), channel_id=1, source_target_pairs={{1,0},{3,2},{5,4},{7,6},{9,8},{11,10},{13,12},{15,14},{17,16},{19,... | collective-permute-start | bytes 393224 | tf_op jit(solution)/shard_map/ppermute | solution.py:32
  67.8 107.9 %copy-start.184 = (bf16[4,2,256]{2,1,0:T(2,128)(2,1)}, bf16[4,2,256]{2,1,0:T(2,128)(2,1)S(1)}, u32[]{:S(2)}) copy-start(bf16[4,2,256]{2,1,0:T(2,128)(2,1)S(1)} %get-tuple-element.479) | copy-start | bytes 12292
  67.8 107.9 %copy-start.186 = (bf16[4,2,256]{2,1,0:T(2,128)(2,1)}, bf16[4,2,256]{2,1,0:T(2,128)(2,1)S(1)}, u32[]{:S(2)}) copy-start(bf16[4,2,256]{2,1,0:T(2,128)(2,1)S(1)} %get-tuple-element.488) | copy-start | bytes 12292
  67.8 109.4 %copy-start.178 = (bf16[4,2,256]{2,1,0:T(2,128)(2,1)}, bf16[4,2,256]{2,1,0:T(2,128)(2,1)S(1)}, u32[]{:S(2)}) copy-start(bf16[4,2,256]{2,1,0:T(2,128)(2,1)S(1)} %get-tuple-element.478) | copy-start | bytes 12292
  67.8 109.4 %copy-start.180 = (bf16[4,2,256]{2,1,0:T(2,128)(2,1)}, bf16[4,2,256]{2,1,0:T(2,128)(2,1)S(1)}, u32[]{:S(2)}) copy-start(bf16[4,2,256]{2,1,0:T(2,128)(2,1)S(1)} %get-tuple-element.487) | copy-start | bytes 12292
  67.8 110.9 %copy-start.174 = (bf16[4,2,256]{2,1,0:T(2,128)(2,1)}, bf16[4,2,256]{2,1,0:T(2,128)(2,1)S(1)}, u32[]{:S(2)}) copy-start(bf16[4,2,256]{2,1,0:T(2,128)(2,1)S(1)} %get-tuple-element.477) | copy-start | bytes 12292
  67.8 110.9 %copy-start.176 = (bf16[4,2,256]{2,1,0:T(2,128)(2,1)}, bf16[4,2,256]{2,1,0:T(2,128)(2,1)S(1)}, u32[]{:S(2)}) copy-start(bf16[4,2,256]{2,1,0:T(2,128)(2,1)S(1)} %get-tuple-element.486) | copy-start | bytes 12292
  67.8 112.3 %copy-start.170 = (bf16[4,2,256]{2,1,0:T(2,128)(2,1)}, bf16[4,2,256]{2,1,0:T(2,128)(2,1)S(1)}, u32[]{:S(2)}) copy-start(bf16[4,2,256]{2,1,0:T(2,128)(2,1)S(1)} %get-tuple-element.476) | copy-start | bytes 12292
  67.9 112.3 %copy-start.172 = (bf16[4,2,256]{2,1,0:T(2,128)(2,1)}, bf16[4,2,256]{2,1,0:T(2,128)(2,1)S(1)}, u32[]{:S(2)}) copy-start(bf16[4,2,256]{2,1,0:T(2,128)(2,1)S(1)} %get-tuple-element.485) | copy-start | bytes 12292
  67.9 113.6 %copy-start.166 = (bf16[4,2,256]{2,1,0:T(2,128)(2,1)}, bf16[4,2,256]{2,1,0:T(2,128)(2,1)S(1)}, u32[]{:S(2)}) copy-start(bf16[4,2,256]{2,1,0:T(2,128)(2,1)S(1)} %get-tuple-element.475) | copy-start | bytes 12292
  67.9 113.6 %copy-start.168 = (bf16[4,2,256]{2,1,0:T(2,128)(2,1)}, bf16[4,2,256]{2,1,0:T(2,128)(2,1)S(1)}, u32[]{:S(2)}) copy-start(bf16[4,2,256]{2,1,0:T(2,128)(2,1)S(1)} %get-tuple-element.484) | copy-start | bytes 12292
  67.9 115.0 %copy-start.162 = (bf16[4,2,256]{2,1,0:T(2,128)(2,1)}, bf16[4,2,256]{2,1,0:T(2,128)(2,1)S(1)}, u32[]{:S(2)}) copy-start(bf16[4,2,256]{2,1,0:T(2,128)(2,1)S(1)} %get-tuple-element.474) | copy-start | bytes 12292
  67.9 115.0 %copy-start.164 = (bf16[4,2,256]{2,1,0:T(2,128)(2,1)}, bf16[4,2,256]{2,1,0:T(2,128)(2,1)S(1)}, u32[]{:S(2)}) copy-start(bf16[4,2,256]{2,1,0:T(2,128)(2,1)S(1)} %get-tuple-element.483) | copy-start | bytes 12292
  67.9 116.3 %copy-start.156 = (bf16[4,2,256]{2,1,0:T(2,128)(2,1)}, bf16[4,2,256]{2,1,0:T(2,128)(2,1)S(1)}, u32[]{:S(2)}) copy-start(bf16[4,2,256]{2,1,0:T(2,128)(2,1)S(1)} %get-tuple-element.473) | copy-start | bytes 12292
  67.9 116.3 %copy-start.158 = (bf16[4,2,256]{2,1,0:T(2,128)(2,1)}, bf16[4,2,256]{2,1,0:T(2,128)(2,1)S(1)}, u32[]{:S(2)}) copy-start(bf16[4,2,256]{2,1,0:T(2,128)(2,1)S(1)} %get-tuple-element.482) | copy-start | bytes 12292
  67.9 116.3 %copy-start.160 = (bf16[4,2,256]{2,1,0:T(2,128)(2,1)}, bf16[4,2,256]{2,1,0:T(2,128)(2,1)S(1)}, u32[]{:S(2)}) copy-start(bf16[4,2,256]{2,1,0:T(2,128)(2,1)S(1)} %get-tuple-element.491) | copy-start | bytes 12292
  73.5 109.4 %copy-start.182 = (bf16[4,2,256]{2,1,0:T(2,128)(2,1)}, bf16[4,2,256]{2,1,0:T(2,128)(2,1)S(1)}, u32[]{:S(2)}) copy-start(bf16[4,2,256]{2,1,0:T(2,128)(2,1)S(1)} %get-tuple-element.492) | copy-start | bytes 12292
  83.2 91.2 %copy-start.11 = (f32[4,2,256,128]{3,2,1,0:T(8,128)}, f32[4,2,256,128]{3,2,1,0:T(8,128)S(1)}, u32[]{:S(2)}) copy-start(f32[4,2,256,128]{3,2,1,0:T(8,128)S(1)} %get-tuple-element.517) | copy-start | bytes 3145732
  83.2 90.1 %copy-start.219 = (bf16[4,2,256]{2,1,0:T(2,128)(2,1)S(1)}, bf16[4,2,256]{2,1,0:T(2,128)(2,1)}, u32[]{:S(2)}) copy-start(bf16[4,2,256]{2,1,0:T(2,128)(2,1)} %copy-done.218) | copy-start | bytes 12292
  167.6 5.4 collective-permute-start.4
  168.9 4.1 collective-permute-start.5
  272.7 4.2 collective-permute-start.6
  274.0 3.4 collective-permute-start.7
  313.6 6.4 collective-permute-start.8
  316.3 5.3 collective-permute-start.9
  319.5 106.1 %copy-start.63 = (bf16[4,4,1024]{2,1,0:T(4,128)(2,1)}, bf16[4,4,1024]{2,1,0:T(4,128)(2,1)S(1)}, u32[]{:S(2)}) copy-start(bf16[4,4,1024]{2,1,0:T(4,128)(2,1)S(1)} %get-tuple-element.401) | copy-start | bytes 98308
  319.9 105.7 %copy-start.71 = (bf16[4,4,1024]{2,1,0:T(4,128)(2,1)}, bf16[4,4,1024]{2,1,0:T(4,128)(2,1)S(1)}, u32[]{:S(2)}) copy-start(bf16[4,4,1024]{2,1,0:T(4,128)(2,1)S(1)} %get-tuple-element.383) | copy-start | bytes 98308
  320.0 105.7 %copy-start.73 = (bf16[4,4,1024]{2,1,0:T(4,128)(2,1)}, bf16[4,4,1024]{2,1,0:T(4,128)(2,1)S(1)}, u32[]{:S(2)}) copy-start(bf16[4,4,1024]{2,1,0:T(4,128)(2,1)S(1)} %get-tuple-element.392) | copy-start | bytes 98308
  320.0 123.8 %copy-start.65 = (bf16[4,4,1024]{2,1,0:T(4,128)(2,1)}, bf16[4,4,1024]{2,1,0:T(4,128)(2,1)S(1)}, u32[]{:S(2)}) copy-start(bf16[4,4,1024]{2,1,0:T(4,128)(2,1)S(1)} %get-tuple-element.382) | copy-start | bytes 98308
  320.0 123.8 %copy-start.67 = (bf16[4,4,1024]{2,1,0:T(4,128)(2,1)}, bf16[4,4,1024]{2,1,0:T(4,128)(2,1)S(1)}, u32[]{:S(2)}) copy-start(bf16[4,4,1024]{2,1,0:T(4,128)(2,1)S(1)} %get-tuple-element.391) | copy-start | bytes 98308
  631.8 26.0 %collective-permute-start.10 = (bf16[4,64,1,1024]{3,1,2,0:T(8,128)(2,1)}, bf16[4,64,1,1024]{3,1,2,0:T(8,128)(2,1)}, u32[]{:S(2)}, u32[]{:S(2)}) collective-permute-start(bf16[4,64,1,1024]{3,1,2,0:T(8,128)(2,1)} %get-tuple-element.282), channel_id=1, source_target_pairs={{0,1},{2,3},{4,5},{6,7},{8,9},{10,11},{12,13},{14,15},{16,17},{18,... | collective-permute-start | bytes 1572872 | tf_op jit(solution)/shard_map/ppermute | solution.py:31
  633.9 23.9 %collective-permute-start.11 = (bf16[4,64,1,1024]{3,1,2,0:T(8,128)(2,1)}, bf16[4,64,1,1024]{3,1,2,0:T(8,128)(2,1)}, u32[]{:S(2)}, u32[]{:S(2)}) collective-permute-start(bf16[4,64,1,1024]{3,1,2,0:T(8,128)(2,1)} %get-tuple-element.283), channel_id=1, source_target_pairs={{1,0},{3,2},{5,4},{7,6},{9,8},{11,10},{13,12},{15,14},{17,16},{19,... | collective-permute-start | bytes 1572872 | tf_op jit(solution)/shard_map/ppermute | solution.py:32
  902.9 16.0 collective-permute-start.12
  904.2 14.7 collective-permute-start.13
  1094.0 37.2 %collective-permute-start.14 = (bf16[4,64,1,1024]{3,1,2,0:T(8,128)(2,1)}, bf16[4,64,1,1024]{3,1,2,0:T(8,128)(2,1)}, u32[]{:S(2)}, u32[]{:S(2)}) collective-permute-start(bf16[4,64,1,1024]{3,1,2,0:T(8,128)(2,1)} %get-tuple-element.272), channel_id=1, source_target_pairs={{0,1},{2,3},{4,5},{6,7},{8,9},{10,11},{12,13},{14,15},{16,17},{18,... | collective-permute-start | bytes 1572872 | tf_op jit(solution)/shard_map/ppermute | solution.py:31
  1096.0 35.1 %collective-permute-start.15 = (bf16[4,64,1,1024]{3,1,2,0:T(8,128)(2,1)}, bf16[4,64,1,1024]{3,1,2,0:T(8,128)(2,1)}, u32[]{:S(2)}, u32[]{:S(2)}) collective-permute-start(bf16[4,64,1,1024]{3,1,2,0:T(8,128)(2,1)} %get-tuple-element.273), channel_id=1, source_target_pairs={{1,0},{3,2},{5,4},{7,6},{9,8},{11,10},{13,12},{15,14},{17,16},{19,... | collective-permute-start | bytes 1572872 | tf_op jit(solution)/shard_map/ppermute | solution.py:32
  1285.8 5.7 collective-permute-start.16
  1289.6 3.4 collective-permute-start.17
  1343.6 5.5 collective-permute-start.18
  1344.9 4.2 collective-permute-start.19
  1415.8 6.3 collective-permute-start.20
  1417.1 5.0 collective-permute-start.21
  1459.3 114.9 %copy-start.21 = (f32[27,192,64]{1,2,0:T(8,128)S(1)}, f32[27,192,64]{1,2,0:T(8,128)}, u32[]{:S(2)}) copy-start(f32[27,192,64]{1,2,0:T(8,128)} %param.30) | copy-start | bytes 3981316
  1459.3 114.9 %copy-start.45 = (f32[27,192,64]{1,2,0:T(8,128)S(1)}, f32[27,192,64]{1,2,0:T(8,128)}, u32[]{:S(2)}) copy-start(f32[27,192,64]{1,2,0:T(8,128)} %param.31) | copy-start | bytes 3981316
  (258 other events, 3643.0 us)
Sparse Core Ops, SparseCore 0:
  1421.5 152.5 all-reduce.16
where the time goes:
time: 1610 us
  blocking collectives  485 us (30%)
  other arithmetic  479 us (30%)
  matrix products  325 us (20%)
  local copies, waits for them, and re-layouts  143 us (9%)
  waiting for transfers between devices  114 us (7%)
  starting transfers between devices  39.6 us (2%)
  between operations  19 us (1%)
    unnamed x116, other arithmetic  307 us
    dot_general x24, matrix products, convolve(): jnp.einsum('pkdv,ko->podv', stacked, weights, preferred_element_type=jnp....  193 us
    psum x4, blocking collectives, norm_forward(): lax.psum(jnp.sum(centred * centred, axis=(0, 2, 3)), ('patch', 'depth'))  163 us
    psum x4, blocking collectives, norm_forward(): totals = lax.psum(jnp.sum(values, axis=(0, 2, 3)), ('patch', 'depth'))  161 us
    psum x4, blocking collectives, norm_backward(): lax.psum((jnp.sum(grad_out, axis=(0, 2, 3)), jnp.sum(grad_out * normed, a...  161 us
    dot_general x12, matrix products, kernel_grad(): jnp.einsum('pkdv,podv->ko', stacked, grad_low, preferred_element_type=jnp...  111 us
    psum x1, waiting for transfers between devices, local(): lax.psum((widening_grad, bottom_grad), ('patch', 'depth'))  110 us
    concatenate x8, other arithmetic, gathered_taps(): return jnp.concatenate(pieces, axis=1)  41.1 us
  transfers between devices with their start and end apart: 23, of which 4 were waited for; matrix products, arithmetic and copies ran while one was open for 11% of the time, Pallas kernels for 0%

commit v1 on v0

v1 whole, which is shorter than its diff:
```python
import functools

import jax
import jax.numpy as jnp
from jax import lax
from jax.experimental import pallas as pl
from jax.experimental.pallas import tpu as pltpu
from jax.sharding import PartitionSpec as P

HEIGHT = 32
WIDTH = 32
HALF_HEIGHT = HEIGHT // 2
HALF_WIDTH = WIDTH // 2
CELLS = HALF_HEIGHT * HALF_WIDTH
GROUP = 64
FINE = 4 * GROUP
RIM = HALF_WIDTH
PADDED = CELLS + 2 * RIM

epsilon = 1e-05
momentum_decay = 0.9
learning_rate = 1e-05
scale_rate = 0.0002
weight_decay = 0.0001
average_decay = 0.75

MESH = pl.DeviceIdType.MESH
F32 = jnp.float32
BF16 = jnp.bfloat16
VMEM_LIMIT = 60 * 1024 * 1024


def params(**kwargs):
    return pltpu.CompilerParams(vmem_limit_bytes=VMEM_LIMIT, **kwargs)


def halo_steps(refs, sems):
    mp, md = lax.axis_index("patch"), lax.axis_index("depth")
    last = lax.axis_size("depth") - 1
    copies = []
    for index, (source, below, above) in enumerate(refs):
        planes = source.shape[1]
        up = pltpu.make_async_remote_copy(
            src_ref=source.at[:, planes - 1],
            dst_ref=below,
            send_sem=sems.at[4 * index],
            recv_sem=sems.at[4 * index + 1],
            device_id=(mp, jnp.minimum(md + 1, last)),
            device_id_type=MESH,
        )
        down = pltpu.make_async_remote_copy(
            src_ref=source.at[:, 0],
            dst_ref=above,
            send_sem=sems.at[4 * index + 2],
            recv_sem=sems.at[4 * index + 3],
            device_id=(mp, jnp.maximum(md - 1, 0)),
            device_id_type=MESH,
        )
        copies.append((up, down))

    def start():
        for up, down in copies:

            @pl.when(md < last)
            def _():
                up.start()

            @pl.when(md > 0)
            def _():
                down.start()

    def finish():
        for up, down in copies:

            @pl.when(md < last)
            def _():
                up.wait_send()
                down.wait_recv()

            @pl.when(md > 0)
            def _():
                down.wait_send()
                up.wait_recv()

    return start, finish


def halo_kernel(count, *refs):
    sources, outs, sems = refs[:count], refs[count : 3 * count], refs[3 * count]
    mp, md = lax.axis_index("patch"), lax.axis_index("depth")
    last = lax.axis_size("depth") - 1
    barrier = pltpu.get_barrier_semaphore()

    @pl.when(md < last)
    def _():
        pl.semaphore_signal(barrier, inc=1, device_id=(mp, md + 1), device_id_type=MESH)

    @pl.when(md > 0)
    def _():
        pl.semaphore_signal(barrier, inc=1, device_id=(mp, md - 1), device_id_type=MESH)

    @pl.when(md < last)
    def _():
        pl.semaphore_wait(barrier, 1)

    @pl.when(md > 0)
    def _():
        pl.semaphore_wait(barrier, 1)

    start, finish = halo_steps(
        [(sources[i], outs[2 * i], outs[2 * i + 1]) for i in range(count)], sems
    )
    start()
    finish()


def rim_shapes(arrays):
    shapes = []
    for array in arrays:
        shape = (array.shape[0],) + array.shape[2:]
        shapes += [jax.ShapeDtypeStruct(shape, array.dtype)] * 2
    return shapes


def exchange_rims(arrays, number):
    anywhere = pl.BlockSpec(memory_space=pl.ANY)
    return pl.pallas_call(
        functools.partial(halo_kernel, len(arrays)),
        out_shape=rim_shapes(arrays),
        in_specs=[anywhere] * len(arrays),
        out_specs=[anywhere] * (2 * len(arrays)),
        scratch_shapes=[pltpu.SemaphoreType.DMA((4 * len(arrays),))],
        compiler_params=params(collective_id=number, has_side_effects=True),
    )(*arrays)


def combine(values, moments, count):
    first = [value[0:1] for value in values]
    second = [value[1:2] for value in values]
    if not moments:
        return functools.reduce(jnp.add, first), functools.reduce(jnp.add, second)
    mean = functools.reduce(jnp.add, first) * (1.0 / len(values))
    spread = functools.reduce(jnp.add, [(value - mean) * (value - mean) for value in first])
    return mean, functools.reduce(jnp.add, second) + count * spread


def reduce_kernel(npat, ndep, low, moments, samples, count, *refs):
    stats, sources = refs[0], refs[1 : 1 + count]
    result, outs = refs[1 + count], refs[2 + count : 2 + 3 * count]
    near, far, near_send, near_recv, far_send, far_recv = refs[2 + 3 * count : 8 + 3 * count]
    mp, md = lax.axis_index("patch"), lax.axis_index("depth")
    high, peers = npat // low, low * ndep
    mine_low, mine_high = lax.rem(mp, low), mp // low
    place = mine_low * ndep + md

    def near_device(step):
        other = lax.rem(place + step, peers)
        return (mine_high * low + other // ndep, lax.rem(other, ndep))

    def far_device(step):
        return (lax.rem(mine_high + step, high) * low + mine_low, md)

    barrier = pltpu.get_barrier_semaphore()
    for device, size in ((far_device, high), (near_device, peers)):
        for step in range(1, size):
            pl.semaphore_signal(barrier, inc=1, device_id=device(step), device_id_type=MESH)
    width = stats.shape[-1]
    amount = samples
    first, second = combine([stats[index] for index in range(stats.shape[0])], moments, amount)
    amount = amount * stats.shape[0]
    if width == FINE:
        pair = jnp.concatenate([first, second, jnp.zeros((6, width), F32)], axis=0)
        turned = [pair] + [pltpu.roll(pair, step * GROUP, 1) for step in range(1, 4)]
        first, second = combine(turned, moments, amount)
        amount = amount * 4
    near[0, 0:1] = first
    near[0, 1:2] = second
    pl.semaphore_wait(barrier, high + peers - 2)
    if count:
        start, finish = halo_steps(
            [(sources[i], outs[2 * i], outs[2 * i + 1]) for i in range(count)], refs[8 + 3 * count]
        )
        start()
    for device, size, buffer, send, recv in (
        (near_device, peers, near, near_send, near_recv),
        (far_device, high, far, far_send, far_recv),
    ):
        copies = [
            pltpu.make_async_remote_copy(
                src_ref=buffer.at[0],
                dst_ref=buffer.at[step],
                send_sem=send.at[step],
                recv_sem=recv.at[step],
                device_id=device(step),
                device_id_type=MESH,
            )
            for step in range(1, size)
        ]
        for copy in copies:
            copy.start()
        for copy in copies:
            copy.wait_recv()
        first, second = combine([buffer[index] for index in range(size)], moments, amount)
        amount = amount * size
        if buffer is near:
            far[0, 0:1] = first
            far[0, 1:2] = second
        for copy in copies:
            copy.wait_send()
    result[0:1] = first * (1.0 if moments else 1.0 / amount)
    result[1:2] = second * (1.0 / amount)
    result[2:3] = first
    result[3:4] = second
    if count:
        finish()


def all_reduce_stats(stats, moments, samples, arrays, number):
    npat, ndep = lax.axis_size("patch"), lax.axis_size("depth")
    low = 4 if npat % 4 == 0 else 1
    width = stats.shape[-1]
    anywhere = pl.BlockSpec(memory_space=pl.ANY)
    inside = pl.BlockSpec(memory_space=pltpu.VMEM)
    dma = pltpu.SemaphoreType.DMA
    scratch = [
        pltpu.VMEM((low * ndep, 2, width), F32),
        pltpu.VMEM((npat // low, 2, width), F32),
        dma((low * ndep,)),
        dma((low * ndep,)),
        dma((npat // low,)),
        dma((npat // low,)),
    ]
    if arrays:
        scratch.append(dma((4 * len(arrays),)))
    return pl.pallas_call(
        functools.partial(reduce_kernel, npat, ndep, low, moments, float(samples), len(arrays)),
        out_shape=[jax.ShapeDtypeStruct((8, width), F32)] + rim_shapes(arrays),
        in_specs=[inside] + [anywhere] * len(arrays),
        out_specs=[inside] + [anywhere] * (2 * len(arrays)),
        scratch_shapes=scratch,
        compiler_params=params(collective_id=number, has_side_effects=True),
    )(stats, *arrays)


def lane_is_low(shape):
    return (lax.broadcasted_iota(jnp.int32, shape, 1) & (2 * GROUP - 1)) < GROUP


def row_column(shape):
    return lax.broadcasted_iota(jnp.int32, shape, 0) & (HALF_WIDTH - 1)


def normalize(values, stats):
    return (values - stats[0:1]) * lax.rsqrt(stats[1:2] + epsilon)


def silu(values):
    return values * jax.nn.sigmoid(values)


def silu_slope(values):
    sigma = jax.nn.sigmoid(values)
    return sigma * (1.0 + values * (1.0 - sigma))


def norm_silu(values, stats, scale):
    return silu(normalize(values, stats) * scale[0:1] + scale[1:2])


def norm_back(grad, normed, stats, sums, scale):
    factor = scale[0:1] * lax.rsqrt(stats[1:2] + epsilon)
    return (grad - sums[0:1] - normed * sums[1:2]) * factor


def edge_flags():
    md = lax.axis_index("depth")
    return md == 0, md == lax.axis_size("depth") - 1


def at_edge(flag, inside, outside):
    keep = jnp.where(flag, 1, 0) + jnp.zeros(inside.shape, jnp.int32)
    return jnp.where(keep > 0, outside, inside)


def zero_rims(spread):
    zeros = jnp.zeros((spread.shape[0], RIM, spread.shape[2]), spread.dtype)
    spread[:, 0:RIM] = zeros
    spread[:, RIM + CELLS :] = zeros


def spread_pair(spread, plane, column, pair, turned, low):
    before = jnp.where(low, pltpu.roll(turned, 1, 0), turned)
    after = jnp.where(low, turned, pltpu.roll(turned, CELLS - 1, 0))
    width = 2 * GROUP
    spread[plane, pl.ds(RIM, CELLS), column : column + width] = before.astype(BF16)
    spread[plane, pl.ds(RIM, CELLS), column + width : column + 2 * width] = after.astype(BF16)


def spread_fine(spread, plane, groups, group, values):
    width = 2 * GROUP
    low = lane_is_low((CELLS, width))
    for parity in range(2):
        pair = values[:, parity * width : (parity + 1) * width]
        turned = pltpu.roll(pair, GROUP, 1)
        spread_pair(spread, plane, (parity * groups + group) * FINE, pair, turned, low)


def spread_coarse(spread, plane, groups, values):
    low = lane_is_low((CELLS, 2 * GROUP))
    turned = pltpu.roll(values, GROUP, 1)
    for group in range(groups):
        one, other = (values, turned) if group == 0 else (turned, values)
        before = jnp.where(low, pltpu.roll(one, 1, 0), other)
        after = jnp.where(low, one, pltpu.roll(other, CELLS - 1, 0))
        column = group * FINE
        spread[plane, pl.ds(RIM, CELLS), column : column + 128] = before.astype(BF16)
        spread[plane, pl.ds(RIM, CELLS), column + 128 : column + 256] = after.astype(BF16)


fine_rows = ((0, 1), (1, 0), (1, 1), (2, 0))


def stack_fine(spread, masks, stack, groups, depth):
    for slot in range(4):
        level = (slot + 1) // 2
        for plane in range(depth):
            for index, (step, parity) in enumerate(fine_rows):
                mask = masks[3 * level + step, 0, plane * CELLS : (plane + 1) * CELLS, :]
                for group in range(groups):
                    source = (parity * groups + group) * FINE
                    target = (index * groups + group) * FINE
                    row = (slot * depth + plane) * CELLS
                    stack[row : row + CELLS, target : target + FINE] = (
                        spread[
                            2 * plane + slot, step * RIM : step * RIM + CELLS, source : source + FINE
                        ]
                        * mask
                    )


def stack_coarse(spread, masks, stack, groups, depth):
    for slot in range(3):
        for plane in range(depth):
            row = (slot * depth + plane) * CELLS
            for step in range(3):
                mask = masks[3 * slot + step, 0, plane * CELLS : (plane + 1) * CELLS, :]
                for group in range(groups):
                    target = (step * groups + group) * FINE
                    stack[row : row + CELLS, target : target + FINE] = (
                        spread[
                            plane + slot,
                            step * RIM : step * RIM + CELLS,
                            group * FINE : (group + 1) * FINE,
                        ]
                        * mask
                    )


def fine_weights(weights, kernel, groups_in, groups_out):
    weights[...] = jnp.zeros(weights.shape, BF16)

    def fill(level, carry):
        for step in range(9):
            row_step, column_step = step // 3, step % 3
            block = kernel[9 * level + step].astype(BF16)
            for phase in range(4):
                row_slot, column_slot = phase // 2 + row_step, phase % 2 + column_step
                for source in range(groups_in):
                    row = ((row_slot * groups_in + source) * 4 + column_slot) * GROUP
                    for target in range(groups_out):
                        column = target * FINE + phase * GROUP
                        weights[level, row : row + GROUP, column : column + GROUP] = block[
                            source * GROUP : (source + 1) * GROUP,
                            target * GROUP : (target + 1) * GROUP,
                        ]
        return carry

    lax.fori_loop(0, 3, fill, 0)


def coarse_weights(weights, kernel, groups_in):
    weights[...] = jnp.zeros(weights.shape, BF16)

    def fill(level, carry):
        for step in range(9):
            row_step, column_slot = step // 3, (0, 1, 3)[step % 3]
            block = kernel[9 * level + step].astype(BF16)
            for source in range(groups_in):
                row = ((row_step * groups_in + source) * 4 + column_slot) * GROUP
                weights[level, row : row + GROUP, :] = block[source * GROUP : (source + 1) * GROUP]
        return carry

    lax.fori_loop(0, 3, fill, 0)


def fine_kernel_grad(out, sums, groups):
    def fill(level, carry):
        for step in range(9):
            row_step, column_step = step // 3, step % 3
            for group in range(groups):
                total = None
                for phase in range(4):
                    row = group * FINE + phase * GROUP
                    slot = (phase // 2 + row_step) * 4 + phase % 2 + column_step
                    block = sums[level, row : row + GROUP, slot * GROUP : (slot + 1) * GROUP]
                    total = block if total is None else total + block
                out[26 - (9 * level + step), group * GROUP : (group + 1) * GROUP, :] = total
        return carry

    lax.fori_loop(0, 3, fill, 0)


def coarse_kernel_grad(out, sums, groups):
    def fill(level, carry):
        for step in range(9):
            row_step, column_slot = step // 3, (0, 1, 3)[step % 3]
            blocks = []
            for group in range(groups):
                slot = (row_step * groups + group) * 4 + column_slot
                blocks.append(sums[level, :, slot * GROUP : (slot + 1) * GROUP])
            out[26 - (9 * level + step)] = jnp.concatenate(blocks, axis=1)
        return carry

    lax.fori_loop(0, 3, fill, 0)


def apply_weights(stack, weights, rows, step_rows):
    total = None
    for level in range(3):
        begin = level * step_rows
        term = jnp.dot(stack[begin : begin + rows, :], weights[level], preferred_element_type=F32)
        total = term if total is None else total + term
    return total


def identity(size):
    rows = lax.broadcasted_iota(jnp.int32, (size, size), 0)
    columns = lax.broadcasted_iota(jnp.int32, (size, size), 1)
    return jnp.where(rows == columns, 1.0, 0.0).astype(BF16)


def transposed(values, unit):
    return lax.dot_general(
        unit, values, (((1,), (1,)), ((), ())), preferred_element_type=F32
    ).astype(BF16)


def two_parts(values):
    high = values.astype(BF16)
    return high, (values - high.astype(F32)).astype(BF16)


def dot_exact(values, weights):
    high, low = two_parts(values)
    return jnp.dot(high, weights, preferred_element_type=F32) + jnp.dot(
        low, weights, preferred_element_type=F32
    )


def moments_of(values):
    mean = jnp.mean(values, axis=0, keepdims=True)
    return mean, jnp.sum(jnp.square(values - mean), axis=0, keepdims=True)


def voxel_order(size, transpose):
    rows = lax.broadcasted_iota(jnp.int32, (size, size), 1 if transpose else 0)
    columns = lax.broadcasted_iota(jnp.int32, (size, size), 0 if transpose else 1)
    phase, cell = rows // CELLS, rows % CELLS
    row = 2 * (cell // HALF_WIDTH) + phase // 2
    column = 2 * (cell % HALF_WIDTH) + phase % 2
    return jnp.where(columns == row * WIDTH + column, 1.0, 0.0).astype(BF16)


def prepare_kernel(skip, grad, ids, skip_out, grad_out, pooled, masks, order, spread):
    planes = skip.shape[1]
    depth = planes // 2
    size = 4 * CELLS

    @pl.when(pl.program_id(0) == 0)
    def _():
        order[...] = voxel_order(size, False)
        spread[...] = jnp.zeros(spread.shape, F32)

    for source, target in ((skip, skip_out), (grad, grad_out)):
        lines = source[0].reshape(planes * GROUP, size)
        turned = lax.dot_general(
            order[...], lines, (((1,), (1,)), ((), ())), preferred_element_type=F32
        )
        for plane in range(planes):
            pieces = [
                turned[phase * CELLS : (phase + 1) * CELLS, plane * GROUP : (plane + 1) * GROUP]
                for phase in range(4)
            ]
            target[0, plane] = jnp.concatenate(pieces, axis=1).astype(BF16)
    for plane in range(depth):
        total = skip_out[0, 2 * plane].astype(F32) + skip_out[0, 2 * plane + 1].astype(F32)
        total = total[:, : 2 * GROUP] + total[:, 2 * GROUP :]
        total = total + pltpu.roll(total, GROUP, 1)
        pooled[0, plane] = (total * 0.125).astype(BF16)
    for plane in range(depth + 2):
        spread[plane, 2 * RIM : 2 * RIM + CELLS] = ids[0, plane].astype(F32)
    column = row_column((CELLS, 2 * GROUP))
    low = lane_is_low((CELLS, 2 * GROUP))
    for plane in range(depth):
        center = ids[0, plane + 1].astype(F32)
        for level in range(3):
            for step in range(3):
                begin = RIM + step * RIM
                found = []
                for side in range(3):
                    beside = spread[plane + level, begin + side - 1 : begin + side - 1 + CELLS]
                    same = beside == center
                    if side == 0:
                        same = same & (column > 0)
                    if side == 2:
                        same = same & (column < HALF_WIDTH - 1)
                    found.append(jnp.where(same, 1.0, 0.0))
                both = jnp.concatenate(
                    [jnp.where(low, found[0], found[1]), jnp.where(low, found[1], found[2])], axis=1
                )
                masks[3 * level + step, 0, plane * CELLS : (plane + 1) * CELLS] = both.astype(BF16)


def first_kernel(pooled, below, above, masks, kernel, pre, stats, spread, stack, weights):
    depth = pooled.shape[1]

    @pl.when(pl.program_id(0) == 0)
    def _():
        zero_rims(spread)
        coarse_weights(weights, kernel, 1)

    first, last = edge_flags()
    for plane in range(depth):
        spread_coarse(spread, plane + 1, 1, pooled[0, plane].astype(F32))
    for flag, rim, plane in ((first, below, 0), (last, above, depth + 1)):
        values = rim[0].astype(F32)
        spread_coarse(spread, plane, 1, at_edge(flag, values, jnp.zeros_like(values)))
    stack_coarse(spread, masks, stack, 1, depth)
    values = apply_weights(stack, weights, depth * CELLS, depth * CELLS)
    for plane in range(depth):
        pre[0, plane] = values[plane * CELLS : (plane + 1) * CELLS]
    stats[0, 0:1], stats[0, 1:2] = moments_of(values)


def second_kernel(
    z, below, above, stats_in, scale, masks, kernel, pre, out, stats, spread, stack, weights
):
    depth = z.shape[1]

    @pl.when(pl.program_id(0) == 0)
    def _():
        zero_rims(spread)
        coarse_weights(weights, kernel, 2)

    first, last = edge_flags()
    for plane in range(depth):
        values = norm_silu(z[0, plane], stats_in, scale)
        out[0, plane] = values.astype(BF16)
        spread_coarse(spread, plane + 1, 2, values)
    for flag, rim, plane in ((first, below, 0), (last, above, depth + 1)):
        values = norm_silu(rim[0], stats_in, scale)
        spread_coarse(spread, plane, 2, at_edge(flag, values, jnp.zeros_like(values)))
    stack_coarse(spread, masks, stack, 2, depth)
    values = apply_weights(stack, weights, depth * CELLS, depth * CELLS)
    for plane in range(depth):
        pre[0, plane] = values[plane * CELLS : (plane + 1) * CELLS]
    stats[0, 0:1], stats[0, 1:2] = moments_of(values)


def widened(values, low, column):
    before = jnp.concatenate([values[:RIM], values[: CELLS - RIM]], axis=0)
    after = jnp.concatenate([values[RIM:], values[CELLS - RIM :]], axis=0)
    result = []
    for beside in (before, after):
        line = 0.75 * values + 0.25 * beside
        left = jnp.where(column == 0, line, pltpu.roll(line, 1, 0))
        right = jnp.where(column == HALF_WIDTH - 1, line, pltpu.roll(line, CELLS - 1, 0))
        result.append((0.75 * line + 0.25 * left, 0.75 * line + 0.25 * right))
    return result


def third_kernel(
    z,
    below,
    above,
    stats_in,
    scale,
    skip,
    skip_below,
    skip_above,
    gates,
    gate_rows,
    masks,
    kernel,
    pre,
    attended,
    upsampled,
    query,
    stats,
    coarse,
    spread,
    stack,
    weights,
):
    depth = z.shape[1]
    planes = 2 * depth
    width = 2 * GROUP

    @pl.when(pl.program_id(0) == 0)
    def _():
        zero_rims(spread)
        fine_weights(weights, kernel, 3, 1)

    first, last = edge_flags()
    for plane in range(depth):
        values = norm_silu(z[0, plane], stats_in, scale)
        coarse[plane + 1] = values.astype(BF16).astype(F32)
    for flag, rim, plane, inner in ((first, below, 0, 1), (last, above, depth + 1, depth)):
        values = norm_silu(rim[0], stats_in, scale).astype(BF16).astype(F32)
        coarse[plane] = at_edge(flag, values, coarse[inner])
    low = lane_is_low((CELLS, width))
    column = row_column((CELLS, width))
    span = gate_rows.shape[1]
    spans = lax.broadcasted_iota(jnp.int32, (span, FINE), 0) // (span // 4)
    lanes = lax.broadcasted_iota(jnp.int32, (span, FINE), 1) // GROUP
    gather = jnp.where(spans == lanes, 1.0, 0.0).astype(BF16)
    for index in range(planes + 2):
        fine = index - 1
        center = fine // 2
        other = center - 1 if fine % 2 == 0 else center + 1
        doubled = 0.75 * coarse[center + 1] + 0.25 * coarse[other + 1]
        grid = widened(doubled, low, column)
        pieces = []
        for group in range(2):
            for parity in range(2):
                even, odd = grid[parity]
                if group == 0:
                    pair = jnp.where(low, even, pltpu.roll(odd, GROUP, 1))
                else:
                    pair = jnp.where(low, pltpu.roll(even, GROUP, 1), odd)
                pair = pair.astype(BF16)
                pieces.append(pair)
                pair = pair.astype(F32)
                turned = pltpu.roll(pair, GROUP, 1)
                spread_pair(spread, index, (parity * 3 + 1 + group) * FINE, pair, turned, low)
        up = jnp.concatenate(pieces, axis=1)
        if fine < 0:
            features = at_edge(first, skip_below[0].astype(F32), 0.0).astype(BF16)
        elif fine == planes:
            features = at_edge(last, skip_above[0].astype(F32), 0.0).astype(BF16)
        else:
            features = skip[0, fine]
        asked = (
            jnp.dot(features, gates[:FINE], preferred_element_type=F32)
            + jnp.dot(up, gates[FINE:], preferred_element_type=F32)
            + gate_rows[0:1]
        )
        logits = dot_exact(silu(asked) * gate_rows[1:2], gather)
        kept = (features.astype(F32) * jax.nn.sigmoid(logits)).astype(BF16)
        spread_fine(spread, index, 3, 0, kept.astype(F32))
        if 0 <= fine < planes:
            attended[0, fine] = kept
            upsampled[0, fine] = up
            query[0, fine] = asked
    stack_fine(spread, masks, stack, 3, depth)
    values = apply_weights(stack, weights, planes * CELLS, depth * CELLS)
    for block in range(planes):
        fine = 2 * (block % depth) + block // depth
        pre[0, fine] = values[block * CELLS : (block + 1) * CELLS]
    stats[0, 0:1], stats[0, 1:2] = moments_of(values)


def fourth_kernel(
    z, below, above, stats_in, scale, masks, kernel, pre, out, stats, spread, stack, weights
):
    planes = z.shape[1]
    depth = planes // 2

    @pl.when(pl.program_id(0) == 0)
    def _():
        zero_rims(spread)
        fine_weights(weights, kernel, 1, 1)

    first, last = edge_flags()
    for plane in range(planes):
        values = norm_silu(z[0, plane], stats_in, scale)
        out[0, plane] = values.astype(BF16)
        spread_fine(spread, plane + 1, 1, 0, values)
    for flag, rim, plane in ((first, below, 0), (last, above, planes + 1)):
        values = norm_silu(rim[0], stats_in, scale)
        spread_fine(spread, plane, 1, 0, at_edge(flag, values, jnp.zeros_like(values)))
    stack_fine(spread, masks, stack, 1, depth)
    values = apply_weights(stack, weights, planes * CELLS, depth * CELLS)
    for block in range(planes):
        fine = 2 * (block % depth) + block // depth
        pre[0, fine] = values[block * CELLS : (block + 1) * CELLS]
    stats[0, 0:1], stats[0, 1:2] = moments_of(values)


def to_voxels(out, planes, order, parts):
    total = None
    for part in range(parts):
        blocks = []
        for phase in range(4):
            pieces = [values[:, phase * GROUP : (phase + 1) * GROUP] for values in planes]
            blocks.append(jnp.concatenate(pieces, axis=1).astype(BF16))
        stacked = jnp.concatenate(blocks, axis=0)
        term = jnp.dot(order[...], stacked, preferred_element_type=F32)
        total = term if total is None else total + term
        if part + 1 < parts:
            planes = [values - values.astype(BF16).astype(F32) for values in planes]
    lines = total.T
    for plane in range(len(planes)):
        out[0, plane] = lines[plane * GROUP : (plane + 1) * GROUP].astype(out.dtype)


def decoded_kernel(z, grad, stats_in, scale, decoded, sums, order):
    planes = z.shape[1]

    @pl.when(pl.program_id(0) == 0)
    def _():
        order[...] = voxel_order(4 * CELLS, True)

    first, second, made = 0.0, 0.0, []
    for plane in range(planes):
        normed = normalize(z[0, plane], stats_in)
        active = normed * scale[0:1] + scale[1:2]
        made.append(silu(active))
        upstream = grad[0, plane].astype(F32) * silu_slope(active)
        first = first + jnp.sum(upstream, axis=0, keepdims=True)
        second = second + jnp.sum(upstream * normed, axis=0, keepdims=True)
    sums[0, 0:1] = first
    sums[0, 1:2] = second
    to_voxels(decoded, made, order, 1)


def closing_back_kernel(
    z,
    below,
    above,
    grad,
    grad_below,
    grad_above,
    stats_in,
    sums_in,
    scale,
    out,
    z_before,
    stats_before,
    scale_before,
    masks,
    kernel,
    back,
    sums,
    kernel_grad,
    spread,
    stack,
    weights,
    turned,
    totals,
    given,
):
    planes = z.shape[1]
    depth = planes // 2
    step = pl.program_id(0)

    @pl.when(step == 0)
    def _():
        zero_rims(spread)
        fine_weights(weights, kernel, 1, 1)
        totals[...] = jnp.zeros(totals.shape, F32)

    first, last = edge_flags()

    def rounded(values, cotangent):
        normed = normalize(values, stats_in)
        upstream = cotangent.astype(F32) * silu_slope(normed * scale[0:1] + scale[1:2])
        return norm_back(upstream, normed, stats_in, sums_in, scale)

    for plane in range(planes):
        spread_fine(spread, plane + 1, 1, 0, rounded(z[0, plane], grad[0, plane]))
    for flag, rim, rim_grad, plane in (
        (first, below, grad_below, 0),
        (last, above, grad_above, planes + 1),
    ):
        values = rounded(rim[0], rim_grad[0])
        spread_fine(spread, plane, 1, 0, at_edge(flag, values, jnp.zeros_like(values)))
    stack_fine(spread, masks, stack, 1, depth)
    unit = identity(FINE)
    for block in range(planes):
        fine = 2 * (block % depth) + block // depth
        turned[:, block * CELLS : (block + 1) * CELLS] = transposed(out[0, fine], unit)
    for level in range(3):
        begin = level * depth * CELLS
        totals[level] += jnp.dot(
            turned[...], stack[begin : begin + planes * CELLS], preferred_element_type=F32
        )
    given[...] = apply_weights(stack, weights, planes * CELLS, depth * CELLS)
    first_sum, second_sum = 0.0, 0.0
    for block in range(planes):
        fine = 2 * (block % depth) + block // depth
        normed = normalize(z_before[0, fine], stats_before)
        slope = silu_slope(normed * scale_before[0:1] + scale_before[1:2])
        values = given[block * CELLS : (block + 1) * CELLS] * slope
        back[0, fine] = values
        first_sum = first_sum + jnp.sum(values, axis=0, keepdims=True)
        second_sum = second_sum + jnp.sum(values * normed, axis=0, keepdims=True)
    sums[0, 0:1] = first_sum
    sums[0, 1:2] = second_sum

    @pl.when(step == pl.num_programs(0) - 1)
    def _():
        fine_kernel_grad(kernel_grad, totals, 1)


def narrowed(values, low, column):
    lines = []
    for parity in range(2):
        pair = values[:, parity * 128 : (parity + 1) * 128]
        turned = pltpu.roll(pair, GROUP, 1)
        later = jnp.where(column == HALF_WIDTH - 1, turned, pltpu.roll(pair, CELLS - 1, 0))
        earlier = jnp.where(column == 0, turned, pltpu.roll(pair, 1, 0))
        mixed = 0.75 * pair + 0.25 * jnp.where(low, later, earlier)
        lines.append(mixed + pltpu.roll(mixed, GROUP, 1))
    even, odd = lines
    later = jnp.concatenate([even[RIM:], odd[CELLS - RIM :]], axis=0)
    earlier = jnp.concatenate([even[:RIM], odd[: CELLS - RIM]], axis=0)
    return 0.75 * (even + odd) + 0.25 * (later + earlier)


def merging_back_kernel(
    grad,
    grad_below,
    grad_above,
    z,
    below,
    above,
    stats_in,
    sums_in,
    scale,
    skip,
    attended,
    upsampled,
    query,
    gates,
    gate_rows,
    masks,
    kernel,
    skip_back,
    coarse_back,
    kernel_grad,
    gate_grad,
    spread,
    stack,
    weights,
    turned,
    totals,
    given,
):
    planes = z.shape[1]
    depth = planes // 2
    step = pl.program_id(0)

    @pl.when(step == 0)
    def _():
        zero_rims(spread)
        fine_weights(weights, kernel, 1, 3)
        totals[...] = jnp.zeros(totals.shape, F32)
        gate_grad[...] = jnp.zeros(gate_grad.shape, F32)

    first, last = edge_flags()

    def rounded(values, upstream):
        return norm_back(upstream, normalize(values, stats_in), stats_in, sums_in, scale)

    for plane in range(planes):
        spread_fine(spread, plane + 1, 1, 0, rounded(z[0, plane], grad[0, plane]))
    for flag, rim, rim_grad, plane in (
        (first, below, grad_below, 0),
        (last, above, grad_above, planes + 1),
    ):
        values = rounded(rim[0], rim_grad[0])
        spread_fine(spread, plane, 1, 0, at_edge(flag, values, jnp.zeros_like(values)))
    stack_fine(spread, masks, stack, 1, depth)
    unit = identity(FINE)
    for block in range(planes):
        fine = 2 * (block % depth) + block // depth
        lines = slice(block * CELLS, (block + 1) * CELLS)
        turned[:FINE, lines] = transposed(attended[0, fine], unit)
        turned[FINE : 2 * FINE, lines] = transposed(upsampled[0, fine, :, :FINE], unit)
        turned[2 * FINE : 3 * FINE, lines] = transposed(upsampled[0, fine, :, FINE:], unit)
        turned[3 * FINE :, lines] = transposed(skip[0, fine], unit)
    for level in range(3):
        begin = level * depth * CELLS
        for group in range(3):
            totals[level, group * FINE : (group + 1) * FINE] += jnp.dot(
                turned[group * FINE : (group + 1) * FINE],
                stack[begin : begin + planes * CELLS],
                preferred_element_type=F32,
            )
    for group in range(3):
        columns = slice(group * FINE, (group + 1) * FINE)
        total = None
        for level in range(3):
            begin = level * depth * CELLS
            term = jnp.dot(
                stack[begin : begin + planes * CELLS],
                weights[level, :, columns],
                preferred_element_type=F32,
            )
            total = term if total is None else total + term
        given[:, columns] = total
    span = gate_rows.shape[1]
    part = span // 4

    def ones(rows, columns, row_part, column_part):
        left = lax.broadcasted_iota(jnp.int32, (rows, columns), 0) // row_part
        right = lax.broadcasted_iota(jnp.int32, (rows, columns), 1) // column_part
        return jnp.where(left == right, 1.0, 0.0).astype(BF16)

    to_lanes, to_span = ones(span, FINE, part, GROUP), ones(span, span, part, part)
    from_lanes = ones(FINE, span, GROUP, part)
    low = lane_is_low((CELLS, 2 * GROUP))
    column = row_column((CELLS, 2 * GROUP))
    contract = (((1,), (1,)), ((), ()))
    for block in range(planes):
        fine = 2 * (block % depth) + block // depth
        lines = slice(block * CELLS, (block + 1) * CELLS)
        features = skip[0, fine]
        asked = query[0, fine]
        active = silu(asked)
        high, rest = two_parts(active * gate_rows[1:2])
        dot = functools.partial(jnp.dot, preferred_element_type=F32)
        attention = jax.nn.sigmoid(dot(high, to_lanes) + dot(rest, to_lanes))
        attention_span = jax.nn.sigmoid(dot(high, to_span) + dot(rest, to_span))
        attended_back = given[lines, :FINE]
        attention_back = dot_exact(attended_back * features.astype(F32), from_lanes)
        logit_back = attention_back * attention_span * (1.0 - attention_span)
        query_back = (logit_back * gate_rows[1:2] * silu_slope(asked)).astype(BF16)
        psi = jnp.sum(logit_back * active, axis=0, keepdims=True)
        bias = jnp.sum(query_back.astype(F32), axis=0, keepdims=True)
        gate_grad[:FINE] += dot(turned[3 * FINE :, lines], query_back)
        gate_grad[FINE : 3 * FINE] += dot(turned[FINE : 3 * FINE, lines], query_back)
        gate_grad[3 * FINE : 3 * FINE + 1] += bias
        gate_grad[3 * FINE + 1 : 3 * FINE + 2] += psi
        skip_back[0, fine] = attended_back * attention + lax.dot_general(
            query_back, gates[:FINE], contract, preferred_element_type=F32
        )
        up = given[lines, FINE:] + lax.dot_general(
            query_back, gates[FINE:], contract, preferred_element_type=F32
        )
        left = narrowed(up[:, :FINE], low, column)
        right = narrowed(up[:, FINE:], low, column)
        coarse_back[0, fine] = jnp.where(low, left, right)

    @pl.when(step == pl.num_programs(0) - 1)
    def _():
        fine_kernel_grad(kernel_grad, totals, 3)


def coarse_grad_kernel(fine_back, below, above, z, stats_in, scale, back, sums):
    depth = z.shape[1]
    first, last = edge_flags()
    first_sum, second_sum = 0.0, 0.0
    for plane in range(depth):
        even, odd = fine_back[0, 2 * plane], fine_back[0, 2 * plane + 1]
        if plane + 1 < depth:
            later = fine_back[0, 2 * plane + 2]
        else:
            later = at_edge(last, above[0], odd)
        if plane > 0:
            earlier = fine_back[0, 2 * plane - 1]
        else:
            earlier = at_edge(first, below[0], even)
        values = 0.75 * (even + odd) + 0.25 * (later + earlier)
        normed = normalize(z[0, plane], stats_in)
        values = values * silu_slope(normed * scale[0:1] + scale[1:2])
        back[0, plane] = values
        first_sum = first_sum + jnp.sum(values, axis=0, keepdims=True)
        second_sum = second_sum + jnp.sum(values * normed, axis=0, keepdims=True)
    sums[0, 0:1] = first_sum
    sums[0, 1:2] = second_sum


def coarse_stack(grad, grad_rims, z, rims, stats_in, sums_in, scale, masks, spread, stack):
    depth = z.shape[1]
    first, last = edge_flags()

    def rounded(values, upstream):
        return norm_back(upstream, normalize(values, stats_in), stats_in, sums_in, scale)

    for plane in range(depth):
        spread_coarse(spread, plane + 1, 2, rounded(z[0, plane], grad[0, plane]))
    for flag, rim, rim_grad, plane in (
        (first, rims[0], grad_rims[0], 0),
        (last, rims[1], grad_rims[1], depth + 1),
    ):
        values = rounded(rim[0], rim_grad[0])
        spread_coarse(spread, plane, 2, at_edge(flag, values, jnp.zeros_like(values)))
    stack_coarse(spread, masks, stack, 2, depth)


def bottom_back_kernel(
    grad,
    grad_below,
    grad_above,
    z,
    below,
    above,
    stats_in,
    sums_in,
    scale,
    out,
    z_before,
    stats_before,
    scale_before,
    masks,
    kernel,
    back,
    sums,
    kernel_grad,
    spread,
    stack,
    weights,
    totals,
):
    depth = z.shape[1]
    step = pl.program_id(0)

    @pl.when(step == 0)
    def _():
        zero_rims(spread)
        coarse_weights(weights, kernel, 2)
        totals[...] = jnp.zeros(totals.shape, F32)

    coarse_stack(
        grad,
        (grad_below, grad_above),
        z,
        (below, above),
        stats_in,
        sums_in,
        scale,
        masks,
        spread,
        stack,
    )
    unit = identity(2 * GROUP)
    turned = jnp.concatenate([transposed(out[0, plane], unit) for plane in range(depth)], axis=1)
    for level in range(3):
        begin = level * depth * CELLS
        totals[level] += jnp.dot(
            turned, stack[begin : begin + depth * CELLS], preferred_element_type=F32
        )
    given = apply_weights(stack, weights, depth * CELLS, depth * CELLS)
    first_sum, second_sum = 0.0, 0.0
    for plane in range(depth):
        normed = normalize(z_before[0, plane], stats_before)
        slope = silu_slope(normed * scale_before[0:1] + scale_before[1:2])
        values = given[plane * CELLS : (plane + 1) * CELLS] * slope
        back[0, plane] = values
        first_sum = first_sum + jnp.sum(values, axis=0, keepdims=True)
        second_sum = second_sum + jnp.sum(values * normed, axis=0, keepdims=True)
    sums[0, 0:1] = first_sum
    sums[0, 1:2] = second_sum

    @pl.when(step == pl.num_programs(0) - 1)
    def _():
        coarse_kernel_grad(kernel_grad, totals, 2)


def widening_back_kernel(
    grad,
    grad_below,
    grad_above,
    z,
    below,
    above,
    stats_in,
    sums_in,
    scale,
    pooled,
    skip_back,
    masks,
    kernel,
    skip_grad,
    kernel_grad,
    spread,
    stack,
    weights,
    totals,
    order,
):
    depth = z.shape[1]
    step = pl.program_id(0)

    @pl.when(step == 0)
    def _():
        zero_rims(spread)
        coarse_weights(weights, kernel, 2)
        totals[...] = jnp.zeros(totals.shape, F32)
        order[...] = voxel_order(4 * CELLS, True)

    coarse_stack(
        grad,
        (grad_below, grad_above),
        z,
        (below, above),
        stats_in,
        sums_in,
        scale,
        masks,
        spread,
        stack,
    )
    unit = identity(2 * GROUP)
    turned = jnp.concatenate([transposed(pooled[0, plane], unit) for plane in range(depth)], axis=1)
    for level in range(3):
        begin = level * depth * CELLS
        totals[level] += jnp.dot(
            turned[:GROUP], stack[begin : begin + depth * CELLS], preferred_element_type=F32
        )
    given = apply_weights(stack, weights, depth * CELLS, depth * CELLS) * 0.125
    made = []
    for plane in range(depth):
        values = given[plane * CELLS : (plane + 1) * CELLS]
        values = jnp.concatenate([values] * 4, axis=1)
        for parity in range(2):
            made.append(skip_back[0, 2 * plane + parity] + values)
    to_voxels(skip_grad, made, order, 2)

    @pl.when(step == pl.num_programs(0) - 1)
    def _():
        coarse_kernel_grad(kernel_grad, totals, 2)


def update_state(weight, grad, velocity, average, decay, rate):
    step = grad + decay * weight
    momentum = momentum_decay * velocity + step
    weight_next = weight - rate * (step + momentum_decay * momentum)
    smoothed = average_decay * average + (1.0 - average_decay) * weight_next
    return (weight_next, momentum, smoothed, weight_next.astype(jnp.bfloat16))


def by_patch(array):
    rest = array.shape[1:]
    zeros = (0,) * len(rest)
    return pl.BlockSpec((1,) + rest, lambda p: (p,) + zeros)


def mask_spec(array):
    shape = array.shape
    return pl.BlockSpec((shape[0], 1) + shape[2:], lambda p: (0, p, 0, 0))


WHOLE = pl.BlockSpec(memory_space=pltpu.VMEM)


def shape(*sizes, dtype=F32):
    return jax.ShapeDtypeStruct(sizes, dtype)


def run(kernel, patches, inputs, outputs, scratch):
    in_specs = [by_patch(array) if spec is None else spec for array, spec in inputs]
    out_specs = [by_patch(array) if spec is None else spec for array, spec in outputs]
    return pl.pallas_call(
        kernel,
        grid=(patches,),
        out_shape=[array for array, _ in outputs],
        in_specs=in_specs,
        out_specs=out_specs,
        scratch_shapes=scratch,
        compiler_params=params(dimension_semantics=("arbitrary",)),
    )(*[array for array, _ in inputs])


def constant(array):
    zeros = (0,) * len(array.shape)
    return pl.BlockSpec(array.shape, lambda p: zeros)


def flipped(kernel):
    return jnp.transpose(kernel[::-1], (0, 2, 1))


def padded_ids(volume_ids, depth):
    patches = volume_ids.shape[0]
    coarse = volume_ids.reshape(patches, depth, 2, HALF_HEIGHT, 2, HALF_WIDTH, 2)
    coarse = coarse[:, :, 0, :, 0, :, 0].reshape(patches, depth, CELLS).astype(BF16)
    peers = lax.axis_size("depth")
    up = [(i, i + 1) for i in range(peers - 1)]
    down = [(j, i) for i, j in up]
    before = lax.ppermute(coarse[:, depth - 1 :], "depth", up)
    after = lax.ppermute(coarse[:, :1], "depth", down)
    return jnp.concatenate([before, coarse, after], axis=1)


def vmem(*sizes, dtype=BF16):
    return pltpu.VMEM(sizes, dtype)


def local(
    skip_features,
    volume_ids,
    output_grad,
    widening,
    widening_velocity,
    widening_average,
    bottom,
    bottom_velocity,
    bottom_average,
    merging,
    merging_velocity,
    merging_average,
    closing,
    closing_velocity,
    closing_average,
    gating,
    gating_velocity,
    gating_average,
    scales,
    scales_velocity,
    scales_average,
    debug=False,
):
    patches, channels, planes, cells = skip_features.shape
    depth = planes // 2
    inner = gating.shape[1]
    span = 4 * inner
    ids = padded_ids(volume_ids, depth)
    ids = jnp.broadcast_to(ids[..., None], ids.shape + (2 * GROUP,))
    gains, shifts = scales[0], scales[1]
    encoder = bottom.shape[2]
    decoder = closing.shape[2]
    scale = []
    begin = 0
    for size, repeat in ((encoder, 1), (encoder, 1), (decoder, 4), (decoder, 4)):
        scale.append(jnp.tile(scales[:, begin : begin + size], (1, repeat)))
        begin += size
    eye = jnp.eye(4, dtype=F32)
    projection = gating[: channels + encoder].reshape(3, GROUP, inner)
    gates = jnp.einsum("gca,pq->gpcqa", projection, eye).reshape(3 * FINE, span).astype(BF16)
    gate_rows = jnp.tile(gating[channels + encoder :], (1, 4))

    skip_by_plane = jnp.transpose(skip_features, (0, 2, 1, 3))
    grad_by_plane = jnp.transpose(output_grad, (0, 2, 1, 3))
    fine = shape(patches, planes, CELLS, FINE)
    fine_low = shape(patches, planes, CELLS, FINE, dtype=BF16)
    coarse = shape(patches, depth, CELLS, 2 * GROUP)
    coarse_low = shape(patches, depth, CELLS, 2 * GROUP, dtype=BF16)
    masks_shape = shape(9, patches, depth * CELLS, FINE, dtype=BF16)
    skip, grad, pooled, masks = run(
        prepare_kernel,
        patches,
        [(skip_by_plane, None), (grad_by_plane, None), (ids, None)],
        [(fine_low, None), (fine_low, None), (coarse_low, None), (masks_shape, mask_spec(masks_shape))],
        [vmem(4 * CELLS, 4 * CELLS), vmem(depth + 2, CELLS + 4 * RIM, 2 * GROUP, dtype=F32)],
    )
    skip_below, skip_above, grad_below, grad_above, pooled_below, pooled_above = exchange_rims(
        [skip, grad, pooled], 1
    )
    masked = (masks, mask_spec(masks))
    stats_fine = shape(patches, 8, FINE)
    stats_coarse = shape(patches, 8, 2 * GROUP)
    fine_spread = lambda groups: vmem(planes + 2, PADDED, groups * 2 * FINE)
    fine_stack = lambda groups: vmem(4 * depth * CELLS, groups * 4 * FINE)
    coarse_spread = lambda groups: vmem(depth + 2, PADDED, groups * FINE)
    coarse_stacked = lambda groups: vmem(3 * depth * CELLS, groups * 3 * FINE)

    z_one, stats_one = run(
        first_kernel,
        patches,
        [(pooled, None), (pooled_below, None), (pooled_above, None), masked, (widening, WHOLE)],
        [(coarse, None), (stats_coarse, None)],
        [coarse_spread(1), coarse_stacked(1), vmem(3, 3 * FINE, 2 * GROUP)],
    )
    norm_one, below_one, above_one = all_reduce_stats(
        stats_one, True, depth * CELLS, [z_one], 2
    )
    z_two, out_one, stats_two = run(
        second_kernel,
        patches,
        [
            (z_one, None),
            (below_one, None),
            (above_one, None),
            (norm_one, WHOLE),
            (scale[0], WHOLE),
            masked,
            (bottom, WHOLE),
        ],
        [(coarse, None), (coarse_low, None), (stats_coarse, None)],
        [coarse_spread(2), coarse_stacked(2), vmem(3, 6 * FINE, 2 * GROUP)],
    )
    norm_two, below_two, above_two = all_reduce_stats(
        stats_two, True, depth * CELLS, [z_two], 3
    )
    z_three, attended, upsampled, query, stats_three = run(
        third_kernel,
        patches,
        [
            (z_two, None),
            (below_two, None),
            (above_two, None),
            (norm_two, WHOLE),
            (scale[1], WHOLE),
            (skip, None),
            (skip_below, None),
            (skip_above, None),
            (gates, WHOLE),
            (gate_rows, WHOLE),
            masked,
            (merging, WHOLE),
        ],
        [
            (fine, None),
            (fine_low, None),
            (shape(patches, planes, CELLS, 2 * FINE, dtype=BF16), None),
            (shape(patches, planes, CELLS, span), None),
            (stats_fine, None),
        ],
        [
            vmem(depth + 2, CELLS, 2 * GROUP, dtype=F32),
            fine_spread(3),
            fine_stack(3),
            vmem(3, 12 * FINE, FINE),
        ],
    )
    norm_three, below_three, above_three = all_reduce_stats(
        stats_three, True, planes * CELLS, [z_three], 4
    )
    z_four, out_three, stats_four = run(
        fourth_kernel,
        patches,
        [
            (z_three, None),
            (below_three, None),
            (above_three, None),
            (norm_three, WHOLE),
            (scale[2], WHOLE),
            masked,
            (closing, WHOLE),
        ],
        [(fine, None), (fine_low, None), (stats_fine, None)],
        [fine_spread(1), fine_stack(1), vmem(3, 4 * FINE, FINE)],
    )
    norm_four, below_four, above_four = all_reduce_stats(
        stats_four, True, planes * CELLS, [z_four], 5
    )

    decoded, partial_four = run(
        decoded_kernel,
        patches,
        [(z_four, None), (grad, None), (norm_four, WHOLE), (scale[3], WHOLE)],
        [(shape(patches, planes, GROUP, cells, dtype=BF16), None), (stats_fine, None)],
        [vmem(4 * CELLS, 4 * CELLS)],
    )
    (sums_four,) = all_reduce_stats(partial_four, False, planes * CELLS, [], 6)
    closing_flipped = flipped(closing.astype(BF16))
    closing_shape = shape(*closing.shape)
    back_three, partial_three, closing_grad = run(
        closing_back_kernel,
        patches,
        [
            (z_four, None),
            (below_four, None),
            (above_four, None),
            (grad, None),
            (grad_below, None),
            (grad_above, None),
            (norm_four, WHOLE),
            (sums_four, WHOLE),
            (scale[3], WHOLE),
            (out_three, None),
            (z_three, None),
            (norm_three, WHOLE),
            (scale[2], WHOLE),
            masked,
            (closing_flipped, WHOLE),
        ],
        [(fine, None), (stats_fine, None), (closing_shape, constant(closing_shape))],
        [
            fine_spread(1),
            fine_stack(1),
            vmem(3, 4 * FINE, FINE),
            vmem(FINE, planes * CELLS),
            vmem(3, FINE, 4 * FINE, dtype=F32),
            vmem(planes * CELLS, FINE, dtype=F32),
        ],
    )
    sums_three, back_below, back_above = all_reduce_stats(
        partial_three, False, planes * CELLS, [back_three], 7
    )
    merging_flipped = flipped(merging.astype(BF16))
    merging_shape = shape(*merging.shape)
    gate_shape = shape(3 * FINE + 8, span)
    skip_back, fine_back, merging_grad, gate_grad = run(
        merging_back_kernel,
        patches,
        [
            (back_three, None),
            (back_below, None),
            (back_above, None),
            (z_three, None),
            (below_three, None),
            (above_three, None),
            (norm_three, WHOLE),
            (sums_three, WHOLE),
            (scale[2], WHOLE),
            (skip, None),
            (attended, None),
            (upsampled, None),
            (query, None),
            (gates, WHOLE),
            (gate_rows, WHOLE),
            masked,
            (merging_flipped, WHOLE),
        ],
        [
            (fine, None),
            (shape(patches, planes, CELLS, 2 * GROUP), None),
            (merging_shape, constant(merging_shape)),
            (gate_shape, constant(gate_shape)),
        ],
        [
            fine_spread(1),
            fine_stack(1),
            vmem(3, 4 * FINE, 3 * FINE),
            vmem(4 * FINE, planes * CELLS),
            vmem(3, 3 * FINE, 4 * FINE, dtype=F32),
            vmem(planes * CELLS, 3 * FINE, dtype=F32),
        ],
    )
    fine_below, fine_above = exchange_rims([fine_back], 8)
    back_two, partial_two = run(
        coarse_grad_kernel,
        patches,
        [
            (fine_back, None),
            (fine_below, None),
            (fine_above, None),
            (z_two, None),
            (norm_two, WHOLE),
            (scale[1], WHOLE),
        ],
        [(coarse, None), (stats_coarse, None)],
        [],
    )
    sums_two, back_below, back_above = all_reduce_stats(
        partial_two, False, depth * CELLS, [back_two], 9
    )
    bottom_flipped = flipped(bottom.astype(BF16))
    bottom_shape = shape(*bottom.shape)
    back_one, partial_one, bottom_grad = run(
        bottom_back_kernel,
        patches,
        [
            (back_two, None),
            (back_below, None),
            (back_above, None),
            (z_two, None),
            (below_two, None),
            (above_two, None),
            (norm_two, WHOLE),
            (sums_two, WHOLE),
            (scale[1], WHOLE),
            (out_one, None),
            (z_one, None),
            (norm_one, WHOLE),
            (scale[0], WHOLE),
            masked,
            (bottom_flipped, WHOLE),
        ],
        [(coarse, None), (stats_coarse, None), (bottom_shape, constant(bottom_shape))],
        [
            coarse_spread(2),
            coarse_stacked(2),
            vmem(3, 6 * FINE, 2 * GROUP),
            vmem(3, 2 * GROUP, 6 * FINE, dtype=F32),
        ],
    )
    sums_one, back_below, back_above = all_reduce_stats(
        partial_one, False, depth * CELLS, [back_one], 10
    )
    widening_flipped = flipped(widening.astype(BF16))
    widening_shape = shape(*widening.shape)
    skip_grad, widening_grad = run(
        widening_back_kernel,
        patches,
        [
            (back_one, None),
            (back_below, None),
            (back_above, None),
            (z_one, None),
            (below_one, None),
            (above_one, None),
            (norm_one, WHOLE),
            (sums_one, WHOLE),
            (scale[0], WHOLE),
            (pooled, None),
            (skip_back, None),
            masked,
            (widening_flipped, WHOLE),
        ],
        [
            (shape(patches, planes, GROUP, cells), None),
            (widening_shape, constant(widening_shape)),
        ],
        [
            coarse_spread(2),
            coarse_stacked(2),
            vmem(3, 6 * FINE, GROUP),
            vmem(3, GROUP, 6 * FINE, dtype=F32),
            vmem(4 * CELLS, 4 * CELLS),
        ],
    )

    blocks = gate_grad[: 3 * FINE].reshape(3, 4, GROUP, 4, inner)
    gate_rows_grad = sum(blocks[:, index, :, index] for index in range(4))
    tail = gate_grad[3 * FINE : 3 * FINE + 2].reshape(2, 4, inner).sum(axis=1)
    gating_grad = jnp.concatenate([gate_rows_grad.reshape(3 * GROUP, inner), tail], axis=0)
    merging_grad, closing_grad, gating_grad, widening_grad, bottom_grad = lax.psum(
        (merging_grad, closing_grad, gating_grad, widening_grad, bottom_grad), ("patch", "depth")
    )
    gain_grad = [sums_one[3], sums_two[3], sums_three[3, :decoder], sums_four[3, :decoder]]
    shift_grad = [sums_one[2], sums_two[2], sums_three[2, :decoder], sums_four[2, :decoder]]
    scales_grad = jnp.stack([jnp.concatenate(gain_grad), jnp.concatenate(shift_grad)])
    states = [
        update_state(*state)
        for state in (
            (widening, widening_grad, widening_velocity, widening_average, weight_decay, learning_rate),
            (bottom, bottom_grad, bottom_velocity, bottom_average, weight_decay, learning_rate),
            (merging, merging_grad, merging_velocity, merging_average, weight_decay, learning_rate),
            (closing, closing_grad, closing_velocity, closing_average, weight_decay, learning_rate),
            (gating, gating_grad, gating_velocity, gating_average, weight_decay, learning_rate),
            (scales, scales_grad, scales_velocity, scales_average, 0.0, scale_rate),
        )
    ]
    outputs = (
        jnp.transpose(decoded, (0, 2, 1, 3)),
        jnp.transpose(skip_grad, (0, 2, 1, 3)),
    ) + tuple(state[index] for index in range(4) for state in states)
    return outputs


def solution(mesh):
    by_device = P("patch", None, "depth", None)
    return jax.shard_map(
        local,
        mesh=mesh,
        in_specs=(by_device, P("patch", "depth", None), by_device) + (P(),) * 18,
        out_specs=(by_device, by_device) + (P(),) * 24,
        check_vma=False,
    )
```

time: 1610 us -> 589 us (0.37)
  other arithmetic: 479 us -> 28.6 us
  blocking collectives: 485 us -> 39.2 us
  Pallas kernels: 0 us -> 332 us
  matrix products: 325 us -> 0 us
  local copies, waits for them, and re-layouts: 143 us -> 59.3 us
  starting transfers between devices: 39.6 us -> 4.34 us
    psum x12 -> x1, blocking collectives: 485 us -> 39.2 us  [local(): lax.psum((merging_grad, closing_grad, gating_grad, widening_grad, bottom_...]
    pallas_call x0 -> x21, Pallas kernels: none -> 332 us  [the longest x11 241 us: run(): pl.pallas_call(kernel, grid=(patches,), out_shape=[array for array, _ in...]
    dot_general x42 -> x0, matrix products: 325 us -> none  [the longest x24 193 us: convolve(): jnp.einsum('pkdv,ko->podv', stacked, weights, preferred_element_type=jnp....]
    unnamed x116 -> x0, other arithmetic: 307 us -> none
    concatenate x24 -> x4, other arithmetic: 73.7 us -> 0.25 us  [the longest x1 0.08 us: local(): jnp.concatenate(shift_grad)]
    ppermute x22 -> x2, starting transfers between devices: 39.5 us -> 4.31 us  [the longest x1 3.03 us: padded_ids(): before = lax.ppermute(coarse[:, depth - 1:], 'depth', up)]
    slice x42 -> x10, local copies, waits for them, and re-layouts: 38.9 us -> 5.43 us  [the longest x2 2.65 us: local(): scale.append(jnp.tile(scales[:, begin:begin + size], (1, repeat)))]
    reduce_sum x9 -> x1, other arithmetic: 28.8 us -> 0.02 us  [local(): tail = gate_grad[3 * FINE:3 * FINE + 2].reshape(2, 4, inner).sum(axis=1)]
  transfers between devices with their start and end apart: 23 -> 3, of which waited for: 4 -> 1; matrix products, arithmetic and copies ran while one was open for 11% -> 8% of each run, Pallas kernels for 0% -> 0%
where the time goes in v1:
time: 589 us; the launch traced here: 580 us
  Pallas kernels  332 us (56%)
  waiting for transfers between devices  102 us (17%)
  local copies, waits for them, and re-layouts  59.3 us (10%)
  blocking collectives  39.2 us (7%)
  other arithmetic  28.6 us (5%)
  between operations  14.9 us (3%)
    pallas_call x11, Pallas kernels, run(): pl.pallas_call(kernel, grid=(patches,), out_shape=[array for array, _ in...  241 us
    psum x1, waiting for transfers between devices, local(): lax.psum((merging_grad, closing_grad, gating_grad, widening_grad, bottom_...  102 us
    pallas_call x8, Pallas kernels, all_reduce_stats(): pl.pallas_call(functools.partial(reduce_kernel, npat, ndep, low, moments,...  84.2 us
    psum x1, blocking collectives, local(): lax.psum((merging_grad, closing_grad, gating_grad, widening_grad, bottom_...  39.2 us
    unnamed x83, local copies, waits for them, and re-layouts  31 us
    convert_element_type x6, other arithmetic, update_state(): return (weight_next, momentum, smoothed, weight_next.astype(jnp.bfloat16))  15.9 us
  transfers between devices with their start and end apart: 3, of which 1 were waited for; matrix products, arithmetic and copies ran while one was open for 8% of the time, Pallas kernels for 0%

profile of v1, /device:TPU:0, one launch (start us, length us, event | category | flops | bytes accessed | tf_op | source)
XLA Modules:
  0.0 580.4 jit_solution(15226816668644070946)
XLA Ops:
  9.9 1.3 collective-permute-start.1
  11.2 3.0 collective-permute-start
  14.3 1.3 fusion.11
  15.5 1.4 fusion.10
  16.9 1.5 reshape.90
  19.4 1.7 convert_element_type.47
  25.8 5.9 %copy_bitcast_fusion = (bf16[4,4,64,1024]{3,2,1,0:T(8,128)(2,1)}, bf16[4,4,64,1024]{3,2,1,0:T(8,128)(2,1)}) fusion(bf16[4,64,4,1024]{3,2,1,0:T(4,128)(2,1)} %param.23, bf16[4,64,4,1024]{3,2,1,0:T(4,128)(2,1)} %param.21), kind=kLoop, calls=%fused_computation.4 | loop fusion | bytes 8388608 | tf_op jit(solution)/shard_map/transpose | solution.py:1246
  34.1 2.2 copy.117.kernel
  36.4 1.3 convert_element_type.45
  42.6 2.3 copy.124
  44.9 2.3 copy.128
  47.2 1.6 broadcast_in_dim.2.ids
  48.8 15.3 %shard_map.404 = (bf16[4,4,256,256]{3,2,1,0:T(8,128)(2,1)}, bf16[4,4,256,256]{3,2,1,0:T(8,128)(2,1)}, bf16[4,2,256,128]{3,2,1,0:T(8,128)(2,1)}, bf16[9,4,512,256]{3,2,1,0:T(8,128)(2,1)}) custom-call(bf16[4,4,64,1024]{3,2,1,0:T(8,128)(2,1)} %get-tuple-element.291.skip, bf16[4,4,64,1024]{3,2,1,0:T(8,128)(2,1)} %get-tuple-element.290.grad, ...), custom_call_target="tpu_custom_call" | custom-call | tf_op jit(solution)/shard_map/pallas_call | solution.py:1166
  64.1 3.7 shard_map.405
  67.8 7.7 %shard_map.406 = (f32[4,2,256,128]{3,2,1,0:T(8,128)}, f32[4,8,128]{2,1,0:T(8,128)}) custom-call(bf16[4,2,256,128]{3,2,1,0:T(8,128)(2,1)} %get-tuple-element.88.refs_2_.pooled, bf16[4,256,128]{2,1,0:T(8,128)(2,1)} %get-tuple-element.91.below, bf16[4,256,128]{2,1,0:T(8,128)(2,1)} %get-tuple-element.92.above, bf16[9,4,512,256]{3,2,1,0:T(8,128)(2,1)} %get-tuple-element.93.masks, ...), custom_call_target="tpu_custom_call" | custom-call | tf_op jit(solution)/shard_map/pallas_call | solution.py:1166
  75.5 12.8 %shard_map.407 = (f32[8,128]{1,0:T(8,128)}, f32[4,256,128]{2,1,0:T(8,128)}, f32[4,256,128]{2,1,0:T(8,128)}) custom-call(f32[4,8,128]{2,1,0:T(8,128)} %get-tuple-element.95.refs_0_, f32[4,2,256,128]{3,2,1,0:T(8,128)} %get-tuple-element.94.refs_1_.z.z_before), custom_call_target="tpu_custom_call" | custom-call | tf_op jit(solution)/shard_map/pallas_call | solution.py:235
  88.3 10.6 %shard_map.408 = (f32[4,2,256,128]{3,2,1,0:T(8,128)}, bf16[4,2,256,128]{3,2,1,0:T(8,128)(2,1)}, f32[4,8,128]{2,1,0:T(8,128)}) custom-call(f32[4,2,256,128]{3,2,1,0:T(8,128)} %get-tuple-element.94.refs_1_.z.z_before, f32[4,256,128]{2,1,0:T(8,128)} %get-tuple-element.96.below, f32[4,256,128]{2,1,0:T(8,128)} %get-tuple-element.97.above, ...), custom_call_target="tpu_custom_call" | custom-call | tf_op jit(solution)/shard_map/pallas_call | solution.py:1166
  98.9 10.9 %shard_map.409 = (f32[8,128]{1,0:T(8,128)}, f32[4,256,128]{2,1,0:T(8,128)}, f32[4,256,128]{2,1,0:T(8,128)}) custom-call(f32[4,8,128]{2,1,0:T(8,128)} %get-tuple-element.100.refs_0_, f32[4,2,256,128]{3,2,1,0:T(8,128)} %get-tuple-element.99.refs_1_.z), custom_call_target="tpu_custom_call" | custom-call | tf_op jit(solution)/shard_map/pallas_call | solution.py:235
  109.8 43.5 %shard_map.410 = (f32[4,4,256,256]{3,2,1,0:T(8,128)}, bf16[4,4,256,256]{3,2,1,0:T(8,128)(2,1)}, bf16[4,4,256,512]{3,2,1,0:T(8,128)(2,1)}, f32[4,4,256,128]{3,2,1,0:T(8,128)}, f32[4,8,256]{2,1,0:T(8,128)}) custom-call(f32[4,2,256,128]{3,2,1,0:T(8,128)} %get-tuple-element.99.refs_1_.z, f32[4,256,128]{2,1,0:T(8,128)} %get-tuple-element.101.below, ...), custom_call_target="tpu_custom_call" | custom-call | tf_op jit(solution)/shard_map/pallas_call | solution.py:1166
  153.3 9.3 %shard_map.411 = (f32[8,256]{1,0:T(8,128)}, f32[4,256,256]{2,1,0:T(8,128)}, f32[4,256,256]{2,1,0:T(8,128)}) custom-call(f32[4,8,256]{2,1,0:T(8,128)} %get-tuple-element.107.refs_0_, f32[4,4,256,256]{3,2,1,0:T(8,128)} %get-tuple-element.106.refs_1_.z.z_before), custom_call_target="tpu_custom_call" | custom-call | tf_op jit(solution)/shard_map/pallas_call | solution.py:235
  162.6 14.7 %shard_map.412 = (f32[4,4,256,256]{3,2,1,0:T(8,128)}, bf16[4,4,256,256]{3,2,1,0:T(8,128)(2,1)}, f32[4,8,256]{2,1,0:T(8,128)}) custom-call(f32[4,4,256,256]{3,2,1,0:T(8,128)} %get-tuple-element.106.refs_1_.z.z_before, f32[4,256,256]{2,1,0:T(8,128)} %get-tuple-element.108.below, f32[4,256,256]{2,1,0:T(8,128)} %get-tuple-element.109.above, ...), custom_call_target="tpu_custom_call" | custom-call | tf_op jit(solution)/shard_map/pallas_call | solution.py:1166
  177.3 11.0 %shard_map.413 = (f32[8,256]{1,0:T(8,128)}, f32[4,256,256]{2,1,0:T(8,128)}, f32[4,256,256]{2,1,0:T(8,128)}) custom-call(f32[4,8,256]{2,1,0:T(8,128)} %get-tuple-element.112.refs_0_, f32[4,4,256,256]{3,2,1,0:T(8,128)} %get-tuple-element.111.refs_1_.z), custom_call_target="tpu_custom_call" | custom-call | tf_op jit(solution)/shard_map/pallas_call | solution.py:235
  188.3 8.3 %shard_map.414 = (bf16[4,4,64,1024]{3,2,1,0:T(8,128)(2,1)}, f32[4,8,256]{2,1,0:T(8,128)}) custom-call(f32[4,4,256,256]{3,2,1,0:T(8,128)} %get-tuple-element.111.refs_1_.z, bf16[4,4,256,256]{3,2,1,0:T(8,128)(2,1)} %get-tuple-element.90.refs_1_.grad, f32[8,256]{1,0:T(8,128)} %get-tuple-element.113.stats_in, f32[2,256]{1,0:T(2,128)} %tile.32.scale), custom_call_target="tpu_custom_call" | custom-call | tf_op jit(solution)/shard_map/pallas_call | solution.py:1166
  196.6 9.3 %shard_map.415.sums_in = f32[8,256]{1,0:T(8,128)} custom-call(f32[4,8,256]{2,1,0:T(8,128)} %get-tuple-element.119.refs_0_), custom_call_target="tpu_custom_call" | custom-call | tf_op jit(solution)/shard_map/pallas_call | solution.py:235
  205.8 25.4 %shard_map.416 = (f32[4,4,256,256]{3,2,1,0:T(8,128)}, f32[4,8,256]{2,1,0:T(8,128)}, f32[27,64,64]{2,1,0:T(8,128)}) custom-call(f32[4,4,256,256]{3,2,1,0:T(8,128)} %get-tuple-element.111.refs_1_.z, f32[4,256,256]{2,1,0:T(8,128)} %get-tuple-element.115.below, f32[4,256,256]{2,1,0:T(8,128)} %get-tuple-element.116.above, ...), custom_call_target="tpu_custom_call" | custom-call | tf_op jit(solution)/shard_map/pallas_call | solution.py:1166
  231.2 10.9 %shard_map.417 = (f32[8,256]{1,0:T(8,128)}, f32[4,256,256]{2,1,0:T(8,128)}, f32[4,256,256]{2,1,0:T(8,128)}) custom-call(f32[4,8,256]{2,1,0:T(8,128)} %get-tuple-element.122.refs_0_, f32[4,4,256,256]{3,2,1,0:T(8,128)} %get-tuple-element.121.refs_1_.grad), custom_call_target="tpu_custom_call" | custom-call | tf_op jit(solution)/shard_map/pallas_call | solution.py:235
  242.1 66.6 %shard_map.418 = (f32[4,4,256,256]{3,2,1,0:T(8,128)}, f32[4,4,256,128]{3,2,1,0:T(8,128)}, f32[27,192,64]{2,1,0:T(8,128)}, f32[776,128]{1,0:T(8,128)}) custom-call(f32[4,4,256,256]{3,2,1,0:T(8,128)} %get-tuple-element.121.refs_1_.grad, f32[4,256,256]{2,1,0:T(8,128)} %get-tuple-element.123.grad_below, f32[4,256,256]{2,1,0:T(8,128)} %get-tuple-element.124.grad_above, ...), custom_call_target="tpu_custom_call" | custom-call | tf_op jit(solution)/shard_map/pallas_call | solution.py:1166
  308.8 2.3 shard_map.419
  311.7 4.3 shard_map.420
  315.9 9.2 %shard_map.421 = (f32[8,128]{1,0:T(8,128)}, f32[4,256,128]{2,1,0:T(8,128)}, f32[4,256,128]{2,1,0:T(8,128)}) custom-call(f32[4,8,128]{2,1,0:T(8,128)} %get-tuple-element.133.refs_0_, f32[4,2,256,128]{3,2,1,0:T(8,128)} %get-tuple-element.132.refs_1_.grad), custom_call_target="tpu_custom_call" | custom-call | tf_op jit(solution)/shard_map/pallas_call | solution.py:235
  325.1 15.1 %shard_map.422 = (f32[4,2,256,128]{3,2,1,0:T(8,128)}, f32[4,8,128]{2,1,0:T(8,128)}, f32[27,128,128]{2,1,0:T(8,128)}) custom-call(f32[4,2,256,128]{3,2,1,0:T(8,128)} %get-tuple-element.132.refs_1_.grad, f32[4,256,128]{2,1,0:T(8,128)} %get-tuple-element.134.grad_below, f32[4,256,128]{2,1,0:T(8,128)} %get-tuple-element.135.grad_above, ...), custom_call_target="tpu_custom_call" | custom-call | tf_op jit(solution)/shard_map/pallas_call | solution.py:1166
  340.2 10.8 %shard_map.423 = (f32[8,128]{1,0:T(8,128)}, f32[4,256,128]{2,1,0:T(8,128)}, f32[4,256,128]{2,1,0:T(8,128)}) custom-call(f32[4,8,128]{2,1,0:T(8,128)} %get-tuple-element.139.refs_0_, f32[4,2,256,128]{3,2,1,0:T(8,128)} %get-tuple-element.138.refs_1_.grad), custom_call_target="tpu_custom_call" | custom-call | tf_op jit(solution)/shard_map/pallas_call | solution.py:235
  351.1 29.9 %shard_map.424 = (f32[4,4,64,1024]{3,2,1,0:T(8,128)}, f32[27,64,128]{2,1,0:T(8,128)}) custom-call(f32[4,2,256,128]{3,2,1,0:T(8,128)} %get-tuple-element.138.refs_1_.grad, f32[4,256,128]{2,1,0:T(8,128)} %get-tuple-element.140.grad_below, f32[4,256,128]{2,1,0:T(8,128)} %get-tuple-element.141.grad_above, ...), custom_call_target="tpu_custom_call" | custom-call | tf_op jit(solution)/shard_map/pallas_call | solution.py:1166
  381.4 1.3 copy-done.14
  382.6 2.9 copy.129
  385.6 4.7 copy.130
  393.9 39.2 %psum.39 = f32[194,32]{0,1:T(8,128)S(1)} all-reduce(f32[194,32]{0,1:T(8,128)S(1)} %pad_maximum_fusion), channel_id=1, replica_groups=mesh['patch'=16,'depth'=2] {'patch','depth'}, use_global_device_ids=true, to_apply=%region_5.0 | all-reduce | flops 6208 | bytes 49664 | tf_op jit(solution)/shard_map/psum | solution.py:1522
  435.6 102.5 %all-reduce.3.cloned.1.call-done = (f32[27,64,128]{2,1,0:T(8,128)}, f32[27,128,128]{2,1,0:T(8,128)}, f32[27,192,64]{2,1,0:T(8,128)}, f32[27,64,64]{2,1,0:T(8,128)}) async-done(((f32[27,64,128]{2,1,0:T(8,128)}, f32[27,128,128]{2,1,0:T(8,128)}, f32[27,192,64]{2,1,0:T(8,128)}, f32[27,64,64]{2,1,0:T(8,128)}), (f32[27,64,128]{2,1,0:T(8,128)}, f32[27,128,128]{2,1,0:T(8,128)}, f32[27,192,64]{2,1,0:T(8,128)}, ...) | async-done | bytes 4423696 | tf_op jit(solution)/shard_map/psum | solution.py:1522
  538.1 6.6 %fusion.6 = (bf16[27,192,64]{2,1,0:T(8,128)(2,1)}, f32[27,192,64]{2,1,0:T(8,128)}, f32[27,192,64]{2,1,0:T(8,128)}) fusion(f32[27,192,64]{2,1,0:T(8,128)S(1)} %copy-done, f32[27,192,64]{2,1,0:T(8,128)} %copy.124, f32[27,192,64]{2,1,0:T(8,128)} %get-tuple-element.256), kind=kLoop, calls=%fused_computation.53 | loop fusion | flops 2985984 | bytes 7299072 | tf_op jit(solution)/shard_map/convert_element_type | solution.py:1142
  544.6 3.3 copy.131
  548.0 3.4 copy.132
  551.4 3.7 multiply_add_fusion
  555.1 3.4 copy.133
  558.5 1.7 copy.134
  560.2 2.7 fusion.8
  563.0 4.0 fusion.7
  567.0 1.4 fusion.5
  570.5 1.5 multiply_add_fusion.3
  (125 shorter events, 25.9 us)
Async XLA Ops:
  7.2 11.2 %copy-start.6 = (f32[27,64,64]{2,1,0:T(8,128)S(1)}, f32[27,64,64]{2,1,0:T(8,128)}, u32[]{:S(2)}) copy-start(f32[27,64,64]{2,1,0:T(8,128)} %kernel.6) | copy-start | bytes 1327108
  7.2 530.9 %all-reduce.3.cloned.1.call-start = ((), (), s32[]{:S(2)}) async-start(), calls=%async_computation | async-start | bytes 12386304 | tf_op jit(solution)/shard_map/psum | solution.py:1522
  9.9 37.3 %collective-permute-start.1 = (bf16[4,1,256]{2,1,0:T(2,128)(2,1)}, bf16[4,1,256]{2,1,0:T(2,128)(2,1)S(1)}, u32[]{:S(2)}, u32[]{:S(2)}) collective-permute-start(bf16[4,1,256]{2,1,0:T(2,128)(2,1)} %get-tuple-element.285), channel_id=1, source_target_pairs={{1,0},{3,2},{5,4},{7,6},{9,8},{11,10},{13,12},{15,14},{17,16},{19,... | collective-permute-start | bytes 6152 | tf_op jit(solution)/shard_map/ppermute | solution.py:1194
  11.2 36.0 %collective-permute-start = (bf16[4,1,256]{2,1,0:T(2,128)(2,1)}, bf16[4,1,256]{2,1,0:T(2,128)(2,1)S(1)}, u32[]{:S(2)}, u32[]{:S(2)}) collective-permute-start(bf16[4,1,256]{2,1,0:T(2,128)(2,1)} %get-tuple-element.284), channel_id=1, source_target_pairs={{0,1},{2,3},{4,5},{6,7},{8,9},{10,11},{12,13},{14,15},{16,17},{18,... | collective-permute-start | bytes 6152 | tf_op jit(solution)/shard_map/ppermute | solution.py:1193
  19.4 2.7 copy-start.2
  22.1 2.2 copy-start.4
  25.8 5.9 %copy-start.26 = (f32[3,64,32]{1,0,2:T(4,128)S(1)}, f32[3,64,32]{1,0,2:T(4,128)}, u32[]{:S(2)}) copy-start(f32[3,64,32]{1,0,2:T(4,128)} %reshape.90) | copy-start | bytes 73732
  25.8 6.9 %copy-start.18 = (bf16[27,64,64]{1,2,0:T(8,128)(2,1)S(1)}, bf16[27,64,64]{1,2,0:T(8,128)(2,1)}, u32[]{:S(2)}) copy-start(bf16[27,64,64]{1,2,0:T(8,128)(2,1)} %copy.118) | copy-start | bytes 663556
  25.8 7.6 %copy-start.27 = (f32[194,32]{0,1:T(8,128)S(1)}, f32[194,32]{0,1:T(8,128)}, u32[]{:S(2)}) copy-start(f32[194,32]{0,1:T(8,128)} %param.36) | copy-start | bytes 74500
  25.8 8.3 %copy-start.8 = (f32[27,192,64]{1,2,0:T(8,128)S(1)}, f32[27,192,64]{1,2,0:T(8,128)}, u32[]{:S(2)}) copy-start(f32[27,192,64]{1,2,0:T(8,128)} %param.30) | copy-start | bytes 3981316
  34.1 8.5 %copy-start.15 = (f32[27,192,64]{1,2,0:T(8,128)S(1)}, f32[27,192,64]{1,2,0:T(8,128)}, u32[]{:S(2)}) copy-start(f32[27,192,64]{1,2,0:T(8,128)} %param.31) | copy-start | bytes 3981316
  42.6 2.3 copy-start.16
  308.8 2.3 copy-start.25
  381.0 1.6 copy-start.14
  382.6 2.9 copy-start.11
  385.6 47.6 %copy-start.32 = (f32[2,384]{1,0:T(2,128)S(1)}, f32[2,384]{1,0:T(2,128)}, u32[]{:S(2)}) copy-start(f32[2,384]{1,0:T(2,128)} %param.39) | copy-start | bytes 9220
  385.6 47.6 %copy-start.35 = (f32[2,384]{1,0:T(2,128)S(1)}, f32[2,384]{1,0:T(2,128)}, u32[]{:S(2)}) copy-start(f32[2,384]{1,0:T(2,128)} %param.40) | copy-start | bytes 9220
  385.6 48.2 %copy-start.34 = (f32[2,384]{1,0:T(2,128)S(1)}, f32[2,384]{1,0:T(2,128)}, u32[]{:S(2)}) copy-start(f32[2,384]{1,0:T(2,128)} %param.41) | copy-start | bytes 9220
  385.6 48.8 %copy-start.28 = (f32[194,32]{0,1:T(8,128)S(1)}, f32[194,32]{0,1:T(8,128)}, u32[]{:S(2)}) copy-start(f32[194,32]{0,1:T(8,128)} %param.36) | copy-start | bytes 74500
  385.6 48.8 %copy-start.31 = (f32[194,32]{0,1:T(8,128)S(1)}, f32[194,32]{0,1:T(8,128)}, u32[]{:S(2)}) copy-start(f32[194,32]{0,1:T(8,128)} %param.37) | copy-start | bytes 74500
  385.6 49.4 %copy-start.30 = (f32[194,32]{0,1:T(8,128)S(1)}, f32[194,32]{0,1:T(8,128)}, u32[]{:S(2)}) copy-start(f32[194,32]{0,1:T(8,128)} %param.38) | copy-start | bytes 74500
  385.6 152.5 %copy-start = (f32[27,192,64]{2,1,0:T(8,128)S(1)}, f32[27,192,64]{2,1,0:T(8,128)}, u32[]{:S(2)}) copy-start(f32[27,192,64]{2,1,0:T(8,128)} %copy.117.kernel) | copy-start | bytes 3981316
  433.7 110.9 %copy-start.33 = (f32[2,384]{1,0:T(2,128)}, f32[2,384]{1,0:T(2,128)S(1)}, u32[]{:S(2)}) copy-start(f32[2,384]{1,0:T(2,128)S(1)} %get-tuple-element.259) | copy-start | bytes 9220
  435.0 109.7 %copy-start.29 = (f32[194,32]{0,1:T(8,128)}, f32[194,32]{0,1:T(8,128)S(1)}, u32[]{:S(2)}) copy-start(f32[194,32]{0,1:T(8,128)S(1)} %get-tuple-element.262) | copy-start | bytes 74500
  548.0 3.5 copy-start.1
  555.1 3.4 copy-start.10
  558.5 1.7 copy-start.5
  558.5 1.7 copy-start.20
  560.2 2.7 copy-start.3
  560.2 2.7 copy-start.17
  562.9 5.5 copy-start.12
  562.9 4.0 copy-start.7
  562.9 4.0 copy-start.21
  562.9 4.0 copy-start.22
  566.9 2.9 copy-start.9
  567.0 1.9 copy-start.23
  568.4 3.7 copy-start.13
  568.4 2.2 copy-start.19
  570.5 1.5 copy-start.24
Sparse Core Ops, SparseCore 0:
  381.2 156.8 all-reduce.2

commit v2 on v1

--- a/solution.py
+++ b/solution.py
@@ -242,12 +242,149 @@
     )(stats, *arrays)
 
 
+def grads_plan(units, ndep, low, high):
+    colours = min(4, units)
+    orders = [(0, 1, 2), (0, 2, 1), (0, 1, 2), (0, 1, 2)][:colours]
+    counts = [units // colours + (1 if index < units % colours else 0) for index in range(colours)]
+    sizes = (ndep, low, high)
+    return counts, orders, sizes
+
+
+def grads_kernel(plan, unit, source, result, held, *refs):
+    counts, orders, sizes = plan
+    colours, stages = len(counts), len(sizes)
+    arrivals, sems = refs[: colours * stages], refs[colours * stages]
+    mp, md = lax.axis_index("patch"), lax.axis_index("depth")
+    ndep, low, high = sizes
+    mine_low, mine_high = lax.rem(mp, low), mp // low
+    places = (md, mine_low, mine_high)
+    devices = (
+        lambda step: (mp, lax.rem(md + step, ndep)),
+        lambda step: (mine_high * low + lax.rem(mine_low + step, low), md),
+        lambda step: (lax.rem(mine_high + step, high) * low + mine_low, md),
+    )
+    barrier = pltpu.get_barrier_semaphore()
+    for stage in range(stages):
+        for step in range(1, sizes[stage]):
+            pl.semaphore_signal(
+                barrier, inc=1, device_id=devices[stage](step), device_id_type=MESH
+            )
+    pl.semaphore_wait(barrier, sum(sizes) - stages)
+    begins = [sum(counts[:index]) * unit for index in range(colours)]
+    lengths = [count * unit for count in counts]
+    used = [0]
+
+    def copy(origin, target, device):
+        send, receive = sems.at[used[0]], sems.at[used[0] + 1]
+        used[0] += 2
+        return pltpu.make_async_remote_copy(
+            src_ref=origin,
+            dst_ref=target,
+            send_sem=send,
+            recv_sem=receive,
+            device_id=device,
+            device_id_type=MESH,
+        )
+
+    history = []
+    for round_ in range(stages):
+        started = []
+        origin = source if round_ == 0 else held
+        for colour in range(colours):
+            axis = orders[colour][round_]
+            size, piece = sizes[axis], lengths[colour] // sizes[axis]
+            arrival = arrivals[colour * stages + round_]
+            copies = []
+            for step in range(1, size):
+                begin = begins[colour] + lax.rem(places[axis] + step, size) * piece
+                begin = pl.multiple_of(begin, 16)
+                copies.append(
+                    copy(origin.at[pl.ds(begin, piece)], arrival.at[step - 1], devices[axis](step))
+                )
+                copies[-1].start()
+            started.append(copies)
+        history.append((list(begins), list(lengths)))
+        for colour in range(colours):
+            axis = orders[colour][round_]
+            size, piece = sizes[axis], lengths[colour] // sizes[axis]
+            arrival = arrivals[colour * stages + round_]
+            begin = pl.multiple_of(begins[colour] + places[axis] * piece, 16)
+            target = result if round_ == stages - 1 else held
+            for item in started[colour]:
+                item.wait_recv()
+            block = next(rows for rows in (128, 64, 48, 32, 16) if piece % rows == 0)
+
+            def add(index, carry):
+                row = pl.multiple_of(index * block, 16)
+                here = pl.ds(pl.multiple_of(begin + row, 16), block)
+                total = origin[here, :].astype(F32)
+                for other in range(size - 1):
+                    total = total + arrival[other, pl.ds(row, block), :].astype(F32)
+                target[here, :] = total.astype(BF16)
+                return carry
+
+            lax.fori_loop(0, piece // block, add, 0)
+            begins[colour], lengths[colour] = begin, piece
+        for copies in started:
+            for item in copies:
+                item.wait_send()
+    for round_ in reversed(range(stages)):
+        started = []
+        for colour in range(colours):
+            axis = orders[colour][round_]
+            rows = result.at[pl.ds(begins[colour], lengths[colour])]
+            for step in range(1, sizes[axis]):
+                started.append(copy(rows, rows, devices[axis](step)))
+                started[-1].start()
+        for item in started:
+            item.wait()
+        begins, lengths = history[round_]
+
+
+def all_reduce_grads(values, number):
+    npat, ndep = lax.axis_size("patch"), lax.axis_size("depth")
+    low = 4 if npat % 4 == 0 else 1
+    high = npat // low
+    unit = 16 * npat * ndep
+    rows = values.shape[0]
+    units = -(-rows // unit)
+    if units * unit > rows:
+        values = jnp.pad(values, ((0, units * unit - rows), (0, 0)))
+    plan = grads_plan(units, ndep, low, high)
+    counts, orders, sizes = plan
+    scratch = [pltpu.VMEM(values.shape, BF16)]
+    total = 0
+    for count, order in zip(counts, orders):
+        length = count * unit
+        for axis in order:
+            length //= sizes[axis]
+            scratch.append(pltpu.VMEM((max(sizes[axis] - 1, 1), length, 2 * GROUP), BF16))
+            total += 4 * (sizes[axis] - 1)
+    scratch.append(pltpu.SemaphoreType.DMA((total,)))
+    inside = pl.BlockSpec(memory_space=pltpu.VMEM)
+    return pl.pallas_call(
+        functools.partial(grads_kernel, plan, unit),
+        out_shape=jax.ShapeDtypeStruct(values.shape, BF16),
+        in_specs=[inside],
+        out_specs=inside,
+        scratch_shapes=scratch,
+        compiler_params=params(collective_id=number, has_side_effects=True),
+    )(values)
+
+
 def lane_is_low(shape):
     return (lax.broadcasted_iota(jnp.int32, shape, 1) & (2 * GROUP - 1)) < GROUP
 
 
 def row_column(shape):
     return lax.broadcasted_iota(jnp.int32, shape, 0) & (HALF_WIDTH - 1)
+
+
+def segment(scales, index):
+    if index < 2:
+        return scales[:, index * 2 * GROUP : (index + 1) * 2 * GROUP]
+    begin = 4 * GROUP + (index - 2) * GROUP
+    return jnp.concatenate([scales[:, begin : begin + GROUP]] * 4, axis=1)
 
 
 def normalize(values, stats):
@@ -270,6 +407,21 @@
 def norm_back(grad, normed, stats, sums, scale):
     factor = scale[0:1] * lax.rsqrt(stats[1:2] + epsilon)
     return (grad - sums[0:1] - normed * sums[1:2]) * factor
+
+
+def fill_gates(gates, gating):
+    gates[...] = jnp.zeros(gates.shape, BF16)
+    inner = gating.shape[1]
+    for group in range(3):
+        block = gating[group * GROUP : (group + 1) * GROUP, :].astype(BF16)
+        for phase in range(4):
+            row = group * FINE + phase * GROUP
+            gates[row : row + GROUP, phase * inner : (phase + 1) * inner] = block
+
+
+def gate_lines(gating):
+    lines = gating[3 * GROUP : 3 * GROUP + 2, :]
+    return jnp.concatenate([lines] * 4, axis=1)
 
 
 def edge_flags():
@@ -356,13 +508,24 @@
                     )
 
 
-def fine_weights(weights, kernel, groups_in, groups_out):
+def tap_block(kernel, tap, way):
+    if way in ("plain", "turned"):
+        block = kernel[tap]
+    else:
+        block = kernel[26 - tap]
+    block = block.astype(BF16)
+    if way in ("turned", "flipped"):
+        block = transposed(block, identity(block.shape[1]))
+    return block
+
+
+def fine_weights(weights, kernel, groups_in, groups_out, way):
     weights[...] = jnp.zeros(weights.shape, BF16)
 
     def fill(level, carry):
         for step in range(9):
             row_step, column_step = step // 3, step % 3
-            block = kernel[9 * level + step].astype(BF16)
+            block = tap_block(kernel, 9 * level + step, way)
             for phase in range(4):
                 row_slot, column_slot = phase // 2 + row_step, phase % 2 + column_step
                 for source in range(groups_in):
@@ -378,13 +541,13 @@
     lax.fori_loop(0, 3, fill, 0)
 
 
-def coarse_weights(weights, kernel, groups_in):
+def coarse_weights(weights, kernel, groups_in, way):
     weights[...] = jnp.zeros(weights.shape, BF16)
 
     def fill(level, carry):
         for step in range(9):
             row_step, column_slot = step // 3, (0, 1, 3)[step % 3]
-            block = kernel[9 * level + step].astype(BF16)
+            block = tap_block(kernel, 9 * level + step, way)
             for source in range(groups_in):
                 row = ((row_step * groups_in + source) * 4 + column_slot) * GROUP
                 weights[level, row : row + GROUP, :] = block[source * GROUP : (source + 1) * GROUP]
@@ -393,10 +556,11 @@
     lax.fori_loop(0, 3, fill, 0)
 
 
-def fine_kernel_grad(out, sums, groups):
+def fine_kernel_grad(out, sums, groups, turn):
     def fill(level, carry):
         for step in range(9):
             row_step, column_step = step // 3, step % 3
+            blocks = []
             for group in range(groups):
                 total = None
                 for phase in range(4):
@@ -404,7 +568,9 @@
                     slot = (phase // 2 + row_step) * 4 + phase % 2 + column_step
                     block = sums[level, row : row + GROUP, slot * GROUP : (slot + 1) * GROUP]
                     total = block if total is None else total + block
-                out[26 - (9 * level + step), group * GROUP : (group + 1) * GROUP, :] = total
+                total = total.astype(BF16)
+                blocks.append(transposed(total, identity(GROUP)) if turn else total)
+            out[26 - (9 * level + step)] = jnp.concatenate(blocks, axis=1)
         return carry
 
     lax.fori_loop(0, 3, fill, 0)
@@ -418,7 +584,7 @@
             for group in range(groups):
                 slot = (row_step * groups + group) * 4 + column_slot
                 blocks.append(sums[level, :, slot * GROUP : (slot + 1) * GROUP])
-            out[26 - (9 * level + step)] = jnp.concatenate(blocks, axis=1)
+            out[26 - (9 * level + step)] = jnp.concatenate(blocks, axis=1).astype(BF16)
         return carry
 
     lax.fori_loop(0, 3, fill, 0)
@@ -471,21 +637,29 @@
     return jnp.where(columns == row * WIDTH + column, 1.0, 0.0).astype(BF16)
 
 
-def prepare_kernel(skip, grad, ids, skip_out, grad_out, pooled, masks, order, spread):
-    planes = skip.shape[1]
+def plane_order(planes):
+    size = planes * GROUP
+    rows = lax.broadcasted_iota(jnp.int32, (size, size), 0)
+    columns = lax.broadcasted_iota(jnp.int32, (size, size), 1)
+    same = (columns % GROUP) * planes + columns // GROUP == rows
+    return jnp.where(same, 1.0, 0.0).astype(BF16)
+
+
+def prepare_kernel(skip, grad, ids, skip_out, grad_out, pooled, ids_out, order):
+    planes = skip.shape[2]
     depth = planes // 2
     size = 4 * CELLS
 
     @pl.when(pl.program_id(0) == 0)
     def _():
         order[...] = voxel_order(size, False)
-        spread[...] = jnp.zeros(spread.shape, F32)
-
+
+    contract = (((1,), (1,)), ((), ()))
+    by_plane = plane_order(planes)
     for source, target in ((skip, skip_out), (grad, grad_out)):
         lines = source[0].reshape(planes * GROUP, size)
-        turned = lax.dot_general(
-            order[...], lines, (((1,), (1,)), ((), ())), preferred_element_type=F32
-        )
+        turned = lax.dot_general(order[...], lines, contract, preferred_element_type=F32)
+        turned = jnp.dot(turned.astype(BF16), by_plane, preferred_element_type=F32)
         for plane in range(planes):
             pieces = [
                 turned[phase * CELLS : (phase + 1) * CELLS, plane * GROUP : (plane + 1) * GROUP]
@@ -497,12 +671,26 @@
         total = total[:, : 2 * GROUP] + total[:, 2 * GROUP :]
         total = total + pltpu.roll(total, GROUP, 1)
         pooled[0, plane] = (total * 0.125).astype(BF16)
-    for plane in range(depth + 2):
-        spread[plane, 2 * RIM : 2 * RIM + CELLS] = ids[0, plane].astype(F32)
+    names = lax.dot_general(
+        order[:CELLS], ids[0].astype(F32).astype(BF16), contract, preferred_element_type=F32
+    )
+    for plane in range(depth):
+        column = names[:, 2 * plane : 2 * plane + 1]
+        ids_out[0, plane] = jnp.broadcast_to(column, (CELLS, 2 * GROUP)).astype(BF16)
+
+
+def fill_masks(masks, centers, rims, flags, spread):
+    depth = centers.shape[1]
+    for plane in range(depth):
+        spread[plane + 1, 2 * RIM : 2 * RIM + CELLS] = centers[0, plane].astype(F32)
+    for flag, rim, plane in ((flags[0], rims[0], 0), (flags[1], rims[1], depth + 1)):
+        values = rim[0].astype(F32)
+        values = at_edge(flag, values, jnp.zeros_like(values))
+        spread[plane, 2 * RIM : 2 * RIM + CELLS] = values
     column = row_column((CELLS, 2 * GROUP))
     low = lane_is_low((CELLS, 2 * GROUP))
     for plane in range(depth):
-        center = ids[0, plane + 1].astype(F32)
+        center = centers[0, plane].astype(F32)
         for level in range(3):
             for step in range(3):
                 begin = RIM + step * RIM
@@ -521,15 +709,19 @@
                 masks[3 * level + step, 0, plane * CELLS : (plane + 1) * CELLS] = both.astype(BF16)
 
 
-def first_kernel(pooled, below, above, masks, kernel, pre, stats, spread, stack, weights):
+def first_kernel(
+    pooled, below, above, ids, ids_below, ids_above, kernel, pre, stats, masks, spread, stack, weights, names
+):
     depth = pooled.shape[1]
 
     @pl.when(pl.program_id(0) == 0)
     def _():
         zero_rims(spread)
-        coarse_weights(weights, kernel, 1)
+        names[...] = jnp.zeros(names.shape, F32)
+        coarse_weights(weights, kernel, 1, "plain")
 
     first, last = edge_flags()
+    fill_masks(masks, ids, (ids_below, ids_above), (first, last), names)
     for plane in range(depth):
         spread_coarse(spread, plane + 1, 1, pooled[0, plane].astype(F32))
     for flag, rim, plane in ((first, below, 0), (last, above, depth + 1)):
@@ -543,15 +735,16 @@
 
 
 def second_kernel(
-    z, below, above, stats_in, scale, masks, kernel, pre, out, stats, spread, stack, weights
+    z, below, above, stats_in, scales, masks, kernel, pre, out, stats, spread, stack, weights
 ):
     depth = z.shape[1]
 
     @pl.when(pl.program_id(0) == 0)
     def _():
         zero_rims(spread)
-        coarse_weights(weights, kernel, 2)
-
+        coarse_weights(weights, kernel, 2, "plain")
+
+    scale = segment(scales, 0)
     first, last = edge_flags()
     for plane in range(depth):
         values = norm_silu(z[0, plane], stats_in, scale)
@@ -584,12 +777,11 @@
     below,
     above,
     stats_in,
-    scale,
+    scales,
     skip,
     skip_below,
     skip_above,
-    gates,
-    gate_rows,
+    gating,
     masks,
     kernel,
     pre,
@@ -601,6 +793,7 @@
     spread,
     stack,
     weights,
+    gates,
 ):
     depth = z.shape[1]
     planes = 2 * depth
@@ -609,8 +802,10 @@
     @pl.when(pl.program_id(0) == 0)
     def _():
         zero_rims(spread)
-        fine_weights(weights, kernel, 3, 1)
-
+        fine_weights(weights, kernel, 3, 1, "turned")
+        fill_gates(gates, gating)
+
+    scale = segment(scales, 1)
     first, last = edge_flags()
     for plane in range(depth):
         values = norm_silu(z[0, plane], stats_in, scale)
@@ -618,6 +813,7 @@
     for flag, rim, plane, inner in ((first, below, 0, 1), (last, above, depth + 1, depth)):
         values = norm_silu(rim[0], stats_in, scale).astype(BF16).astype(F32)
         coarse[plane] = at_edge(flag, values, coarse[inner])
+    gate_rows = gate_lines(gating)
     low = lane_is_low((CELLS, width))
     column = row_column((CELLS, width))
     span = gate_rows.shape[1]
@@ -671,7 +867,7 @@
 
 
 def fourth_kernel(
-    z, below, above, stats_in, scale, masks, kernel, pre, out, stats, spread, stack, weights
+    z, below, above, stats_in, scales, masks, kernel, pre, out, stats, spread, stack, weights
 ):
     planes = z.shape[1]
     depth = planes // 2
@@ -679,8 +875,9 @@
     @pl.when(pl.program_id(0) == 0)
     def _():
         zero_rims(spread)
-        fine_weights(weights, kernel, 1, 1)
-
+        fine_weights(weights, kernel, 1, 1, "plain")
+
+    scale = segment(scales, 2)
     first, last = edge_flags()
     for plane in range(planes):
         values = norm_silu(z[0, plane], stats_in, scale)
@@ -698,6 +895,7 @@
 
 
 def to_voxels(out, planes, order, parts):
+    count = len(planes)
     total = None
     for part in range(parts):
         blocks = []
@@ -705,22 +903,24 @@
             pieces = [values[:, phase * GROUP : (phase + 1) * GROUP] for values in planes]
             blocks.append(jnp.concatenate(pieces, axis=1).astype(BF16))
         stacked = jnp.concatenate(blocks, axis=0)
+        stacked = lax.dot_general(
+            stacked, plane_order(count), (((1,), (1,)), ((), ())), preferred_element_type=F32
+        ).astype(BF16)
         term = jnp.dot(order[...], stacked, preferred_element_type=F32)
         total = term if total is None else total + term
         if part + 1 < parts:
             planes = [values - values.astype(BF16).astype(F32) for values in planes]
-    lines = total.T
-    for plane in range(len(planes)):
-        out[0, plane] = lines[plane * GROUP : (plane + 1) * GROUP].astype(out.dtype)
-
-
-def decoded_kernel(z, grad, stats_in, scale, decoded, sums, order):
+    out[0] = total.T.reshape(GROUP, count, total.shape[0]).astype(out.dtype)
+
+
+def decoded_kernel(z, grad, stats_in, scales, decoded, sums, order):
     planes = z.shape[1]
 
     @pl.when(pl.program_id(0) == 0)
     def _():
         order[...] = voxel_order(4 * CELLS, True)
 
+    scale = segment(scales, 3)
     first, second, made = 0.0, 0.0, []
     for plane in range(planes):
         normed = normalize(z[0, plane], stats_in)
@@ -743,11 +943,10 @@
     grad_above,
     stats_in,
     sums_in,
-    scale,
+    scales,
     out,
     z_before,
     stats_before,
-    scale_before,
     masks,
     kernel,
     back,
@@ -767,9 +966,10 @@
     @pl.when(step == 0)
     def _():
         zero_rims(spread)
-        fine_weights(weights, kernel, 1, 1)
+        fine_weights(weights, kernel, 1, 1, "flipped")
         totals[...] = jnp.zeros(totals.shape, F32)
 
+    scale, scale_before = segment(scales, 3), segment(scales, 2)
     first, last = edge_flags()
 
     def rounded(values, cotangent):
@@ -810,7 +1010,7 @@
 
     @pl.when(step == pl.num_programs(0) - 1)
     def _():
-        fine_kernel_grad(kernel_grad, totals, 1)
+        fine_kernel_grad(kernel_grad, totals, 1, False)
 
 
 def narrowed(values, low, column):
@@ -828,6 +1028,28 @@
     return 0.75 * (even + odd) + 0.25 * (later + earlier)
 
 
+def gate_gradient(out, sums):
+    span = sums.shape[1]
+    inner = span // 4
+    lanes = lax.broadcasted_iota(jnp.int32, (GROUP, span), 1) // inner
+    pieces = []
+    for group in range(3):
+        total = None
+        for phase in range(4):
+            row = group * FINE + phase * GROUP
+            block = jnp.where(lanes == phase, sums[row : row + GROUP], 0.0)
+            total = block if total is None else total + block
+        pieces.append(total)
+    pieces.append(sums[3 * FINE : 3 * FINE + 8])
+    pieces.append(jnp.zeros((GROUP - 8, span), F32))
+    total = jnp.concatenate(pieces, axis=0)
+    total = total + pltpu.roll(total, 2 * inner, 1)
+    total = total + pltpu.roll(total, inner, 1)
+    turned = total.T[:inner]
+    out[0:inner] = turned[:, : 2 * GROUP].astype(BF16)
+    out[inner : 2 * inner] = turned[:, 2 * GROUP :].astype(BF16)
+
+
 def merging_back_kernel(
     grad,
     grad_below,
@@ -837,13 +1059,12 @@
     above,
     stats_in,
     sums_in,
-    scale,
+    scales,
     skip,
     attended,
     upsampled,
     query,
-    gates,
-    gate_rows,
+    gating,
     masks,
     kernel,
     skip_back,
@@ -856,6 +1077,8 @@
     turned,
     totals,
     given,
+    gates,
+    gate_sums,
 ):
     planes = z.shape[1]
     depth = planes // 2
@@ -864,10 +1087,12 @@
     @pl.when(step == 0)
     def _():
         zero_rims(spread)
-        fine_weights(weights, kernel, 1, 3)
+        fine_weights(weights, kernel, 1, 3, "back")
+        fill_gates(gates, gating)
         totals[...] = jnp.zeros(totals.shape, F32)
-        gate_grad[...] = jnp.zeros(gate_grad.shape, F32)
-
+        gate_sums[...] = jnp.zeros(gate_sums.shape, F32)
+
+    scale = segment(scales, 2)
     first, last = edge_flags()
 
     def rounded(values, upstream):
@@ -910,6 +1135,7 @@
             )
             total = term if total is None else total + term
         given[:, columns] = total
+    gate_rows = gate_lines(gating)
     span = gate_rows.shape[1]
     part = span // 4
 
@@ -939,10 +1165,10 @@
         query_back = (logit_back * gate_rows[1:2] * silu_slope(asked)).astype(BF16)
         psi = jnp.sum(logit_back * active, axis=0, keepdims=True)
         bias = jnp.sum(query_back.astype(F32), axis=0, keepdims=True)
-        gate_grad[:FINE] += dot(turned[3 * FINE :, lines], query_back)
-        gate_grad[FINE : 3 * FINE] += dot(turned[FINE : 3 * FINE, lines], query_back)
-        gate_grad[3 * FINE : 3 * FINE + 1] += bias
-        gate_grad[3 * FINE + 1 : 3 * FINE + 2] += psi
+        gate_sums[:FINE] += dot(turned[3 * FINE :, lines], query_back)
+        gate_sums[FINE : 3 * FINE] += dot(turned[FINE : 3 * FINE, lines], query_back)
+        gate_sums[3 * FINE : 3 * FINE + 1] += bias
+        gate_sums[3 * FINE + 1 : 3 * FINE + 2] += psi
         skip_back[0, fine] = attended_back * attention + lax.dot_general(
             query_back, gates[:FINE], contract, preferred_element_type=F32
         )
@@ -955,11 +1181,13 @@
 
     @pl.when(step == pl.num_programs(0) - 1)
     def _():
-        fine_kernel_grad(kernel_grad, totals, 3)
-
-
-def coarse_grad_kernel(fine_back, below, above, z, stats_in, scale, back, sums):
+        fine_kernel_grad(kernel_grad, totals, 3, True)
+        gate_gradient(gate_grad, gate_sums)
+
+
+def coarse_grad_kernel(fine_back, below, above, z, stats_in, scales, back, sums):
     depth = z.shape[1]
+    scale = segment(scales, 1)
     first, last = edge_flags()
     first_sum, second_sum = 0.0, 0.0
     for plane in range(depth):
@@ -1009,11 +1237,10 @@
     above,
     stats_in,
     sums_in,
-    scale,
+    scales,
     out,
     z_before,
     stats_before,
-    scale_before,
     masks,
     kernel,
     back,
@@ -1030,9 +1257,10 @@
     @pl.when(step == 0)
     def _():
         zero_rims(spread)
-        coarse_weights(weights, kernel, 2)
+        coarse_weights(weights, kernel, 2, "flipped")
         totals[...] = jnp.zeros(totals.shape, F32)
 
+    scale, scale_before = segment(scales, 1), segment(scales, 0)
     coarse_stack(
         grad,
         (grad_below, grad_above),
@@ -1078,7 +1306,7 @@
     above,
     stats_in,
     sums_in,
-    scale,
+    scales,
     pooled,
     skip_back,
     masks,
@@ -1097,10 +1325,11 @@
     @pl.when(step == 0)
     def _():
         zero_rims(spread)
-        coarse_weights(weights, kernel, 2)
+        coarse_weights(weights, kernel, 2, "flipped")
         totals[...] = jnp.zeros(totals.shape, F32)
         order[...] = voxel_order(4 * CELLS, True)
 
+    scale = segment(scales, 0)
     coarse_stack(
         grad,
         (grad_below, grad_above),
@@ -1142,6 +1371,67 @@
     return (weight_next, momentum, smoothed, weight_next.astype(jnp.bfloat16))
 
 
+def update_kernel(grads, one, two, three, four, *refs):
+    inputs, outs = refs[:18], refs[18:]
+    step = pl.program_id(0)
+    taps = inputs[0].shape[0]
+    width = 2 * GROUP
+
+    def rows(first, count):
+        begin = pl.multiple_of(first + step * taps * count, 16)
+        return grads[pl.ds(begin, taps * count), :].astype(F32).reshape(taps, count, width)
+
+    def store(index, grad, decay, rate):
+        weight, velocity, average = [ref[...] for ref in inputs[3 * index : 3 * index + 3]]
+        state = update_state(weight, grad, velocity, average, decay, rate)
+        for kind in range(4):
+            outs[6 * kind + index][...] = state[kind]
+
+    base = 27 * GROUP
+    store(0, rows(0, GROUP), weight_decay, learning_rate)
+    store(1, rows(base, 2 * GROUP), weight_decay, learning_rate)
+    both = rows(4 * base, GROUP)
+    merged = jnp.concatenate([rows(3 * base, GROUP), both[:, :, :GROUP]], axis=2)
+    store(2, merged, weight_decay, learning_rate)
+    store(3, both[:, :, GROUP:], weight_decay, learning_rate)
+
+    @pl.when(step == 0)
+    def _():
+        inner, count = inputs[12].shape
+        first = grads[5 * base : 5 * base + inner, :].astype(F32)
+        second = grads[5 * base + inner : 5 * base + 2 * inner, :].astype(F32)
+        gate = jnp.concatenate([first, second[:, : count - width]], axis=1)
+        store(4, gate, weight_decay, learning_rate)
+        lines = [one[...], two[...], three[:, :GROUP], four[:, :GROUP]]
+        lines = jnp.concatenate(lines, axis=1)
+        store(5, jnp.concatenate([lines[3:4], lines[2:3]], axis=0), 0.0, scale_rate)
+
+
+def update(grads, sums, states):
+    taps = states[0][0].shape[0]
+    steps = 9
+    flat = [array for state in states for array in state]
+
+    def spec(array):
+        if len(array.shape) == 3:
+            return pl.BlockSpec((taps // steps,) + array.shape[1:], lambda p: (p, 0, 0))
+        return pl.BlockSpec(array.shape, lambda p: (0, 0))
+
+    outs = []
+    for kind in range(4):
+        for state in states:
+            outs.append(jax.ShapeDtypeStruct(state[0].shape, BF16 if kind == 3 else F32))
+    results = pl.pallas_call(
+        update_kernel,
+        grid=(steps,),
+        out_shape=outs,
+        in_specs=[WHOLE] * 5 + [spec(array) for array in flat],
+        out_specs=[spec(array) for array in outs],
+        compiler_params=params(dimension_semantics=("arbitrary",)),
+    )(grads, *sums, *flat)
+    return [[results[6 * kind + index] for kind in range(4)] for index in range(len(states))]
+
+
 def by_patch(array):
     rest = array.shape[1:]
     zeros = (0,) * len(rest)
@@ -1177,22 +1467,6 @@
 def constant(array):
     zeros = (0,) * len(array.shape)
     return pl.BlockSpec(array.shape, lambda p: zeros)
-
-
-def flipped(kernel):
-    return jnp.transpose(kernel[::-1], (0, 2, 1))
-
-
-def padded_ids(volume_ids, depth):
-    patches = volume_ids.shape[0]
-    coarse = volume_ids.reshape(patches, depth, 2, HALF_HEIGHT, 2, HALF_WIDTH, 2)
-    coarse = coarse[:, :, 0, :, 0, :, 0].reshape(patches, depth, CELLS).astype(BF16)
-    peers = lax.axis_size("depth")
-    up = [(i, i + 1) for i in range(peers - 1)]
-    down = [(j, i) for i, j in up]
-    before = lax.ppermute(coarse[:, depth - 1 :], "depth", up)
-    after = lax.ppermute(coarse[:, :1], "depth", down)
-    return jnp.concatenate([before, coarse, after], axis=1)
 
 
 def vmem(*sizes, dtype=BF16):
@@ -1227,39 +1501,31 @@
     depth = planes // 2
     inner = gating.shape[1]
     span = 4 * inner
-    ids = padded_ids(volume_ids, depth)
-    ids = jnp.broadcast_to(ids[..., None], ids.shape + (2 * GROUP,))
-    gains, shifts = scales[0], scales[1]
-    encoder = bottom.shape[2]
     decoder = closing.shape[2]
-    scale = []
-    begin = 0
-    for size, repeat in ((encoder, 1), (encoder, 1), (decoder, 4), (decoder, 4)):
-        scale.append(jnp.tile(scales[:, begin : begin + size], (1, repeat)))
-        begin += size
-    eye = jnp.eye(4, dtype=F32)
-    projection = gating[: channels + encoder].reshape(3, GROUP, inner)
-    gates = jnp.einsum("gca,pq->gpcqa", projection, eye).reshape(3 * FINE, span).astype(BF16)
-    gate_rows = jnp.tile(gating[channels + encoder :], (1, 4))
-
-    skip_by_plane = jnp.transpose(skip_features, (0, 2, 1, 3))
-    grad_by_plane = jnp.transpose(output_grad, (0, 2, 1, 3))
+    merging_turned = jnp.swapaxes(merging, 1, 2)
+
     fine = shape(patches, planes, CELLS, FINE)
     fine_low = shape(patches, planes, CELLS, FINE, dtype=BF16)
     coarse = shape(patches, depth, CELLS, 2 * GROUP)
     coarse_low = shape(patches, depth, CELLS, 2 * GROUP, dtype=BF16)
     masks_shape = shape(9, patches, depth * CELLS, FINE, dtype=BF16)
-    skip, grad, pooled, masks = run(
+    skip, grad, pooled, ids = run(
         prepare_kernel,
         patches,
-        [(skip_by_plane, None), (grad_by_plane, None), (ids, None)],
-        [(fine_low, None), (fine_low, None), (coarse_low, None), (masks_shape, mask_spec(masks_shape))],
-        [vmem(4 * CELLS, 4 * CELLS), vmem(depth + 2, CELLS + 4 * RIM, 2 * GROUP, dtype=F32)],
-    )
-    skip_below, skip_above, grad_below, grad_above, pooled_below, pooled_above = exchange_rims(
-        [skip, grad, pooled], 1
-    )
-    masked = (masks, mask_spec(masks))
+        [(skip_features, None), (output_grad, None), (volume_ids, None)],
+        [(fine_low, None), (fine_low, None), (coarse_low, None), (coarse_low, None)],
+        [vmem(4 * CELLS, 4 * CELLS)],
+    )
+    (
+        skip_below,
+        skip_above,
+        grad_below,
+        grad_above,
+        pooled_below,
+        pooled_above,
+        ids_below,
+        ids_above,
+    ) = exchange_rims([skip, grad, pooled, ids], 1)
     stats_fine = shape(patches, 8, FINE)
     stats_coarse = shape(patches, 8, 2 * GROUP)
     fine_spread = lambda groups: vmem(planes + 2, PADDED, groups * 2 * FINE)
@@ -1267,13 +1533,27 @@
     coarse_spread = lambda groups: vmem(depth + 2, PADDED, groups * FINE)
     coarse_stacked = lambda groups: vmem(3 * depth * CELLS, groups * 3 * FINE)
 
-    z_one, stats_one = run(
+    z_one, stats_one, masks = run(
         first_kernel,
         patches,
-        [(pooled, None), (pooled_below, None), (pooled_above, None), masked, (widening, WHOLE)],
-        [(coarse, None), (stats_coarse, None)],
-        [coarse_spread(1), coarse_stacked(1), vmem(3, 3 * FINE, 2 * GROUP)],
-    )
+        [
+            (pooled, None),
+            (pooled_below, None),
+            (pooled_above, None),
+            (ids, None),
+            (ids_below, None),
+            (ids_above, None),
+            (widening, WHOLE),
+        ],
+        [(coarse, None), (stats_coarse, None), (masks_shape, mask_spec(masks_shape))],
+        [
+            coarse_spread(1),
+            coarse_stacked(1),
+            vmem(3, 3 * FINE, 2 * GROUP),
+            vmem(depth + 2, CELLS + 4 * RIM, 2 * GROUP, dtype=F32),
+        ],
+    )
+    masked = (masks, mask_spec(masks))
     norm_one, below_one, above_one = all_reduce_stats(
         stats_one, True, depth * CELLS, [z_one], 2
     )
@@ -1285,7 +1565,7 @@
             (below_one, None),
             (above_one, None),
             (norm_one, WHOLE),
-            (scale[0], WHOLE),
+            (scales, WHOLE),
             masked,
             (bottom, WHOLE),
         ],
@@ -1303,14 +1583,13 @@
             (below_two, None),
             (above_two, None),
             (norm_two, WHOLE),
-            (scale[1], WHOLE),
+            (scales, WHOLE),
             (skip, None),
             (skip_below, None),
             (skip_above, None),
-            (gates, WHOLE),
-            (gate_rows, WHOLE),
+            (gating, WHOLE),
             masked,
-            (merging, WHOLE),
+            (merging_turned, WHOLE),
         ],
         [
             (fine, None),
@@ -1324,6 +1603,7 @@
             fine_spread(3),
             fine_stack(3),
             vmem(3, 12 * FINE, FINE),
+            vmem(3 * FINE, span),
         ],
     )
     norm_three, below_three, above_three = all_reduce_stats(
@@ -1337,7 +1617,7 @@
             (below_three, None),
             (above_three, None),
             (norm_three, WHOLE),
-            (scale[2], WHOLE),
+            (scales, WHOLE),
             masked,
             (closing, WHOLE),
         ],
@@ -1351,13 +1631,12 @@
     decoded, partial_four = run(
         decoded_kernel,
         patches,
-        [(z_four, None), (grad, None), (norm_four, WHOLE), (scale[3], WHOLE)],
-        [(shape(patches, planes, GROUP, cells, dtype=BF16), None), (stats_fine, None)],
+        [(z_four, None), (grad, None), (norm_four, WHOLE), (scales, WHOLE)],
+        [(shape(*skip_features.shape, dtype=BF16), None), (stats_fine, None)],
         [vmem(4 * CELLS, 4 * CELLS)],
     )
     (sums_four,) = all_reduce_stats(partial_four, False, planes * CELLS, [], 6)
-    closing_flipped = flipped(closing.astype(BF16))
-    closing_shape = shape(*closing.shape)
+    closing_shape = shape(*closing.shape, dtype=BF16)
     back_three, partial_three, closing_grad = run(
         closing_back_kernel,
         patches,
@@ -1370,13 +1649,12 @@
             (grad_above, None),
             (norm_four, WHOLE),
             (sums_four, WHOLE),
-            (scale[3], WHOLE),
+            (scales, WHOLE),
             (out_three, None),
             (z_three, None),
             (norm_three, WHOLE),
-            (scale[2], WHOLE),
             masked,
-            (closing_flipped, WHOLE),
+            (closing, WHOLE),
         ],
         [(fine, None), (stats_fine, None), (closing_shape, constant(closing_shape))],
         [
@@ -1391,9 +1669,8 @@
     sums_three, back_below, back_above = all_reduce_stats(
         partial_three, False, planes * CELLS, [back_three], 7
     )
-    merging_flipped = flipped(merging.astype(BF16))
-    merging_shape = shape(*merging.shape)
-    gate_shape = shape(3 * FINE + 8, span)
+    merging_shape = shape(*merging_turned.shape, dtype=BF16)
+    gate_shape = shape(2 * inner, 2 * GROUP, dtype=BF16)
     skip_back, fine_back, merging_grad, gate_grad = run(
         merging_back_kernel,
         patches,
@@ -1406,15 +1683,14 @@
             (above_three, None),
             (norm_three, WHOLE),
             (sums_three, WHOLE),
-            (scale[2], WHOLE),
+            (scales, WHOLE),
             (skip, None),
             (attended, None),
             (upsampled, None),
             (query, None),
-            (gates, WHOLE),
-            (gate_rows, WHOLE),
+            (gating, WHOLE),
             masked,
-            (merging_flipped, WHOLE),
+            (merging_turned, WHOLE),
         ],
         [
             (fine, None),
@@ -1429,6 +1705,8 @@
             vmem(4 * FINE, planes * CELLS),
             vmem(3, 3 * FINE, 4 * FINE, dtype=F32),
             vmem(planes * CELLS, 3 * FINE, dtype=F32),
+            vmem(3 * FINE, span),
+            vmem(3 * FINE + 8, span, dtype=F32),
         ],
     )
     fine_below, fine_above = exchange_rims([fine_back], 8)
@@ -1441,7 +1719,7 @@
             (fine_above, None),
             (z_two, None),
             (norm_two, WHOLE),
-            (scale[1], WHOLE),
+            (scales, WHOLE),
         ],
         [(coarse, None), (stats_coarse, None)],
         [],
@@ -1449,8 +1727,7 @@
     sums_two, back_below, back_above = all_reduce_stats(
         partial_two, False, depth * CELLS, [back_two], 9
     )
-    bottom_flipped = flipped(bottom.astype(BF16))
-    bottom_shape = shape(*bottom.shape)
+    bottom_shape = shape(*bottom.shape, dtype=BF16)
     back_one, partial_one, bottom_grad = run(
         bottom_back_kernel,
         patches,
@@ -1463,13 +1740,12 @@
             (above_two, None),
             (norm_two, WHOLE),
             (sums_two, WHOLE),
-            (scale[1], WHOLE),
+            (scales, WHOLE),
             (out_one, None),
             (z_one, None),
             (norm_one, WHOLE),
-            (scale[0], WHOLE),
             masked,
-            (bottom_flipped, WHOLE),
+            (bottom, WHOLE),
         ],
         [(coarse, None), (stats_coarse, None), (bottom_shape, constant(bottom_shape))],
         [
@@ -1482,8 +1758,7 @@
     sums_one, back_below, back_above = all_reduce_stats(
         partial_one, False, depth * CELLS, [back_one], 10
     )
-    widening_flipped = flipped(widening.astype(BF16))
-    widening_shape = shape(*widening.shape)
+    widening_shape = shape(*widening.shape, dtype=BF16)
     skip_grad, widening_grad = run(
         widening_back_kernel,
         patches,
@@ -1496,14 +1771,14 @@
             (above_one, None),
             (norm_one, WHOLE),
             (sums_one, WHOLE),
-            (scale[0], WHOLE),
+            (scales, WHOLE),
             (pooled, None),
             (skip_back, None),
             masked,
-            (widening_flipped, WHOLE),
+            (widening, WHOLE),
         ],
         [
-            (shape(patches, planes, GROUP, cells), None),
+            (shape(*skip_features.shape), None),
             (widening_shape, constant(widening_shape)),
         ],
         [
@@ -1515,32 +1790,30 @@
         ],
     )
 
-    blocks = gate_grad[: 3 * FINE].reshape(3, 4, GROUP, 4, inner)
-    gate_rows_grad = sum(blocks[:, index, :, index] for index in range(4))
-    tail = gate_grad[3 * FINE : 3 * FINE + 2].reshape(2, 4, inner).sum(axis=1)
-    gating_grad = jnp.concatenate([gate_rows_grad.reshape(3 * GROUP, inner), tail], axis=0)
-    merging_grad, closing_grad, gating_grad, widening_grad, bottom_grad = lax.psum(
-        (merging_grad, closing_grad, gating_grad, widening_grad, bottom_grad), ("patch", "depth")
-    )
-    gain_grad = [sums_one[3], sums_two[3], sums_three[3, :decoder], sums_four[3, :decoder]]
-    shift_grad = [sums_one[2], sums_two[2], sums_three[2, :decoder], sums_four[2, :decoder]]
-    scales_grad = jnp.stack([jnp.concatenate(gain_grad), jnp.concatenate(shift_grad)])
-    states = [
-        update_state(*state)
-        for state in (
-            (widening, widening_grad, widening_velocity, widening_average, weight_decay, learning_rate),
-            (bottom, bottom_grad, bottom_velocity, bottom_average, weight_decay, learning_rate),
-            (merging, merging_grad, merging_velocity, merging_average, weight_decay, learning_rate),
-            (closing, closing_grad, closing_velocity, closing_average, weight_decay, learning_rate),
-            (gating, gating_grad, gating_velocity, gating_average, weight_decay, learning_rate),
-            (scales, scales_grad, scales_velocity, scales_average, 0.0, scale_rate),
-        )
+    second_half = jnp.concatenate([merging_grad[:, :, 2 * GROUP :], closing_grad], axis=2)
+    parts = [
+        widening_grad.reshape(-1, 2 * GROUP),
+        bottom_grad.reshape(-1, 2 * GROUP),
+        merging_grad[:, :, : 2 * GROUP].reshape(-1, 2 * GROUP),
+        second_half.reshape(-1, 2 * GROUP),
+        gate_grad,
     ]
-    outputs = (
-        jnp.transpose(decoded, (0, 2, 1, 3)),
-        jnp.transpose(skip_grad, (0, 2, 1, 3)),
-    ) + tuple(state[index] for index in range(4) for state in states)
-    return outputs
+    total = all_reduce_grads(jnp.concatenate(parts, axis=0), 11)
+    turned = lambda *arrays: [jnp.swapaxes(array, -1, -2) for array in arrays]
+    states = update(
+        total,
+        [sums_one, sums_two, sums_three, sums_four],
+        [
+            (widening, widening_velocity, widening_average),
+            (bottom, bottom_velocity, bottom_average),
+            turned(merging, merging_velocity, merging_average),
+            (closing, closing_velocity, closing_average),
+            turned(gating, gating_velocity, gating_average),
+            (scales, scales_velocity, scales_average),
+        ],
+    )
+    states[2], states[4] = turned(*states[2]), turned(*states[4])
+    return (decoded, skip_grad) + tuple(state[index] for index in range(4) for state in states)
 
 
 def solution(mesh):

time: 589 us -> 415 us (0.70)
  waiting for transfers between devices: 102 us -> 0 us
  Pallas kernels: 332 us -> 401 us
  local copies, waits for them, and re-layouts: 59.3 us -> 6.28 us
  blocking collectives: 39.2 us -> 0 us
  other arithmetic: 28.6 us -> 0.25 us
  between operations: 14.9 us -> 1.35 us
    psum x1 -> x0, waiting for transfers between devices: 102 us -> none  [local(): lax.psum((merging_grad, closing_grad, gating_grad, widening_grad, bottom_...]
    pallas_call x0 -> x2, Pallas kernels: none -> 61.6 us  [the longest x1 43 us: all_reduce_grads(): pl.pallas_call(functools.partial(grads_kernel, plan, unit), out_shape=jax...]
    psum x1 -> x0, blocking collectives: 39.2 us -> none  [local(): lax.psum((merging_grad, closing_grad, gating_grad, widening_grad, bottom_...]
    unnamed x83 -> x13, local copies, waits for them, and re-layouts: 31 us -> 4.18 us
    convert_element_type x9 -> x0, other arithmetic: 18.6 us -> none  [the longest x6 15.9 us: update_state(): return (weight_next, momentum, smoothed, weight_next.astype(jnp.bfloat16))]
    transpose x5 -> x0, local copies, waits for them, and re-layouts: 9.64 us -> none  [the longest x1 5.9 us: local(): grad_by_plane = jnp.transpose(output_grad, (0, 2, 1, 3))]
    add x7 -> x0, other arithmetic: 8.77 us -> none  [the longest x6 8.49 us: update_state(): smoothed = average_decay * average + (1.0 - average_decay) * weight_next]
    pallas_call x11, Pallas kernels: 241 us -> 249 us  [run(): pl.pallas_call(kernel, grid=(patches,), out_shape=[array for array, _ in...]
  transfers between devices with their start and end apart: 3 -> 0, of which waited for: 1 -> 0; matrix products, arithmetic and copies ran while one was open for 8% -> 0% of each run, Pallas kernels for 0% -> 0%
where the time goes in v2:
time: 415 us; the launch traced here: 409 us
  Pallas kernels  401 us (97%)
  local copies, waits for them, and re-layouts  6.28 us (2%)
    pallas_call x11, Pallas kernels, run(): pl.pallas_call(kernel, grid=(patches,), out_shape=[array for array, _ in...  249 us
    pallas_call x8, Pallas kernels, all_reduce_stats(): pl.pallas_call(functools.partial(reduce_kernel, npat, ndep, low, moments,...  84.1 us
    pallas_call x1, Pallas kernels, all_reduce_grads(): pl.pallas_call(functools.partial(grads_kernel, plan, unit), out_shape=jax...  43 us
    pallas_call x1, Pallas kernels, update(): pl.pallas_call(update_kernel, grid=(steps,), out_shape=outs, in_specs=[WH...  18.6 us

profile of v2, /device:TPU:0, one launch (start us, length us, event | category | flops | bytes accessed | tf_op | source)
XLA Modules:
  0.0 408.7 jit_solution(5170698283277368574)
XLA Ops:
  0.7 1.5 copy.47.gating
  2.2 14.0 %shard_map.404 = (bf16[4,4,256,256]{3,2,1,0:T(8,128)(2,1)}, bf16[4,4,256,256]{3,2,1,0:T(8,128)(2,1)}, bf16[4,2,256,128]{3,2,1,0:T(8,128)(2,1)}, bf16[4,2,256,128]{3,2,1,0:T(8,128)(2,1)}) custom-call(bf16[4,64,4,1024]{3,2,1,0:T(4,128)(2,1)} %skip.1, bf16[4,64,4,1024]{3,2,1,0:T(4,128)(2,1)} %grad.1, s32[4,4,1024]{2,1,0:T(4,128)} %ids.1), custom_call_target="tpu_custom_call" | custom-call | tf_op jit(solution)/shard_map/pallas_call | solution.py:1456
  16.1 4.0 shard_map.405
  20.1 9.1 %shard_map.406 = (f32[4,2,256,128]{3,2,1,0:T(8,128)}, f32[4,8,128]{2,1,0:T(8,128)}, bf16[9,4,512,256]{3,2,1,0:T(8,128)(2,1)}) custom-call(bf16[4,2,256,128]{3,2,1,0:T(8,128)(2,1)} %get-tuple-element.115.refs_2_.pooled, bf16[4,256,128]{2,1,0:T(8,128)(2,1)} %get-tuple-element.119.below, bf16[4,256,128]{2,1,0:T(8,128)(2,1)} %get-tuple-element.120.above, ...), custom_call_target="tpu_custom_call" | custom-call | tf_op jit(solution)/shard_map/pallas_call | solution.py:1456
  29.2 12.7 %shard_map.407 = (f32[8,128]{1,0:T(8,128)}, f32[4,256,128]{2,1,0:T(8,128)}, f32[4,256,128]{2,1,0:T(8,128)}) custom-call(f32[4,8,128]{2,1,0:T(8,128)} %get-tuple-element.124.refs_0_, f32[4,2,256,128]{3,2,1,0:T(8,128)} %get-tuple-element.123.refs_1_.z.z_before), custom_call_target="tpu_custom_call" | custom-call | tf_op jit(solution)/shard_map/pallas_call | solution.py:235
  41.9 10.6 %shard_map.408 = (f32[4,2,256,128]{3,2,1,0:T(8,128)}, bf16[4,2,256,128]{3,2,1,0:T(8,128)(2,1)}, f32[4,8,128]{2,1,0:T(8,128)}) custom-call(f32[4,2,256,128]{3,2,1,0:T(8,128)} %get-tuple-element.123.refs_1_.z.z_before, f32[4,256,128]{2,1,0:T(8,128)} %get-tuple-element.125.below, f32[4,256,128]{2,1,0:T(8,128)} %get-tuple-element.126.above, ...), custom_call_target="tpu_custom_call" | custom-call | tf_op jit(solution)/shard_map/pallas_call | solution.py:1456
  52.5 10.9 %shard_map.409 = (f32[8,128]{1,0:T(8,128)}, f32[4,256,128]{2,1,0:T(8,128)}, f32[4,256,128]{2,1,0:T(8,128)}) custom-call(f32[4,8,128]{2,1,0:T(8,128)} %get-tuple-element.130.refs_0_, f32[4,2,256,128]{3,2,1,0:T(8,128)} %get-tuple-element.129.refs_1_.z), custom_call_target="tpu_custom_call" | custom-call | tf_op jit(solution)/shard_map/pallas_call | solution.py:235
  63.4 44.3 %shard_map.410 = (f32[4,4,256,256]{3,2,1,0:T(8,128)}, bf16[4,4,256,256]{3,2,1,0:T(8,128)(2,1)}, bf16[4,4,256,512]{3,2,1,0:T(8,128)(2,1)}, f32[4,4,256,128]{3,2,1,0:T(8,128)}, f32[4,8,256]{2,1,0:T(8,128)}) custom-call(f32[4,2,256,128]{3,2,1,0:T(8,128)} %get-tuple-element.129.refs_1_.z, f32[4,256,128]{2,1,0:T(8,128)} %get-tuple-element.131.below, ...), custom_call_target="tpu_custom_call" | custom-call | tf_op jit(solution)/shard_map/pallas_call | solution.py:1456
  107.7 9.3 %shard_map.411 = (f32[8,256]{1,0:T(8,128)}, f32[4,256,256]{2,1,0:T(8,128)}, f32[4,256,256]{2,1,0:T(8,128)}) custom-call(f32[4,8,256]{2,1,0:T(8,128)} %get-tuple-element.137.refs_0_, f32[4,4,256,256]{3,2,1,0:T(8,128)} %get-tuple-element.136.refs_1_.z.z_before), custom_call_target="tpu_custom_call" | custom-call | tf_op jit(solution)/shard_map/pallas_call | solution.py:235
  117.0 15.5 %shard_map.412 = (f32[4,4,256,256]{3,2,1,0:T(8,128)}, bf16[4,4,256,256]{3,2,1,0:T(8,128)(2,1)}, f32[4,8,256]{2,1,0:T(8,128)}) custom-call(f32[4,4,256,256]{3,2,1,0:T(8,128)} %get-tuple-element.136.refs_1_.z.z_before, f32[4,256,256]{2,1,0:T(8,128)} %get-tuple-element.138.below, f32[4,256,256]{2,1,0:T(8,128)} %get-tuple-element.139.above, ...), custom_call_target="tpu_custom_call" | custom-call | tf_op jit(solution)/shard_map/pallas_call | solution.py:1456
  132.5 11.0 %shard_map.413 = (f32[8,256]{1,0:T(8,128)}, f32[4,256,256]{2,1,0:T(8,128)}, f32[4,256,256]{2,1,0:T(8,128)}) custom-call(f32[4,8,256]{2,1,0:T(8,128)} %get-tuple-element.142.refs_0_, f32[4,4,256,256]{3,2,1,0:T(8,128)} %get-tuple-element.141.refs_1_.z), custom_call_target="tpu_custom_call" | custom-call | tf_op jit(solution)/shard_map/pallas_call | solution.py:235
  143.4 9.8 %shard_map.414 = (bf16[4,64,4,1024]{3,2,1,0:T(4,128)(2,1)}, f32[4,8,256]{2,1,0:T(8,128)}) custom-call(f32[4,4,256,256]{3,2,1,0:T(8,128)} %get-tuple-element.141.refs_1_.z, bf16[4,4,256,256]{3,2,1,0:T(8,128)(2,1)} %get-tuple-element.117.refs_1_.grad, f32[8,256]{1,0:T(8,128)} %get-tuple-element.143.stats_in, f32[2,384]{1,0:T(2,128)} %refs_15_.1), custom_call_target="tpu_custom_call" | custom-call | tf_op jit(solution)/shard_map/pallas_call | solution.py:1456
  153.2 9.3 %shard_map.415.sums_in.four = f32[8,256]{1,0:T(8,128)} custom-call(f32[4,8,256]{2,1,0:T(8,128)} %get-tuple-element.149.refs_0_), custom_call_target="tpu_custom_call" | custom-call | tf_op jit(solution)/shard_map/pallas_call | solution.py:235
  162.5 26.3 %shard_map.416 = (f32[4,4,256,256]{3,2,1,0:T(8,128)}, f32[4,8,256]{2,1,0:T(8,128)}, bf16[27,64,64]{2,1,0:T(8,128)(2,1)}) custom-call(f32[4,4,256,256]{3,2,1,0:T(8,128)} %get-tuple-element.141.refs_1_.z, f32[4,256,256]{2,1,0:T(8,128)} %get-tuple-element.145.below, f32[4,256,256]{2,1,0:T(8,128)} %get-tuple-element.146.above, ...), custom_call_target="tpu_custom_call" | custom-call | tf_op jit(solution)/shard_map/pallas_call | solution.py:1456
  188.8 10.9 %shard_map.417 = (f32[8,256]{1,0:T(8,128)}, f32[4,256,256]{2,1,0:T(8,128)}, f32[4,256,256]{2,1,0:T(8,128)}) custom-call(f32[4,8,256]{2,1,0:T(8,128)} %get-tuple-element.152.refs_0_, f32[4,4,256,256]{3,2,1,0:T(8,128)} %get-tuple-element.151.refs_1_.grad), custom_call_target="tpu_custom_call" | custom-call | tf_op jit(solution)/shard_map/pallas_call | solution.py:235
  199.7 0.0 copy-start.2
  199.7 67.3 %shard_map.418 = (f32[4,4,256,256]{3,2,1,0:T(8,128)}, f32[4,4,256,128]{3,2,1,0:T(8,128)}, bf16[27,64,192]{2,1,0:T(8,128)(2,1)}, bf16[64,128]{1,0:T(8,128)(2,1)}) custom-call(f32[4,4,256,256]{3,2,1,0:T(8,128)} %get-tuple-element.151.refs_1_.grad, f32[4,256,256]{2,1,0:T(8,128)} %get-tuple-element.153.grad_below, f32[4,256,256]{2,1,0:T(8,128)} %get-tuple-element.154.grad_above, ...), custom_call_target="tpu_custom_call" | custom-call | tf_op jit(solution)/shard_map/pallas_call | solution.py:1456
  267.0 1.0 slice.7
  268.1 1.0 slice.6
  269.1 0.0 copy-done.2
  269.1 0.2 pad_maximum_fusion
  269.4 2.3 shard_map.419
  271.7 4.3 %shard_map.420 = (f32[4,2,256,128]{3,2,1,0:T(8,128)}, f32[4,8,128]{2,1,0:T(8,128)}) custom-call(f32[4,4,256,128]{3,2,1,0:T(8,128)} %get-tuple-element.159.refs_0_.fine_back, f32[4,256,128]{2,1,0:T(8,128)} %get-tuple-element.160.below, f32[4,256,128]{2,1,0:T(8,128)} %get-tuple-element.161.above, f32[4,2,256,128]{3,2,1,0:T(8,128)} %get-tuple-element.129.refs_1_.z, ...), custom_call_target="tpu_custom_call" | custom-call | tf_op jit(solution)/shard_map/pallas_call | solution.py:1456
  276.0 9.2 %shard_map.421 = (f32[8,128]{1,0:T(8,128)}, f32[4,256,128]{2,1,0:T(8,128)}, f32[4,256,128]{2,1,0:T(8,128)}) custom-call(f32[4,8,128]{2,1,0:T(8,128)} %get-tuple-element.163.refs_0_, f32[4,2,256,128]{3,2,1,0:T(8,128)} %get-tuple-element.162.refs_1_.grad), custom_call_target="tpu_custom_call" | custom-call | tf_op jit(solution)/shard_map/pallas_call | solution.py:235
  285.2 15.8 %shard_map.422 = (f32[4,2,256,128]{3,2,1,0:T(8,128)}, f32[4,8,128]{2,1,0:T(8,128)}, bf16[27,128,128]{2,1,0:T(8,128)(2,1)}) custom-call(f32[4,2,256,128]{3,2,1,0:T(8,128)} %get-tuple-element.162.refs_1_.grad, f32[4,256,128]{2,1,0:T(8,128)} %get-tuple-element.164.grad_below, f32[4,256,128]{2,1,0:T(8,128)} %get-tuple-element.165.grad_above, ...), custom_call_target="tpu_custom_call" | custom-call | tf_op jit(solution)/shard_map/pallas_call | solution.py:1456
  301.0 10.9 %shard_map.423 = (f32[8,128]{1,0:T(8,128)}, f32[4,256,128]{2,1,0:T(8,128)}, f32[4,256,128]{2,1,0:T(8,128)}) custom-call(f32[4,8,128]{2,1,0:T(8,128)} %get-tuple-element.169.refs_0_, f32[4,2,256,128]{3,2,1,0:T(8,128)} %get-tuple-element.168.refs_1_.grad), custom_call_target="tpu_custom_call" | custom-call | tf_op jit(solution)/shard_map/pallas_call | solution.py:235
  311.9 0.0 copy-start.1
  311.9 32.1 %shard_map.424 = (f32[4,64,4,1024]{3,2,1,0:T(4,128)}, bf16[27,64,128]{2,1,0:T(8,128)(2,1)}) custom-call(f32[4,2,256,128]{3,2,1,0:T(8,128)} %get-tuple-element.168.refs_1_.grad, f32[4,256,128]{2,1,0:T(8,128)} %get-tuple-element.170.grad_below, f32[4,256,128]{2,1,0:T(8,128)} %get-tuple-element.171.grad_above, ...), custom_call_target="tpu_custom_call" | custom-call | tf_op jit(solution)/shard_map/pallas_call | solution.py:1456
  343.9 0.0 copy-start.3
  344.0 1.0 constant_dynamic-update-slice_fusion.4
  345.0 0.0 copy-done.1
  345.0 0.1 constant_dynamic-update-slice_fusion.3
  345.1 0.1 constant_dynamic-update-slice_fusion.2
  345.2 0.1 constant_dynamic-update-slice_fusion.1
  345.3 0.0 copy-done.3
  345.3 0.0 copy-start
  345.3 1.4 copy-done
  346.7 43.0 %shard_map.425.grads = bf16[8704,128]{1,0:T(8,128)(2,1)} custom-call(bf16[8704,128]{1,0:T(8,128)(2,1)} %copy-done), custom_call_target="tpu_custom_call" | custom-call | tf_op jit(solution)/shard_map/pallas_call | solution.py:365
  389.6 18.6 %shard_map.426 = (f32[27,64,128]{2,1,0:T(8,128)}, f32[27,128,128]{2,1,0:T(8,128)}, f32[27,64,192]{2,1,0:T(8,128)}, f32[27,64,64]{2,1,0:T(8,128)}, f32[32,194]{1,...) custom-call(bf16[8704,128]{1,0:T(8,128)(2,1)} %shard_map.425.grads, ...), custom_call_target="tpu_custom_call" | custom-call | tf_op jit(solution)/shard_map/pallas_call | solution.py:1424
  (1 shorter events, 0.0 us)
Async XLA Ops:
  199.7 69.4 %copy-start.2 = (bf16[27,64,64]{2,1,0:T(8,128)(2,1)S(1)}, bf16[27,64,64]{2,1,0:T(8,128)(2,1)}, u32[]{:S(2)}) copy-start(bf16[27,64,64]{2,1,0:T(8,128)(2,1)} %get-tuple-element.178) | copy-start | bytes 663556
  311.9 33.1 %copy-start.1 = (bf16[27,128,128]{2,1,0:T(8,128)(2,1)S(1)}, bf16[27,128,128]{2,1,0:T(8,128)(2,1)}, u32[]{:S(2)}) copy-start(bf16[27,128,128]{2,1,0:T(8,128)(2,1)} %get-tuple-element.176) | copy-start | bytes 2654212
  343.9 1.3 copy-start.3
  345.3 1.4 copy-start

commit v3 on v2

--- a/solution.py
+++ b/solution.py
@@ -144,13 +144,17 @@
     return mean, functools.reduce(jnp.add, second) + count * spread
 
 
-def reduce_kernel(npat, ndep, low, moments, samples, count, *refs):
-    stats, sources = refs[0], refs[1 : 1 + count]
-    result, outs = refs[1 + count], refs[2 + count : 2 + 3 * count]
-    near, far, near_send, near_recv, far_send, far_recv = refs[2 + 3 * count : 8 + 3 * count]
+def stats_plan():
+    npat, ndep = lax.axis_size("patch"), lax.axis_size("depth")
+    low = 4 if npat % 4 == 0 else 1
+    return ndep, low, npat // low
+
+
+def stats_devices(plan):
+    ndep, low, high = plan
     mp, md = lax.axis_index("patch"), lax.axis_index("depth")
-    high, peers = npat // low, low * ndep
     mine_low, mine_high = lax.rem(mp, low), mp // low
+    peers = low * ndep
     place = mine_low * ndep + md
 
     def near_device(step):
@@ -160,14 +164,26 @@
     def far_device(step):
         return (lax.rem(mine_high + step, high) * low + mine_low, md)
 
+    return (near_device, peers), (far_device, high)
+
+
+def greet(plan):
     barrier = pltpu.get_barrier_semaphore()
-    for device, size in ((far_device, high), (near_device, peers)):
+    for device, size in reversed(stats_devices(plan)):
         for step in range(1, size):
             pl.semaphore_signal(barrier, inc=1, device_id=device(step), device_id_type=MESH)
-    width = stats.shape[-1]
+
+
+def await_greetings(plan):
+    ndep, low, high = plan
+    pl.semaphore_wait(pltpu.get_barrier_semaphore(), low * ndep + high - 2)
+
+
+def sum_stats(plan, moments, samples, parts, result, near, far, sems):
+    width = parts.shape[-1]
     amount = samples
-    first, second = combine([stats[index] for index in range(stats.shape[0])], moments, amount)
-    amount = amount * stats.shape[0]
+    first, second = combine([parts[index] for index in range(parts.shape[0])], moments, amount)
+    amount = amount * parts.shape[0]
     if width == FINE:
         pair = jnp.concatenate([first, second, jnp.zeros((6, width), F32)], axis=0)
         turned = [pair] + [pltpu.roll(pair, step * GROUP, 1) for step in range(1, 4)]
@@ -175,27 +191,21 @@
         amount = amount * 4
     near[0, 0:1] = first
     near[0, 1:2] = second
-    pl.semaphore_wait(barrier, high + peers - 2)
-    if count:
-        start, finish = halo_steps(
-            [(sources[i], outs[2 * i], outs[2 * i + 1]) for i in range(count)], refs[8 + 3 * count]
-        )
-        start()
-    for device, size, buffer, send, recv in (
-        (near_device, peers, near, near_send, near_recv),
-        (far_device, high, far, far_send, far_recv),
-    ):
-        copies = [
-            pltpu.make_async_remote_copy(
-                src_ref=buffer.at[0],
-                dst_ref=buffer.at[step],
-                send_sem=send.at[step],
-                recv_sem=recv.at[step],
-                device_id=device(step),
-                device_id_type=MESH,
+    used = 0
+    for (device, size), buffer in zip(stats_devices(plan), (near, far)):
+        copies = []
+        for step in range(1, size):
+            copies.append(
+                pltpu.make_async_remote_copy(
+                    src_ref=buffer.at[0],
+                    dst_ref=buffer.at[step],
+                    send_sem=sems.at[used],
+                    recv_sem=sems.at[used + 1],
+                    device_id=device(step),
+                    device_id_type=MESH,
+                )
             )
-            for step in range(1, size)
-        ]
+            used += 2
         for copy in copies:
             copy.start()
         for copy in copies:
@@ -211,35 +221,41 @@
     result[1:2] = second * (1.0 / amount)
     result[2:3] = first
     result[3:4] = second
-    if count:
-        finish()
-
-
-def all_reduce_stats(stats, moments, samples, arrays, number):
-    npat, ndep = lax.axis_size("patch"), lax.axis_size("depth")
-    low = 4 if npat % 4 == 0 else 1
-    width = stats.shape[-1]
-    anywhere = pl.BlockSpec(memory_space=pl.ANY)
-    inside = pl.BlockSpec(memory_space=pltpu.VMEM)
-    dma = pltpu.SemaphoreType.DMA
-    scratch = [
-        pltpu.VMEM((low * ndep, 2, width), F32),
-        pltpu.VMEM((npat // low, 2, width), F32),
-        dma((low * ndep,)),
-        dma((low * ndep,)),
-        dma((npat // low,)),
-        dma((npat // low,)),
-    ]
-    if arrays:
-        scratch.append(dma((4 * len(arrays),)))
-    return pl.pallas_call(
-        functools.partial(reduce_kernel, npat, ndep, low, moments, float(samples), len(arrays)),
-        out_shape=[jax.ShapeDtypeStruct((8, width), F32)] + rim_shapes(arrays),
-        in_specs=[inside] + [anywhere] * len(arrays),
-        out_specs=[inside] + [anywhere] * (2 * len(arrays)),
-        scratch_shapes=scratch,
-        compiler_params=params(collective_id=number, has_side_effects=True),
-    )(stats, *arrays)
+
+
+def with_stats(kernel, plan, moments, samples, counts, stats_at, rims_of, *refs):
+    inputs, outputs, scratch = counts
+    ins, refs = refs[:inputs], refs[inputs:]
+    outs, refs = list(refs[: outputs - 1]), refs[outputs - 1 :]
+    result, refs = refs[0], refs[1:]
+    if rims_of is not None:
+        below, above, refs = refs[0], refs[1], refs[2:]
+    own, refs = refs[:scratch], refs[scratch:]
+    stats, parts, near, far, sems = refs[:5]
+    step = pl.program_id(0)
+
+    @pl.when(step == 0)
+    def _():
+        greet(plan)
+
+    source = None if rims_of is None else outs[rims_of]
+    outs.insert(stats_at, stats)
+    kernel(*ins, *outs, *own)
+    parts[step] = stats[0]
+    if rims_of is not None:
+        rims, rim_sems = refs[5:]
+        rims[step, 0] = source[0, 0]
+        rims[step, 1] = source[0, source.shape[1] - 1]
+
+    @pl.when(step == pl.num_programs(0) - 1)
+    def _():
+        await_greetings(plan)
+        if rims_of is not None:
+            start, finish = halo_steps([(rims, below, above)], rim_sems)
+            start()
+        sum_stats(plan, moments, samples, parts, result, near, far, sems)
+        if rims_of is not None:
+            finish()
 
 
 def grads_plan(units, ndep, low, high):
@@ -472,22 +488,27 @@
 fine_rows = ((0, 1), (1, 0), (1, 1), (2, 0))
 
 
-def stack_fine(spread, masks, stack, groups, depth):
-    for slot in range(4):
-        level = (slot + 1) // 2
-        for plane in range(depth):
-            for index, (step, parity) in enumerate(fine_rows):
-                mask = masks[3 * level + step, 0, plane * CELLS : (plane + 1) * CELLS, :]
-                for group in range(groups):
-                    source = (parity * groups + group) * FINE
-                    target = (index * groups + group) * FINE
-                    row = (slot * depth + plane) * CELLS
-                    stack[row : row + CELLS, target : target + FINE] = (
-                        spread[
-                            2 * plane + slot, step * RIM : step * RIM + CELLS, source : source + FINE
-                        ]
-                        * mask
-                    )
+def stack_fine(spread, masks, stack, groups, depth, slot):
+    level = (slot + 1) // 2
+    for plane in range(depth):
+        for index, (step, parity) in enumerate(fine_rows):
+            mask = masks[3 * level + step, 0, plane * CELLS : (plane + 1) * CELLS, :]
+            for group in range(groups):
+                source = (parity * groups + group) * FINE
+                target = (index * groups + group) * FINE
+                row = (slot * depth + plane) * CELLS
+                stack[row : row + CELLS, target : target + FINE] = (
+                    spread[2 * plane + slot, step * RIM : step * RIM + CELLS, source : source + FINE]
+                    * mask
+                )
+
+
+def fine_products(spread, masks, stack, groups, depth, product):
+    stack_fine(spread, masks, stack, groups, depth, 0)
+    for level in range(3):
+        stack_fine(spread, masks, stack, groups, depth, level + 1)
+        begin = level * depth * CELLS
+        product(level, slice(begin, begin + 2 * depth * CELLS))
 
 
 def stack_coarse(spread, masks, stack, groups, depth):
@@ -519,6 +540,14 @@
     return block
 
 
+def fine_column(groups, group, phase):
+    if groups == 1:
+        return phase * GROUP
+    if group == 2:
+        return 2 * FINE + phase * GROUP
+    return phase // 2 * FINE + group * 2 * GROUP + phase % 2 * GROUP
+
+
 def fine_weights(weights, kernel, groups_in, groups_out, way):
     weights[...] = jnp.zeros(weights.shape, BF16)
 
@@ -531,7 +560,7 @@
                 for source in range(groups_in):
                     row = ((row_slot * groups_in + source) * 4 + column_slot) * GROUP
                     for target in range(groups_out):
-                        column = target * FINE + phase * GROUP
+                        column = fine_column(groups_out, target, phase)
                         weights[level, row : row + GROUP, column : column + GROUP] = block[
                             source * GROUP : (source + 1) * GROUP,
                             target * GROUP : (target + 1) * GROUP,
@@ -564,9 +593,10 @@
             for group in range(groups):
                 total = None
                 for phase in range(4):
-                    row = group * FINE + phase * GROUP
-                    slot = (phase // 2 + row_step) * 4 + phase % 2 + column_step
-                    block = sums[level, row : row + GROUP, slot * GROUP : (slot + 1) * GROUP]
+                    row = (2 * group + phase % 2) * GROUP
+                    slot = row_step * 4 + phase % 2 + column_step
+                    columns = slice(slot * GROUP, (slot + 1) * GROUP)
+                    block = sums[level, phase // 2, row : row + GROUP, columns]
                     total = block if total is None else total + block
                 total = total.astype(BF16)
                 blocks.append(transposed(total, identity(GROUP)) if turn else total)
@@ -590,6 +620,16 @@
     lax.fori_loop(0, 3, fill, 0)
 
 
+def add_kernel_products(totals, turned, stack, level, rows, groups):
+    size = groups * 2 * GROUP
+    for parity in range(2):
+        totals[level, parity] += jnp.dot(
+            turned[parity * size : (parity + 1) * size],
+            stack[rows, parity * FINE : (parity + 3) * FINE],
+            preferred_element_type=F32,
+        )
+
+
 def apply_weights(stack, weights, rows, step_rows):
     total = None
     for level in range(3):
@@ -599,6 +639,16 @@
     return total
 
 
+def forward_products(spread, masks, stack, weights, groups, depth):
+    terms = []
+
+    def product(level, rows):
+        terms.append(jnp.dot(stack[rows, :], weights[level], preferred_element_type=F32))
+
+    fine_products(spread, masks, stack, groups, depth, product)
+    return terms[0] + terms[1] + terms[2]
+
+
 def identity(size):
     rows = lax.broadcasted_iota(jnp.int32, (size, size), 0)
     columns = lax.broadcasted_iota(jnp.int32, (size, size), 1)
@@ -628,10 +678,11 @@
     return mean, jnp.sum(jnp.square(values - mean), axis=0, keepdims=True)
 
 
-def voxel_order(size, transpose):
-    rows = lax.broadcasted_iota(jnp.int32, (size, size), 1 if transpose else 0)
-    columns = lax.broadcasted_iota(jnp.int32, (size, size), 0 if transpose else 1)
-    phase, cell = rows // CELLS, rows % CELLS
+def voxel_order():
+    size = 4 * GROUP
+    rows = lax.broadcasted_iota(jnp.int32, (size, size), 0)
+    columns = lax.broadcasted_iota(jnp.int32, (size, size), 1)
+    phase, cell = rows // GROUP, rows % GROUP
     row = 2 * (cell // HALF_WIDTH) + phase // 2
     column = 2 * (cell % HALF_WIDTH) + phase % 2
     return jnp.where(columns == row * WIDTH + column, 1.0, 0.0).astype(BF16)
@@ -645,38 +696,48 @@
     return jnp.where(same, 1.0, 0.0).astype(BF16)
 
 
-def prepare_kernel(skip, grad, ids, skip_out, grad_out, pooled, ids_out, order):
+def prepare_kernel(skip, grad, ids, skip_out, grad_out, pooled, ids_out):
     planes = skip.shape[2]
     depth = planes // 2
     size = 4 * CELLS
-
-    @pl.when(pl.program_id(0) == 0)
-    def _():
-        order[...] = voxel_order(size, False)
-
     contract = (((1,), (1,)), ((), ()))
-    by_plane = plane_order(planes)
+    by_plane, order = plane_order(planes), voxel_order()
     for source, target in ((skip, skip_out), (grad, grad_out)):
         lines = source[0].reshape(planes * GROUP, size)
-        turned = lax.dot_general(order[...], lines, contract, preferred_element_type=F32)
-        turned = jnp.dot(turned.astype(BF16), by_plane, preferred_element_type=F32)
-        for plane in range(planes):
-            pieces = [
-                turned[phase * CELLS : (phase + 1) * CELLS, plane * GROUP : (plane + 1) * GROUP]
-                for phase in range(4)
-            ]
-            target[0, plane] = jnp.concatenate(pieces, axis=1).astype(BF16)
+        lines = lax.dot_general(
+            by_plane, lines, (((0,), (0,)), ((), ())), preferred_element_type=F32
+        ).astype(BF16)
+        for block in range(size // FINE):
+            turned = lax.dot_general(
+                order,
+                lines[:, block * FINE : (block + 1) * FINE],
+                contract,
+                preferred_element_type=F32,
+            )
+            for plane in range(planes):
+                pieces = [
+                    turned[phase * GROUP : (phase + 1) * GROUP, plane * GROUP : (plane + 1) * GROUP]
+                    for phase in range(4)
+                ]
+                target[0, plane, block * GROUP : (block + 1) * GROUP, :] = jnp.concatenate(
+                    pieces, axis=1
+                ).astype(BF16)
     for plane in range(depth):
         total = skip_out[0, 2 * plane].astype(F32) + skip_out[0, 2 * plane + 1].astype(F32)
         total = total[:, : 2 * GROUP] + total[:, 2 * GROUP :]
         total = total + pltpu.roll(total, GROUP, 1)
         pooled[0, plane] = (total * 0.125).astype(BF16)
-    names = lax.dot_general(
-        order[:CELLS], ids[0].astype(F32).astype(BF16), contract, preferred_element_type=F32
-    )
-    for plane in range(depth):
-        column = names[:, 2 * plane : 2 * plane + 1]
-        ids_out[0, plane] = jnp.broadcast_to(column, (CELLS, 2 * GROUP)).astype(BF16)
+    names = ids[0].astype(F32).astype(BF16)
+    for block in range(size // FINE):
+        found = lax.dot_general(
+            order[:GROUP],
+            names[:, block * FINE : (block + 1) * FINE],
+            contract,
+            preferred_element_type=F32,
+        )
+        for plane in range(depth):
+            column = jnp.broadcast_to(found[:, 2 * plane : 2 * plane + 1], (GROUP, 2 * GROUP))
+            ids_out[0, plane, block * GROUP : (block + 1) * GROUP, :] = column.astype(BF16)
 
 
 def fill_masks(masks, centers, rims, flags, spread):
@@ -820,46 +881,55 @@
     spans = lax.broadcasted_iota(jnp.int32, (span, FINE), 0) // (span // 4)
     lanes = lax.broadcasted_iota(jnp.int32, (span, FINE), 1) // GROUP
     gather = jnp.where(spans == lanes, 1.0, 0.0).astype(BF16)
-    for index in range(planes + 2):
-        fine = index - 1
-        center = fine // 2
-        other = center - 1 if fine % 2 == 0 else center + 1
-        doubled = 0.75 * coarse[center + 1] + 0.25 * coarse[other + 1]
-        grid = widened(doubled, low, column)
-        pieces = []
-        for group in range(2):
-            for parity in range(2):
-                even, odd = grid[parity]
-                if group == 0:
-                    pair = jnp.where(low, even, pltpu.roll(odd, GROUP, 1))
-                else:
-                    pair = jnp.where(low, pltpu.roll(even, GROUP, 1), odd)
-                pair = pair.astype(BF16)
-                pieces.append(pair)
-                pair = pair.astype(F32)
-                turned = pltpu.roll(pair, GROUP, 1)
-                spread_pair(spread, index, (parity * 3 + 1 + group) * FINE, pair, turned, low)
-        up = jnp.concatenate(pieces, axis=1)
-        if fine < 0:
-            features = at_edge(first, skip_below[0].astype(F32), 0.0).astype(BF16)
-        elif fine == planes:
-            features = at_edge(last, skip_above[0].astype(F32), 0.0).astype(BF16)
-        else:
-            features = skip[0, fine]
+    def make_planes(indices):
+        ups, kinds = [], []
+        for index in indices:
+            fine = index - 1
+            center = fine // 2
+            other = center - 1 if fine % 2 == 0 else center + 1
+            doubled = 0.75 * coarse[center + 1] + 0.25 * coarse[other + 1]
+            grid = widened(doubled, low, column)
+            pieces = []
+            for group in range(2):
+                for parity in range(2):
+                    even, odd = grid[parity]
+                    if group == 0:
+                        pair = jnp.where(low, even, pltpu.roll(odd, GROUP, 1))
+                    else:
+                        pair = jnp.where(low, pltpu.roll(even, GROUP, 1), odd)
+                    pair = pair.astype(BF16)
+                    pieces.append(pair)
+                    pair = pair.astype(F32)
+                    turned = pltpu.roll(pair, GROUP, 1)
+                    spread_pair(spread, index, (parity * 3 + 1 + group) * FINE, pair, turned, low)
+            ups.append(jnp.concatenate(pieces, axis=1))
+            if fine < 0:
+                features = at_edge(first, skip_below[0].astype(F32), 0.0).astype(BF16)
+            elif fine == planes:
+                features = at_edge(last, skip_above[0].astype(F32), 0.0).astype(BF16)
+            else:
+                features = skip[0, fine]
+            kinds.append(features)
+        features = jnp.concatenate(kinds, axis=0)
         asked = (
             jnp.dot(features, gates[:FINE], preferred_element_type=F32)
-            + jnp.dot(up, gates[FINE:], preferred_element_type=F32)
+            + jnp.dot(jnp.concatenate(ups, axis=0), gates[FINE:], preferred_element_type=F32)
             + gate_rows[0:1]
         )
         logits = dot_exact(silu(asked) * gate_rows[1:2], gather)
         kept = (features.astype(F32) * jax.nn.sigmoid(logits)).astype(BF16)
-        spread_fine(spread, index, 3, 0, kept.astype(F32))
-        if 0 <= fine < planes:
-            attended[0, fine] = kept
-            upsampled[0, fine] = up
-            query[0, fine] = asked
-    stack_fine(spread, masks, stack, 3, depth)
-    values = apply_weights(stack, weights, planes * CELLS, depth * CELLS)
+        for place, index in enumerate(indices):
+            fine = index - 1
+            lines = slice(place * CELLS, (place + 1) * CELLS)
+            spread_fine(spread, index, 3, 0, kept[lines].astype(F32))
+            if 0 <= fine < planes:
+                attended[0, fine] = kept[lines]
+                upsampled[0, fine] = ups[place]
+                query[0, fine] = asked[lines]
+
+    make_planes(range(planes))
+    make_planes((planes, planes + 1))
+    values = forward_products(spread, masks, stack, weights, 3, depth)
     for block in range(planes):
         fine = 2 * (block % depth) + block // depth
         pre[0, fine] = values[block * CELLS : (block + 1) * CELLS]
@@ -886,39 +956,38 @@
     for flag, rim, plane in ((first, below, 0), (last, above, planes + 1)):
         values = norm_silu(rim[0], stats_in, scale)
         spread_fine(spread, plane, 1, 0, at_edge(flag, values, jnp.zeros_like(values)))
-    stack_fine(spread, masks, stack, 1, depth)
-    values = apply_weights(stack, weights, planes * CELLS, depth * CELLS)
+    values = forward_products(spread, masks, stack, weights, 1, depth)
     for block in range(planes):
         fine = 2 * (block % depth) + block // depth
         pre[0, fine] = values[block * CELLS : (block + 1) * CELLS]
     stats[0, 0:1], stats[0, 1:2] = moments_of(values)
 
 
-def to_voxels(out, planes, order, parts):
+def to_voxels(out, planes):
     count = len(planes)
-    total = None
-    for part in range(parts):
-        blocks = []
+    order = voxel_order()
+    stacked = []
+    for block in range(CELLS // GROUP):
+        lines = slice(block * GROUP, (block + 1) * GROUP)
         for phase in range(4):
-            pieces = [values[:, phase * GROUP : (phase + 1) * GROUP] for values in planes]
-            blocks.append(jnp.concatenate(pieces, axis=1).astype(BF16))
-        stacked = jnp.concatenate(blocks, axis=0)
-        stacked = lax.dot_general(
-            stacked, plane_order(count), (((1,), (1,)), ((), ())), preferred_element_type=F32
-        ).astype(BF16)
-        term = jnp.dot(order[...], stacked, preferred_element_type=F32)
-        total = term if total is None else total + term
-        if part + 1 < parts:
-            planes = [values - values.astype(BF16).astype(F32) for values in planes]
-    out[0] = total.T.reshape(GROUP, count, total.shape[0]).astype(out.dtype)
-
-
-def decoded_kernel(z, grad, stats_in, scales, decoded, sums, order):
+            pieces = [values[lines, phase * GROUP : (phase + 1) * GROUP] for values in planes]
+            stacked.append(jnp.concatenate(pieces, axis=1).astype(BF16))
+    turned = lax.dot_general(
+        plane_order(count),
+        jnp.concatenate(stacked, axis=0),
+        (((1,), (1,)), ((), ())),
+        preferred_element_type=F32,
+    ).astype(BF16)
+    blocks = [
+        jnp.dot(turned[:, block * FINE : (block + 1) * FINE], order, preferred_element_type=F32)
+        for block in range(CELLS // GROUP)
+    ]
+    total = jnp.concatenate(blocks, axis=1)
+    out[0] = total.reshape(GROUP, count, total.shape[1]).astype(out.dtype)
+
+
+def decoded_kernel(z, grad, stats_in, scales, decoded, sums):
     planes = z.shape[1]
-
-    @pl.when(pl.program_id(0) == 0)
-    def _():
-        order[...] = voxel_order(4 * CELLS, True)
 
     scale = segment(scales, 3)
     first, second, made = 0.0, 0.0, []
@@ -931,7 +1000,7 @@
         second = second + jnp.sum(upstream * normed, axis=0, keepdims=True)
     sums[0, 0:1] = first
     sums[0, 1:2] = second
-    to_voxels(decoded, made, order, 1)
+    to_voxels(decoded, made)
 
 
 def closing_back_kernel(
@@ -985,17 +1054,18 @@
     ):
         values = rounded(rim[0], rim_grad[0])
         spread_fine(spread, plane, 1, 0, at_edge(flag, values, jnp.zeros_like(values)))
-    stack_fine(spread, masks, stack, 1, depth)
     unit = identity(FINE)
     for block in range(planes):
         fine = 2 * (block % depth) + block // depth
         turned[:, block * CELLS : (block + 1) * CELLS] = transposed(out[0, fine], unit)
-    for level in range(3):
-        begin = level * depth * CELLS
-        totals[level] += jnp.dot(
-            turned[...], stack[begin : begin + planes * CELLS], preferred_element_type=F32
-        )
-    given[...] = apply_weights(stack, weights, planes * CELLS, depth * CELLS)
+    terms = []
+
+    def product(level, rows):
+        terms.append(jnp.dot(stack[rows, :], weights[level], preferred_element_type=F32))
+        add_kernel_products(totals, turned, stack, level, rows, 1)
+
+    fine_products(spread, masks, stack, 1, depth, product)
+    given[...] = terms[0] + terms[1] + terms[2]
     first_sum, second_sum = 0.0, 0.0
     for block in range(planes):
         fine = 2 * (block % depth) + block // depth
@@ -1036,7 +1106,9 @@
     for group in range(3):
         total = None
         for phase in range(4):
-            row = group * FINE + phase * GROUP
+            row = phase * GROUP
+            if group > 0:
+                row = (1 + phase // 2) * FINE + (2 * group - 2 + phase % 2) * GROUP
             block = jnp.where(lanes == phase, sums[row : row + GROUP], 0.0)
             total = block if total is None else total + block
         pieces.append(total)
@@ -1106,35 +1178,31 @@
     ):
         values = rounded(rim[0], rim_grad[0])
         spread_fine(spread, plane, 1, 0, at_edge(flag, values, jnp.zeros_like(values)))
-    stack_fine(spread, masks, stack, 1, depth)
     unit = identity(FINE)
-    for block in range(planes):
-        fine = 2 * (block % depth) + block // depth
+    width = 2 * GROUP
+    order = [2 * (block % depth) + block // depth for block in range(planes)]
+    for block, fine in enumerate(order):
         lines = slice(block * CELLS, (block + 1) * CELLS)
-        turned[:FINE, lines] = transposed(attended[0, fine], unit)
-        turned[FINE : 2 * FINE, lines] = transposed(upsampled[0, fine, :, :FINE], unit)
-        turned[2 * FINE : 3 * FINE, lines] = transposed(upsampled[0, fine, :, FINE:], unit)
+        for group in range(3):
+            source = attended[0, fine] if group == 0 else None
+            if source is None:
+                source = upsampled[0, fine, :, (group - 1) * FINE : group * FINE]
+            flat = transposed(source, unit)
+            turned[group * width : (group + 1) * width, lines] = flat[:width]
+            turned[(3 + group) * width : (4 + group) * width, lines] = flat[width:]
         turned[3 * FINE :, lines] = transposed(skip[0, fine], unit)
-    for level in range(3):
-        begin = level * depth * CELLS
-        for group in range(3):
-            totals[level, group * FINE : (group + 1) * FINE] += jnp.dot(
-                turned[group * FINE : (group + 1) * FINE],
-                stack[begin : begin + planes * CELLS],
-                preferred_element_type=F32,
-            )
-    for group in range(3):
-        columns = slice(group * FINE, (group + 1) * FINE)
-        total = None
-        for level in range(3):
-            begin = level * depth * CELLS
-            term = jnp.dot(
-                stack[begin : begin + planes * CELLS],
-                weights[level, :, columns],
-                preferred_element_type=F32,
-            )
-            total = term if total is None else total + term
-        given[:, columns] = total
+    dot = functools.partial(jnp.dot, preferred_element_type=F32)
+    parts = ((0, 3 * FINE, 0), (FINE, 4 * FINE, FINE), (0, 4 * FINE, 2 * FINE))
+
+    def product(level, rows):
+        for begin, end, column in parts:
+            term = dot(stack[rows, begin:end], weights[level, begin:end, column : column + FINE])
+            if level > 0:
+                term = given[:, column : column + FINE] + term
+            given[:, column : column + FINE] = term
+        add_kernel_products(totals, turned, stack, level, rows, 3)
+
+    fine_products(spread, masks, stack, 1, depth, product)
     gate_rows = gate_lines(gating)
     span = gate_rows.shape[1]
     part = span // 4
@@ -1146,37 +1214,36 @@
 
     to_lanes, to_span = ones(span, FINE, part, GROUP), ones(span, span, part, part)
     from_lanes = ones(FINE, span, GROUP, part)
-    low = lane_is_low((CELLS, 2 * GROUP))
-    column = row_column((CELLS, 2 * GROUP))
+    low = lane_is_low((CELLS, width))
+    column = row_column((CELLS, width))
     contract = (((1,), (1,)), ((), ()))
-    for block in range(planes):
-        fine = 2 * (block % depth) + block // depth
+    features = jnp.concatenate([skip[0, fine] for fine in order], axis=0)
+    asked = jnp.concatenate([query[0, fine] for fine in order], axis=0)
+    active = silu(asked)
+    high, rest = two_parts(active * gate_rows[1:2])
+    attention = jax.nn.sigmoid(dot(high, to_lanes) + dot(rest, to_lanes))
+    attention_span = jax.nn.sigmoid(dot(high, to_span) + dot(rest, to_span))
+    attended_back = jnp.concatenate([given[:, :width], given[:, FINE : FINE + width]], axis=1)
+    attention_back = dot_exact(attended_back * features.astype(F32), from_lanes)
+    logit_back = attention_back * attention_span * (1.0 - attention_span)
+    query_back = (logit_back * gate_rows[1:2] * silu_slope(asked)).astype(BF16)
+    gate_sums[3 * FINE : 3 * FINE + 1] += jnp.sum(query_back.astype(F32), axis=0, keepdims=True)
+    gate_sums[3 * FINE + 1 : 3 * FINE + 2] += jnp.sum(logit_back * active, axis=0, keepdims=True)
+    gate_sums[:FINE] += dot(turned[3 * FINE :], query_back)
+    for parity in range(2):
+        begin = (3 * parity + 1) * width
+        gate_sums[(1 + parity) * FINE : (2 + parity) * FINE] += dot(
+            turned[begin : begin + FINE], query_back
+        )
+    through_gate = lax.dot_general(query_back, gates[...], contract, preferred_element_type=F32)
+    skip_part = attended_back * attention + through_gate[:, :FINE]
+    for block, fine in enumerate(order):
         lines = slice(block * CELLS, (block + 1) * CELLS)
-        features = skip[0, fine]
-        asked = query[0, fine]
-        active = silu(asked)
-        high, rest = two_parts(active * gate_rows[1:2])
-        dot = functools.partial(jnp.dot, preferred_element_type=F32)
-        attention = jax.nn.sigmoid(dot(high, to_lanes) + dot(rest, to_lanes))
-        attention_span = jax.nn.sigmoid(dot(high, to_span) + dot(rest, to_span))
-        attended_back = given[lines, :FINE]
-        attention_back = dot_exact(attended_back * features.astype(F32), from_lanes)
-        logit_back = attention_back * attention_span * (1.0 - attention_span)
-        query_back = (logit_back * gate_rows[1:2] * silu_slope(asked)).astype(BF16)
-        psi = jnp.sum(logit_back * active, axis=0, keepdims=True)
-        bias = jnp.sum(query_back.astype(F32), axis=0, keepdims=True)
-        gate_sums[:FINE] += dot(turned[3 * FINE :, lines], query_back)
-        gate_sums[FINE : 3 * FINE] += dot(turned[FINE : 3 * FINE, lines], query_back)
-        gate_sums[3 * FINE : 3 * FINE + 1] += bias
-        gate_sums[3 * FINE + 1 : 3 * FINE + 2] += psi
-        skip_back[0, fine] = attended_back * attention + lax.dot_general(
-            query_back, gates[:FINE], contract, preferred_element_type=F32
-        )
-        up = given[lines, FINE:] + lax.dot_general(
-            query_back, gates[FINE:], contract, preferred_element_type=F32
-        )
-        left = narrowed(up[:, :FINE], low, column)
-        right = narrowed(up[:, FINE:], low, column)
+        skip_back[0, fine] = skip_part[lines]
+        left = jnp.concatenate([given[lines, width:FINE], given[lines, FINE + width : 2 * FINE]], axis=1)
+        left = narrowed(left + through_gate[lines, FINE : 2 * FINE], low, column)
+        right = given[lines, 2 * FINE :] + through_gate[lines, 2 * FINE :]
+        right = narrowed(right, low, column)
         coarse_back[0, fine] = jnp.where(low, left, right)
 
     @pl.when(step == pl.num_programs(0) - 1)
@@ -1317,7 +1384,6 @@
     stack,
     weights,
     totals,
-    order,
 ):
     depth = z.shape[1]
     step = pl.program_id(0)
@@ -1327,7 +1393,6 @@
         zero_rims(spread)
         coarse_weights(weights, kernel, 2, "flipped")
         totals[...] = jnp.zeros(totals.shape, F32)
-        order[...] = voxel_order(4 * CELLS, True)
 
     scale = segment(scales, 0)
     coarse_stack(
@@ -1356,7 +1421,7 @@
         values = jnp.concatenate([values] * 4, axis=1)
         for parity in range(2):
             made.append(skip_back[0, 2 * plane + parity] + values)
-    to_voxels(skip_grad, made, order, 2)
+    to_voxels(skip_grad, made)
 
     @pl.when(step == pl.num_programs(0) - 1)
     def _():
@@ -1467,6 +1532,45 @@
 def constant(array):
     zeros = (0,) * len(array.shape)
     return pl.BlockSpec(array.shape, lambda p: zeros)
+
+
+def run_with_stats(
+    kernel, patches, inputs, outputs, scratch, stats_at, rims_of, moments, samples, number
+):
+    plan = stats_plan()
+    ndep, low, high = plan
+    width = outputs[stats_at][0].shape[-1]
+    rest = [output for index, output in enumerate(outputs) if index != stats_at]
+    rims = None if rims_of is None else rest[rims_of][0]
+    shapes = [array for array, _ in rest] + [shape(8, width)]
+    specs = [by_patch(array) if spec is None else spec for array, spec in rest]
+    specs.append(constant(shapes[-1]))
+    extra = [
+        vmem(1, 8, width, dtype=F32),
+        vmem(patches, 8, width, dtype=F32),
+        vmem(low * ndep, 2, width, dtype=F32),
+        vmem(high, 2, width, dtype=F32),
+        pltpu.SemaphoreType.DMA((2 * (low * ndep + high),)),
+    ]
+    if rims is not None:
+        shapes += rim_shapes([rims])
+        specs += [pl.BlockSpec(memory_space=pl.ANY)] * 2
+        extra.append(vmem(patches, 2, *rims.shape[2:], dtype=rims.dtype))
+        extra.append(pltpu.SemaphoreType.DMA((4,)))
+    counts = (len(inputs), len(outputs), len(scratch))
+    return pl.pallas_call(
+        functools.partial(
+            with_stats, kernel, plan, moments, float(samples), counts, stats_at, rims_of
+        ),
+        grid=(patches,),
+        out_shape=shapes,
+        in_specs=[by_patch(array) if spec is None else spec for array, spec in inputs],
+        out_specs=specs,
+        scratch_shapes=list(scratch) + extra,
+        compiler_params=params(
+            dimension_semantics=("arbitrary",), collective_id=number, has_side_effects=True
+        ),
+    )(*[array for array, _ in inputs])
 
 
 def vmem(*sizes, dtype=BF16):
@@ -1514,7 +1618,7 @@
         patches,
         [(skip_features, None), (output_grad, None), (volume_ids, None)],
         [(fine_low, None), (fine_low, None), (coarse_low, None), (coarse_low, None)],
-        [vmem(4 * CELLS, 4 * CELLS)],
+        [],
     )
     (
         skip_below,
@@ -1533,7 +1637,7 @@
     coarse_spread = lambda groups: vmem(depth + 2, PADDED, groups * FINE)
     coarse_stacked = lambda groups: vmem(3 * depth * CELLS, groups * 3 * FINE)
 
-    z_one, stats_one, masks = run(
+    z_one, masks, norm_one, below_one, above_one = run_with_stats(
         first_kernel,
         patches,
         [
@@ -1552,12 +1656,14 @@
             vmem(3, 3 * FINE, 2 * GROUP),
             vmem(depth + 2, CELLS + 4 * RIM, 2 * GROUP, dtype=F32),
         ],
+        1,
+        0,
+        True,
+        depth * CELLS,
+        2,
     )
     masked = (masks, mask_spec(masks))
-    norm_one, below_one, above_one = all_reduce_stats(
-        stats_one, True, depth * CELLS, [z_one], 2
-    )
-    z_two, out_one, stats_two = run(
+    z_two, out_one, norm_two, below_two, above_two = run_with_stats(
         second_kernel,
         patches,
         [
@@ -1571,11 +1677,13 @@
         ],
         [(coarse, None), (coarse_low, None), (stats_coarse, None)],
         [coarse_spread(2), coarse_stacked(2), vmem(3, 6 * FINE, 2 * GROUP)],
+        2,
+        0,
+        True,
+        depth * CELLS,
+        3,
     )
-    norm_two, below_two, above_two = all_reduce_stats(
-        stats_two, True, depth * CELLS, [z_two], 3
-    )
-    z_three, attended, upsampled, query, stats_three = run(
+    z_three, attended, upsampled, query, norm_three, below_three, above_three = run_with_stats(
         third_kernel,
         patches,
         [
@@ -1605,11 +1713,13 @@
             vmem(3, 12 * FINE, FINE),
             vmem(3 * FINE, span),
         ],
+        4,
+        0,
+        True,
+        planes * CELLS,
+        4,
     )
-    norm_three, below_three, above_three = all_reduce_stats(
-        stats_three, True, planes * CELLS, [z_three], 4
-    )
-    z_four, out_three, stats_four = run(
+    z_four, out_three, norm_four, below_four, above_four = run_with_stats(
         fourth_kernel,
         patches,
         [
@@ -1623,21 +1733,27 @@
         ],
         [(fine, None), (fine_low, None), (stats_fine, None)],
         [fine_spread(1), fine_stack(1), vmem(3, 4 * FINE, FINE)],
+        2,
+        0,
+        True,
+        planes * CELLS,
+        5,
     )
-    norm_four, below_four, above_four = all_reduce_stats(
-        stats_four, True, planes * CELLS, [z_four], 5
-    )
-
-    decoded, partial_four = run(
+
+    decoded, sums_four = run_with_stats(
         decoded_kernel,
         patches,
         [(z_four, None), (grad, None), (norm_four, WHOLE), (scales, WHOLE)],
         [(shape(*skip_features.shape, dtype=BF16), None), (stats_fine, None)],
-        [vmem(4 * CELLS, 4 * CELLS)],
+        [],
+        1,
+        None,
+        False,
+        planes * CELLS,
+        6,
     )
-    (sums_four,) = all_reduce_stats(partial_four, False, planes * CELLS, [], 6)
     closing_shape = shape(*closing.shape, dtype=BF16)
-    back_three, partial_three, closing_grad = run(
+    back_three, closing_grad, sums_three, back_below, back_above = run_with_stats(
         closing_back_kernel,
         patches,
         [
@@ -1662,12 +1778,14 @@
             fine_stack(1),
             vmem(3, 4 * FINE, FINE),
             vmem(FINE, planes * CELLS),
-            vmem(3, FINE, 4 * FINE, dtype=F32),
+            vmem(3, 2, 2 * GROUP, 3 * FINE, dtype=F32),
             vmem(planes * CELLS, FINE, dtype=F32),
         ],
-    )
-    sums_three, back_below, back_above = all_reduce_stats(
-        partial_three, False, planes * CELLS, [back_three], 7
+        1,
+        0,
+        False,
+        planes * CELLS,
+        7,
     )
     merging_shape = shape(*merging_turned.shape, dtype=BF16)
     gate_shape = shape(2 * inner, 2 * GROUP, dtype=BF16)
@@ -1703,14 +1821,14 @@
             fine_stack(1),
             vmem(3, 4 * FINE, 3 * FINE),
             vmem(4 * FINE, planes * CELLS),
-            vmem(3, 3 * FINE, 4 * FINE, dtype=F32),
+            vmem(3, 2, 6 * GROUP, 3 * FINE, dtype=F32),
             vmem(planes * CELLS, 3 * FINE, dtype=F32),
             vmem(3 * FINE, span),
             vmem(3 * FINE + 8, span, dtype=F32),
         ],
     )
     fine_below, fine_above = exchange_rims([fine_back], 8)
-    back_two, partial_two = run(
+    back_two, sums_two, back_below, back_above = run_with_stats(
         coarse_grad_kernel,
         patches,
         [
@@ -1723,12 +1841,14 @@
         ],
         [(coarse, None), (stats_coarse, None)],
         [],
-    )
-    sums_two, back_below, back_above = all_reduce_stats(
-        partial_two, False, depth * CELLS, [back_two], 9
+        1,
+        0,
+        False,
+        depth * CELLS,
+        9,
     )
     bottom_shape = shape(*bottom.shape, dtype=BF16)
-    back_one, partial_one, bottom_grad = run(
+    back_one, bottom_grad, sums_one, back_below, back_above = run_with_stats(
         bottom_back_kernel,
         patches,
         [
@@ -1754,9 +1874,11 @@
             vmem(3, 6 * FINE, 2 * GROUP),
             vmem(3, 2 * GROUP, 6 * FINE, dtype=F32),
         ],
-    )
-    sums_one, back_below, back_above = all_reduce_stats(
-        partial_one, False, depth * CELLS, [back_one], 10
+        1,
+        0,
+        False,
+        depth * CELLS,
+        10,
     )
     widening_shape = shape(*widening.shape, dtype=BF16)
     skip_grad, widening_grad = run(
@@ -1786,7 +1908,6 @@
             coarse_stacked(2),
             vmem(3, 6 * FINE, GROUP),
             vmem(3, GROUP, 6 * FINE, dtype=F32),
-            vmem(4 * CELLS, 4 * CELLS),
         ],
     )
 

time: 415 us -> 363 us (0.87)
  Pallas kernels: 401 us -> 349 us
    pallas_call x11 -> x3, Pallas kernels: 249 us -> 85.7 us  [run(): pl.pallas_call(kernel, grid=(patches,), out_shape=[array for array, _ in...]
    pallas_call x8, Pallas kernels: 84.1 us -> 194 us  [run_with_stats(): pl.pallas_call(functools.partial(with_stats, kernel, plan, moments, float...]
where the time goes in v3:
time: 363 us; the launch traced here: 358 us
  Pallas kernels  349 us (96%)
  local copies, waits for them, and re-layouts  7.59 us (2%)
    pallas_call x8, Pallas kernels, run_with_stats(): pl.pallas_call(functools.partial(with_stats, kernel, plan, moments, float...  194 us
    pallas_call x3, Pallas kernels, run(): pl.pallas_call(kernel, grid=(patches,), out_shape=[array for array, _ in...  85.7 us
    pallas_call x1, Pallas kernels, all_reduce_grads(): pl.pallas_call(functools.partial(grads_kernel, plan, unit), out_shape=jax...  43.9 us
    pallas_call x1, Pallas kernels, update(): pl.pallas_call(update_kernel, grid=(steps,), out_shape=outs, in_specs=[WH...  18.7 us

profile of v3, /device:TPU:0, one launch (start us, length us, event | category | flops | bytes accessed | tf_op | source)
XLA Modules:
  0.0 357.7 jit_solution(5540877883942245637)
XLA Ops:
  0.7 1.5 copy.47.refs_8_.gating
  2.2 6.8 %shard_map.404 = (bf16[4,4,256,256]{3,2,1,0:T(8,128)(2,1)}, bf16[4,4,256,256]{3,2,1,0:T(8,128)(2,1)}, bf16[4,2,256,128]{3,2,1,0:T(8,128)(2,1)}, bf16[4,2,256,128]{3,2,1,0:T(8,128)(2,1)}) custom-call(bf16[4,64,4,1024]{3,2,1,0:T(4,128)(2,1)} %skip.1, bf16[4,64,4,1024]{3,2,1,0:T(4,128)(2,1)} %grad.1, s32[4,4,1024]{2,1,0:T(4,128)} %ids.1), custom_call_target="tpu_custom_call" | custom-call | tf_op jit(solution)/shard_map/pallas_call | solution.py:1521
  9.0 4.0 %shard_map.405 = (bf16[4,256,256]{2,1,0:T(8,128)(2,1)}, bf16[4,256,256]{2,1,0:T(8,128)(2,1)}, bf16[4,256,256]{2,1,0:T(8,128)(2,1)}, bf16[4,256,256]{2,1,0:T(8,12...) custom-call(bf16[4,4,256,256]{3,2,1,0:T(8,128)(2,1)} %get-tuple-elem, ...), custom_call_target="tpu_custom_call" | custom-call | tf_op jit(solution)/shard_map/pallas_call | solution.py:127
  13.0 20.1 %shard_map.406 = (f32[4,2,256,128]{3,2,1,0:T(8,128)}, bf16[9,4,512,256]{3,2,1,0:T(8,128)(2,1)}, f32[8,128]{1,0:T(8,128)}, f32[4,256,128]{2,1,0:T(8,128)}, f32[4,256,128]{2,1,0:T(8,128)}) custom-call(bf16[4,2,256,128]{3,2,1,0:T(8,128)(2,1)} %get-tuple-element.108.refs_2_.refs_0_.pooled, bf16[4,256,128]{2,1,0:T(8,128)(2,1)} %get-tuple-element.112.refs_1_, ...), custom_call_target="tpu_custom_call" | custom-call | tf_op jit(solution)/shard_map/pallas_call | solution.py:1561
  33.1 15.6 %shard_map.407 = (f32[4,2,256,128]{3,2,1,0:T(8,128)}, bf16[4,2,256,128]{3,2,1,0:T(8,128)(2,1)}, f32[8,128]{1,0:T(8,128)}, f32[4,256,128]{2,1,0:T(8,128)}, f32[4,256,128]{2,1,0:T(8,128)}) custom-call(f32[4,2,256,128]{3,2,1,0:T(8,128)} %get-tuple-element.116.refs_0_.refs_10_.z, f32[4,256,128]{2,1,0:T(8,128)} %get-tuple-element.117.refs_1_.below, ...), custom_call_target="tpu_custom_call" | custom-call | tf_op jit(solution)/shard_map/pallas_call | solution.py:1561
  48.7 56.5 %shard_map.408 = (f32[4,4,256,256]{3,2,1,0:T(8,128)}, bf16[4,4,256,256]{3,2,1,0:T(8,128)(2,1)}, bf16[4,4,256,512]{3,2,1,0:T(8,128)(2,1)}, f32[4,4,256,128]{3,2,1...) custom-call(f32[4,2,256,128]{3,2,1,0:T(8,128)} %get-tuple-element.121.refs_0_.refs_3_, ...), custom_call_target="tpu_custom_call" | custom-call | tf_op jit(solution)/shard_map/pallas_call | solution.py:1561
  105.2 21.1 %shard_map.409 = (f32[4,4,256,256]{3,2,1,0:T(8,128)}, bf16[4,4,256,256]{3,2,1,0:T(8,128)(2,1)}, f32[8,256]{1,0:T(8,128)}, f32[4,256,256]{2,1,0:T(8,128)}, f32[4,256,256]{2,1,0:T(8,128)}) custom-call(f32[4,4,256,256]{3,2,1,0:T(8,128)} %get-tuple-element.127.refs_0_.refs_10_.z, f32[4,256,256]{2,1,0:T(8,128)} %get-tuple-element.128.refs_1_.below, ...), custom_call_target="tpu_custom_call" | custom-call | tf_op jit(solution)/shard_map/pallas_call | solution.py:1561
  126.3 16.4 %shard_map.410 = (bf16[4,64,4,1024]{3,2,1,0:T(4,128)(2,1)}, f32[8,256]{1,0:T(8,128)}) custom-call(f32[4,4,256,256]{3,2,1,0:T(8,128)} %get-tuple-element.131.refs_0_, bf16[4,4,256,256]{3,2,1,0:T(8,128)(2,1)} %get-tuple-element.110.refs_1_.refs_3_, f32[8,256]{1,0:T(8,128)} %get-tuple-element.132.refs_2_.refs_6_, f32[2,384]{1,0:T(2,128)} %refs_15_.1), custom_call_target="tpu_custom_call" | custom-call | tf_op jit(solution)/shard_map/pallas_call | solution.py:1561
  142.7 29.7 %shard_map.411 = (f32[4,4,256,256]{3,2,1,0:T(8,128)}, bf16[27,64,64]{2,1,0:T(8,128)(2,1)}, f32[8,256]{1,0:T(8,128)}, f32[4,256,256]{2,1,0:T(8,128)}, f32[4,256,256]{2,1,0:T(8,128)}) custom-call(f32[4,4,256,256]{3,2,1,0:T(8,128)} %get-tuple-element.131.refs_0_, f32[4,256,256]{2,1,0:T(8,128)} %get-tuple-element.134.refs_1_, ...), custom_call_target="tpu_custom_call" | custom-call | tf_op jit(solution)/shard_map/pallas_call | solution.py:1561
  172.5 0.0 copy-start.3
  172.5 58.8 %shard_map.412 = (f32[4,4,256,256]{3,2,1,0:T(8,128)}, f32[4,4,256,128]{3,2,1,0:T(8,128)}, bf16[27,64,192]{2,1,0:T(8,128)(2,1)}, bf16[64,128]{1,0:T(8,128)(2,1)}) custom-call(f32[4,4,256,256]{3,2,1,0:T(8,128)} %get-tuple-element.140.grad, f32[4,256,256]{2,1,0:T(8,128)} %get-tuple-element.141.grad_below, f32[4,256,256]{2,1,0:T(8,128)} %get-tuple-element.142.grad_above, ...), custom_call_target="tpu_custom_call" | custom-call | tf_op jit(solution)/shard_map/pallas_call | solution.py:1521
  231.2 1.0 slice.7
  232.3 1.0 slice.6
  233.3 0.0 copy-done.3
  233.3 0.2 pad_maximum_fusion
  233.6 2.3 shard_map.413
  235.9 13.4 %shard_map.414 = (f32[4,2,256,128]{3,2,1,0:T(8,128)}, f32[8,128]{1,0:T(8,128)}, f32[4,256,128]{2,1,0:T(8,128)}, f32[4,256,128]{2,1,0:T(8,128)}) custom-call(f32[4,4,256,128]{3,2,1,0:T(8,128)} %get-tuple-element.147.refs_0_, f32[4,256,128]{2,1,0:T(8,128)} %get-tuple-element.148.refs_1_, f32[4,256,128]{2,1,0:T(8,128)} %get-tuple-element.149.refs_2_, ...), custom_call_target="tpu_custom_call" | custom-call | tf_op jit(solution)/shard_map/pallas_call | solution.py:1561
  249.3 21.2 %shard_map.415 = (f32[4,2,256,128]{3,2,1,0:T(8,128)}, bf16[27,128,128]{2,1,0:T(8,128)(2,1)}, f32[8,128]{1,0:T(8,128)}, f32[4,256,128]{2,1,0:T(8,128)}, f32[4,256,128]{2,1,0:T(8,128)}) custom-call(f32[4,2,256,128]{3,2,1,0:T(8,128)} %get-tuple-element.150.refs_0_, f32[4,256,128]{2,1,0:T(8,128)} %get-tuple-element.151.refs_1_, ...), custom_call_target="tpu_custom_call" | custom-call | tf_op jit(solution)/shard_map/pallas_call | solution.py:1561
  270.5 0.0 copy-start.2
  270.6 20.2 %shard_map.416 = (f32[4,64,4,1024]{3,2,1,0:T(4,128)}, bf16[27,64,128]{2,1,0:T(8,128)(2,1)}) custom-call(f32[4,2,256,128]{3,2,1,0:T(8,128)} %get-tuple-element.155.grad, f32[4,256,128]{2,1,0:T(8,128)} %get-tuple-element.156.grad_below, f32[4,256,128]{2,1,0:T(8,128)} %get-tuple-element.157.grad_above, ...), custom_call_target="tpu_custom_call" | custom-call | tf_op jit(solution)/shard_map/pallas_call | solution.py:1521
  290.7 0.0 copy-start.4
  290.7 1.0 constant_dynamic-update-slice_fusion.4
  291.8 0.0 copy-done.2
  291.8 0.1 constant_dynamic-update-slice_fusion.3
  291.9 0.1 constant_dynamic-update-slice_fusion.2
  292.0 0.1 constant_dynamic-update-slice_fusion.1
  292.0 0.0 copy-done.4
  292.1 0.0 copy-start
  292.1 1.4 copy-done
  293.4 43.9 %shard_map.417.grads = bf16[8704,128]{1,0:T(8,128)(2,1)} custom-call(bf16[8704,128]{1,0:T(8,128)(2,1)} %copy-done), custom_call_target="tpu_custom_call" | custom-call | tf_op jit(solution)/shard_map/pallas_call | solution.py:381
  337.4 0.0 copy-start.1
  337.4 18.7 %shard_map.418 = (f32[27,64,128]{2,1,0:T(8,128)}, f32[27,128,128]{2,1,0:T(8,128)}, f32[27,64,192]{2,1,0:T(8,128)}, f32[27,64,64]{2,1,0:T(8,128)}, f32[32,194]{1,...) custom-call(bf16[8704,128]{1,0:T(8,128)(2,1)} %shard_map.417.grads, ...), custom_call_target="tpu_custom_call" | custom-call | tf_op jit(solution)/shard_map/pallas_call | solution.py:1489
  356.1 0.0 copy-done.1
  356.1 1.3 copy.54
  (1 shorter events, 0.0 us)
Async XLA Ops:
  172.5 60.9 %copy-start.3 = (bf16[27,64,64]{2,1,0:T(8,128)(2,1)S(1)}, bf16[27,64,64]{2,1,0:T(8,128)(2,1)}, u32[]{:S(2)}) copy-start(bf16[27,64,64]{2,1,0:T(8,128)(2,1)} %get-tuple-element.164) | copy-start | bytes 663556
  270.5 21.2 %copy-start.2 = (bf16[27,128,128]{2,1,0:T(8,128)(2,1)S(1)}, bf16[27,128,128]{2,1,0:T(8,128)(2,1)}, u32[]{:S(2)}) copy-start(bf16[27,128,128]{2,1,0:T(8,128)(2,1)} %get-tuple-element.162) | copy-start | bytes 2654212
  290.7 1.3 copy-start.4
  292.1 1.4 copy-start
  337.4 18.7 %copy-start.1 = (bf16[4,64,4,1024]{3,2,1,0:T(4,128)(2,1)S(1)}, bf16[4,64,4,1024]{3,2,1,0:T(4,128)(2,1)}, u32[]{:S(2)}) copy-start(bf16[4,64,4,1024]{3,2,1,0:T(4,128)(2,1)} %get-tuple-element.216) | copy-start | bytes 6291460

commit v4 on v3

--- a/solution.py
+++ b/solution.py
@@ -223,15 +223,21 @@
     result[3:4] = second
 
 
-def with_stats(kernel, plan, moments, samples, counts, stats_at, rims_of, *refs):
+def with_stats(kernel, plan, moments, samples, counts, stats_at, rims_of, beside, *refs):
     inputs, outputs, scratch = counts
     ins, refs = refs[:inputs], refs[inputs:]
+    if beside is not None:
+        make, hook_ins, hook_outs, hook_scratch = beside
+        hook_in, refs = refs[:hook_ins], refs[hook_ins:]
     outs, refs = list(refs[: outputs - 1]), refs[outputs - 1 :]
     result, refs = refs[0], refs[1:]
+    if beside is not None:
+        hook_out, refs = refs[:hook_outs], refs[hook_outs:]
     if rims_of is not None:
         below, above, refs = refs[0], refs[1], refs[2:]
     own, refs = refs[:scratch], refs[scratch:]
     stats, parts, near, far, sems = refs[:5]
+    refs = refs[5:]
     step = pl.program_id(0)
 
     @pl.when(step == 0)
@@ -243,149 +249,286 @@
     kernel(*ins, *outs, *own)
     parts[step] = stats[0]
     if rims_of is not None:
-        rims, rim_sems = refs[5:]
+        rims, rim_sems, refs = refs[0], refs[1], refs[2:]
         rims[step, 0] = source[0, 0]
         rims[step, 1] = source[0, source.shape[1] - 1]
 
+    if beside is not None:
+
+        @pl.when(step == 0)
+        def _():
+            await_greetings(plan)
+
+        actions, after = make(hook_in, hook_out, refs)
+        in_steps(step, parts.shape[0], actions)
+
     @pl.when(step == pl.num_programs(0) - 1)
     def _():
-        await_greetings(plan)
+        if beside is None:
+            await_greetings(plan)
         if rims_of is not None:
             start, finish = halo_steps([(rims, below, above)], rim_sems)
             start()
         sum_stats(plan, moments, samples, parts, result, near, far, sems)
         if rims_of is not None:
             finish()
-
-
-def grads_plan(units, ndep, low, high):
-    colours = min(4, units)
-    orders = [(0, 1, 2), (0, 2, 1), (0, 1, 2), (0, 1, 2)][:colours]
-    counts = [units // colours + (1 if index < units % colours else 0) for index in range(colours)]
-    sizes = (ndep, low, high)
-    return counts, orders, sizes
-
-
-def grads_kernel(plan, unit, source, result, held, *refs):
-    counts, orders, sizes = plan
-    colours, stages = len(counts), len(sizes)
-    arrivals, sems = refs[: colours * stages], refs[colours * stages]
-    mp, md = lax.axis_index("patch"), lax.axis_index("depth")
-    ndep, low, high = sizes
-    mine_low, mine_high = lax.rem(mp, low), mp // low
-    places = (md, mine_low, mine_high)
-    devices = (
-        lambda step: (mp, lax.rem(md + step, ndep)),
-        lambda step: (mine_high * low + lax.rem(mine_low + step, low), md),
-        lambda step: (lax.rem(mine_high + step, high) * low + mine_low, md),
-    )
-    barrier = pltpu.get_barrier_semaphore()
-    for stage in range(stages):
-        for step in range(1, sizes[stage]):
-            pl.semaphore_signal(
-                barrier, inc=1, device_id=devices[stage](step), device_id_type=MESH
-            )
-    pl.semaphore_wait(barrier, sum(sizes) - stages)
-    begins = [sum(counts[:index]) * unit for index in range(colours)]
-    lengths = [count * unit for count in counts]
-    used = [0]
-
-    def copy(origin, target, device):
-        send, receive = sems.at[used[0]], sems.at[used[0] + 1]
-        used[0] += 2
+        if beside is not None:
+            for action in after:
+                action()
+
+
+class GradSum:
+    def __init__(self, rows):
+        npat, ndep = lax.axis_size("patch"), lax.axis_size("depth")
+        low = 4 if npat % 4 == 0 else 1
+        self.sizes = (ndep, low, npat // low)
+        self.devices = npat * ndep
+        self.unit = 16 * self.devices
+        units = -(-rows // self.unit)
+        self.rows = units * self.unit
+        colours = min(4, units)
+        self.orders = [(0, 1, 2), (0, 2, 1), (0, 1, 2), (0, 1, 2)][:colours]
+        self.counts = [
+            units // colours + (1 if index < units % colours else 0) for index in range(colours)
+        ]
+        self.places, total = {}, 0
+        for colour, order in enumerate(self.orders):
+            for round_ in range(3):
+                self.places[colour, round_] = total
+                total += 2 * (self.sizes[order[round_]] - 1)
+        self.sems = total
+
+    def full(self):
+        return vmem(self.rows, 2 * GROUP)
+
+    def lengths(self, level):
+        result = []
+        for count, order in zip(self.counts, self.orders):
+            length = count * self.unit
+            for axis in order[:level]:
+                length //= self.sizes[axis]
+            result.append(length)
+        return result
+
+    def pieces(self, level):
+        return shape(sum(self.lengths(level)), 2 * GROUP, dtype=BF16)
+
+    def scatter_scratch(self):
+        scratch = [self.full()]
+        for count, order in zip(self.counts, self.orders):
+            length = count * self.unit
+            for axis in order:
+                length //= self.sizes[axis]
+                scratch.append(vmem(max(self.sizes[axis] - 1, 1), length, 2 * GROUP))
+        return scratch + [pltpu.SemaphoreType.DMA((self.sems,))]
+
+    def gather_scratch(self):
+        return [self.full(), pltpu.SemaphoreType.DMA((self.sems,))]
+
+    def device(self, axis, step):
+        ndep, low, high = self.sizes
+        mp, md = lax.axis_index("patch"), lax.axis_index("depth")
+        mine_low, mine_high = lax.rem(mp, low), mp // low
+        if axis == 0:
+            return (mp, lax.rem(md + step, ndep))
+        if axis == 1:
+            return (mine_high * low + lax.rem(mine_low + step, low), md)
+        return (lax.rem(mine_high + step, high) * low + mine_low, md)
+
+    def place(self, axis):
+        ndep, low, high = self.sizes
+        mp, md = lax.axis_index("patch"), lax.axis_index("depth")
+        return (md, lax.rem(mp, low), mp // low)[axis]
+
+    def region(self, colour, round_):
+        begin, length = sum(self.counts[:colour]) * self.unit, self.counts[colour] * self.unit
+        for axis in self.orders[colour][:round_]:
+            length //= self.sizes[axis]
+            begin = begin + self.place(axis) * length
+        return begin, length
+
+    def piece(self, colour, level):
+        begin, length = self.region(colour, level)
+        first = sum(self.lengths(level)[:colour])
+        return pl.ds(pl.multiple_of(begin, 16), length), slice(first, first + length)
+
+    def copy(self, origin, target, sems, colour, round_, step):
+        place = self.places[colour, round_] + 2 * (step - 1)
         return pltpu.make_async_remote_copy(
             src_ref=origin,
             dst_ref=target,
-            send_sem=send,
-            recv_sem=receive,
-            device_id=device,
+            send_sem=sems.at[place],
+            recv_sem=sems.at[place + 1],
+            device_id=self.device(self.orders[colour][round_], step),
             device_id_type=MESH,
         )
 
-    history = []
-    for round_ in range(stages):
-        started = []
+    def scatter_copies(self, refs, round_, colour):
+        source, held, arrivals, sems = refs[0], refs[1], refs[2:-1], refs[-1]
         origin = source if round_ == 0 else held
-        for colour in range(colours):
-            axis = orders[colour][round_]
-            size, piece = sizes[axis], lengths[colour] // sizes[axis]
-            arrival = arrivals[colour * stages + round_]
-            copies = []
-            for step in range(1, size):
-                begin = begins[colour] + lax.rem(places[axis] + step, size) * piece
-                begin = pl.multiple_of(begin, 16)
-                copies.append(
-                    copy(origin.at[pl.ds(begin, piece)], arrival.at[step - 1], devices[axis](step))
-                )
-                copies[-1].start()
-            started.append(copies)
-        history.append((list(begins), list(lengths)))
-        for colour in range(colours):
-            axis = orders[colour][round_]
-            size, piece = sizes[axis], lengths[colour] // sizes[axis]
-            arrival = arrivals[colour * stages + round_]
-            begin = pl.multiple_of(begins[colour] + places[axis] * piece, 16)
-            target = result if round_ == stages - 1 else held
-            for item in started[colour]:
-                item.wait_recv()
-            block = next(rows for rows in (128, 64, 48, 32, 16) if piece % rows == 0)
+        axis = self.orders[colour][round_]
+        begin, length = self.region(colour, round_)
+        piece = length // self.sizes[axis]
+        copies = []
+        for step in range(1, self.sizes[axis]):
+            other = lax.rem(self.place(axis) + step, self.sizes[axis])
+            rows = pl.ds(pl.multiple_of(begin + other * piece, 16), piece)
+            target = arrivals[3 * colour + round_].at[step - 1]
+            copies.append(self.copy(origin.at[rows], target, sems, colour, round_, step))
+        return copies
+
+    def scatter_start(self, refs, round_):
+        for colour in range(len(self.orders)):
+            for copy in self.scatter_copies(refs, round_, colour):
+                copy.start()
+
+    def scatter_finish(self, refs, round_):
+        source, held, arrivals = refs[0], refs[1], refs[2:-1]
+        origin = source if round_ == 0 else held
+        for colour in range(len(self.orders)):
+            copies = self.scatter_copies(refs, round_, colour)
+            for copy in copies:
+                copy.wait_recv()
+            begin, length = self.region(colour, round_ + 1)
+            arrival = arrivals[3 * colour + round_]
+            block = next(rows for rows in (128, 64, 48, 32, 16) if length % rows == 0)
+            others = self.sizes[self.orders[colour][round_]] - 1
 
             def add(index, carry):
                 row = pl.multiple_of(index * block, 16)
                 here = pl.ds(pl.multiple_of(begin + row, 16), block)
                 total = origin[here, :].astype(F32)
-                for other in range(size - 1):
+                for other in range(others):
                     total = total + arrival[other, pl.ds(row, block), :].astype(F32)
-                target[here, :] = total.astype(BF16)
+                held[here, :] = total.astype(BF16)
                 return carry
 
-            lax.fori_loop(0, piece // block, add, 0)
-            begins[colour], lengths[colour] = begin, piece
-        for copies in started:
-            for item in copies:
-                item.wait_send()
-    for round_ in reversed(range(stages)):
-        started = []
-        for colour in range(colours):
-            axis = orders[colour][round_]
-            rows = result.at[pl.ds(begins[colour], lengths[colour])]
-            for step in range(1, sizes[axis]):
-                started.append(copy(rows, rows, devices[axis](step)))
-                started[-1].start()
-        for item in started:
-            item.wait()
-        begins, lengths = history[round_]
-
-
-def all_reduce_grads(values, number):
-    npat, ndep = lax.axis_size("patch"), lax.axis_size("depth")
-    low = 4 if npat % 4 == 0 else 1
-    high = npat // low
-    unit = 16 * npat * ndep
-    rows = values.shape[0]
-    units = -(-rows // unit)
-    if units * unit > rows:
-        values = jnp.pad(values, ((0, units * unit - rows), (0, 0)))
-    plan = grads_plan(units, ndep, low, high)
-    counts, orders, sizes = plan
-    scratch = [pltpu.VMEM(values.shape, BF16)]
-    total = 0
-    for count, order in zip(counts, orders):
-        length = count * unit
-        for axis in order:
-            length //= sizes[axis]
-            scratch.append(pltpu.VMEM((max(sizes[axis] - 1, 1), length, 2 * GROUP), BF16))
-            total += 4 * (sizes[axis] - 1)
-    scratch.append(pltpu.SemaphoreType.DMA((total,)))
+            lax.fori_loop(0, length // block, add, 0)
+            for copy in copies:
+                copy.wait_send()
+
+    def gather_copies(self, refs, round_):
+        full, sems = refs
+        copies = []
+        for colour in range(len(self.orders)):
+            begin, length = self.region(colour, round_ + 1)
+            rows = full.at[pl.ds(pl.multiple_of(begin, 16), length)]
+            for step in range(1, self.sizes[self.orders[colour][round_]]):
+                copies.append(self.copy(rows, rows, sems, colour, round_, step))
+        return copies
+
+    def gather_start(self, refs, round_):
+        for copy in self.gather_copies(refs, round_):
+            copy.start()
+
+    def gather_finish(self, refs, round_):
+        for copy in self.gather_copies(refs, round_):
+            copy.wait()
+
+    def store_pieces(self, source, out, level):
+        for colour in range(len(self.orders)):
+            rows, lines = self.piece(colour, level)
+            out[lines, :] = source[rows, :]
+
+    def load_pieces(self, pieces, target, level):
+        for colour in range(len(self.orders)):
+            rows, lines = self.piece(colour, level)
+            target[rows, :] = pieces[lines, :]
+
+    def move_pieces(self, source, target, level):
+        for colour in range(len(self.orders)):
+            rows, _ = self.piece(colour, level)
+            target[rows, :] = source[rows, :]
+
+
+def last_sums_kernel(gathered, summed, pieces, source, first_out, second_out, *refs):
+    full, gather_sems, again_sems = refs[0], refs[1], refs[2]
+    scatter_refs = (source,) + refs[3:]
+    plan = stats_plan()
+    greet(plan)
+    gathered.load_pieces(pieces, full, 3)
+    await_greetings(plan)
+    first = (full, gather_sems)
+    second = (second_out, again_sems)
+    gathered.gather_start(first, 2)
+    summed.scatter_start(scatter_refs, 0)
+    summed.scatter_finish(scatter_refs, 0)
+    summed.scatter_start(scatter_refs, 1)
+    gathered.gather_finish(first, 2)
+    gathered.gather_start(first, 1)
+    summed.scatter_finish(scatter_refs, 1)
+    summed.scatter_start(scatter_refs, 2)
+    gathered.gather_finish(first, 1)
+    gathered.gather_start(first, 0)
+    summed.scatter_finish(scatter_refs, 2)
+    summed.move_pieces(scatter_refs[1], second_out, 3)
+    for round_ in (2, 1, 0):
+        summed.gather_start(second, round_)
+        summed.gather_finish(second, round_)
+    gathered.gather_finish(first, 0)
+    first_out[...] = full[...]
+
+
+def last_sums(gathered, pieces, summed, source, number):
     inside = pl.BlockSpec(memory_space=pltpu.VMEM)
     return pl.pallas_call(
-        functools.partial(grads_kernel, plan, unit),
-        out_shape=jax.ShapeDtypeStruct(values.shape, BF16),
-        in_specs=[inside],
-        out_specs=inside,
-        scratch_shapes=scratch,
+        functools.partial(last_sums_kernel, gathered, summed),
+        out_shape=[
+            shape(gathered.rows, 2 * GROUP, dtype=BF16),
+            shape(summed.rows, 2 * GROUP, dtype=BF16),
+        ],
+        in_specs=[inside] * 2,
+        out_specs=[inside] * 2,
+        scratch_shapes=gathered.gather_scratch()
+        + [pltpu.SemaphoreType.DMA((summed.sems,))]
+        + summed.scatter_scratch(),
         compiler_params=params(collective_id=number, has_side_effects=True),
-    )(values)
+    )(pieces, source)
+
+
+def in_steps(step, steps, actions):
+    for index in range(steps):
+        now = actions[index : index + 1] if index < steps - 1 else actions[index:]
+
+        @pl.when(step == index)
+        def _():
+            for group in now:
+                for action in group:
+                    action()
+
+
+def first_rounds(plan, ins, outs, scratch):
+    refs = (ins[0],) + tuple(scratch)
+    actions = [
+        [lambda: plan.scatter_start(refs, 0)],
+        [],
+        [],
+        [lambda: plan.scatter_finish(refs, 0), lambda: plan.scatter_start(refs, 1)],
+    ]
+    after = [
+        lambda: plan.scatter_finish(refs, 1),
+        lambda: plan.store_pieces(refs[1], outs[0], 2),
+    ]
+    return actions, after
+
+
+def middle_rounds(plan, ins, outs, scratch):
+    gather, refs = tuple(scratch[:2]), (None,) + tuple(scratch[2:])
+    actions = [
+        [lambda: plan.load_pieces(ins[0], refs[1], 2), lambda: plan.scatter_start(refs, 2)],
+        [
+            lambda: plan.scatter_finish(refs, 2),
+            lambda: plan.move_pieces(refs[1], gather[0], 3),
+            lambda: plan.gather_start(gather, 2),
+        ],
+        [lambda: plan.gather_finish(gather, 2), lambda: plan.gather_start(gather, 1)],
+        [],
+    ]
+    after = [
+        lambda: plan.gather_finish(gather, 1),
+        lambda: plan.store_pieces(gather[0], outs[0], 1),
+    ]
+    return actions, after
 
 
 def lane_is_low(shape):
@@ -456,33 +599,51 @@
     spread[:, RIM + CELLS :] = zeros
 
 
-def spread_pair(spread, plane, column, pair, turned, low):
-    before = jnp.where(low, pltpu.roll(turned, 1, 0), turned)
-    after = jnp.where(low, turned, pltpu.roll(turned, CELLS - 1, 0))
-    width = 2 * GROUP
-    spread[plane, pl.ds(RIM, CELLS), column : column + width] = before.astype(BF16)
-    spread[plane, pl.ds(RIM, CELLS), column + width : column + 2 * width] = after.astype(BF16)
-
-
-def spread_fine(spread, plane, groups, group, values):
-    width = 2 * GROUP
-    low = lane_is_low((CELLS, width))
-    for parity in range(2):
-        pair = values[:, parity * width : (parity + 1) * width]
-        turned = pltpu.roll(pair, GROUP, 1)
-        spread_pair(spread, plane, (parity * groups + group) * FINE, pair, turned, low)
-
-
-def spread_coarse(spread, plane, groups, values):
-    low = lane_is_low((CELLS, 2 * GROUP))
-    turned = pltpu.roll(values, GROUP, 1)
-    for group in range(groups):
-        one, other = (values, turned) if group == 0 else (turned, values)
-        before = jnp.where(low, pltpu.roll(one, 1, 0), other)
-        after = jnp.where(low, one, pltpu.roll(other, CELLS - 1, 0))
-        column = group * FINE
-        spread[plane, pl.ds(RIM, CELLS), column : column + 128] = before.astype(BF16)
-        spread[plane, pl.ds(RIM, CELLS), column + 128 : column + 256] = after.astype(BF16)
+def row_blocks(size):
+    return [slice(begin, begin + size) for begin in range(0, CELLS, size)]
+
+
+def spread_fine(spread, plane, groups, group, make):
+    width, block = 2 * GROUP, 2 * HALF_WIDTH
+    low = lane_is_low((block, width))
+    for rows in row_blocks(block):
+        values = make(rows)
+        lines = slice(RIM + rows.start, RIM + rows.stop)
+        for parity in range(2):
+            pair = values[:, parity * width : (parity + 1) * width]
+            turned = pltpu.roll(pair, GROUP, 1)
+            before = jnp.where(low, pltpu.roll(turned, 1, 0), turned)
+            after = jnp.where(low, turned, pltpu.roll(turned, block - 1, 0))
+            column = (parity * groups + group) * FINE
+            spread[plane, lines, column : column + width] = before.astype(BF16)
+            spread[plane, lines, column + width : column + 2 * width] = after.astype(BF16)
+
+
+def spread_coarse(spread, plane, groups, make):
+    block = 4 * HALF_WIDTH
+    low = lane_is_low((block, 2 * GROUP))
+    for rows in row_blocks(block):
+        values = make(rows)
+        lines = slice(RIM + rows.start, RIM + rows.stop)
+        turned = pltpu.roll(values, GROUP, 1)
+        for group in range(groups):
+            one, other = (values, turned) if group == 0 else (turned, values)
+            before = jnp.where(low, pltpu.roll(one, 1, 0), other)
+            after = jnp.where(low, one, pltpu.roll(other, block - 1, 0))
+            column = group * FINE
+            spread[plane, lines, column : column + 128] = before.astype(BF16)
+            spread[plane, lines, column + 128 : column + 256] = after.astype(BF16)
+
+
+def spread_rim(store, spread, plane, groups, flag, make):
+    def values(rows):
+        found = make(rows)
+        return at_edge(flag, found, jnp.zeros_like(found))
+
+    if store is spread_fine:
+        spread_fine(spread, plane, groups, 0, values)
+    else:
+        spread_coarse(spread, plane, groups, values)
 
 
 fine_rows = ((0, 1), (1, 0), (1, 1), (2, 0))
@@ -585,7 +746,15 @@
     lax.fori_loop(0, 3, fill, 0)
 
 
-def fine_kernel_grad(out, sums, groups, turn):
+def merging_rows(out, tap, blocks, closing):
+    taps = closing.shape[0]
+    row = pl.multiple_of(tap * GROUP, GROUP)
+    out[pl.ds(row, GROUP), :] = jnp.concatenate(blocks[:2], axis=1)
+    row = pl.multiple_of((taps + tap) * GROUP, GROUP)
+    out[pl.ds(row, GROUP), :] = jnp.concatenate([blocks[2], closing[tap]], axis=1)
+
+
+def fine_kernel_grad(out, sums, groups, closing=None):
     def fill(level, carry):
         for step in range(9):
             row_step, column_step = step // 3, step % 3
@@ -599,8 +768,11 @@
                     block = sums[level, phase // 2, row : row + GROUP, columns]
                     total = block if total is None else total + block
                 total = total.astype(BF16)
-                blocks.append(transposed(total, identity(GROUP)) if turn else total)
-            out[26 - (9 * level + step)] = jnp.concatenate(blocks, axis=1)
+                blocks.append(total if closing is None else transposed(total, identity(GROUP)))
+            if closing is None:
+                out[26 - (9 * level + step)] = jnp.concatenate(blocks, axis=1)
+            else:
+                merging_rows(out, 26 - (9 * level + step), blocks, closing)
         return carry
 
     lax.fori_loop(0, 3, fill, 0)
@@ -618,6 +790,9 @@
         return carry
 
     lax.fori_loop(0, 3, fill, 0)
+    rest = out.shape[0] - 27
+    if rest:
+        out[27:] = jnp.zeros((rest,) + out.shape[1:], BF16)
 
 
 def add_kernel_products(totals, turned, stack, level, rows, groups):
@@ -784,10 +959,9 @@
     first, last = edge_flags()
     fill_masks(masks, ids, (ids_below, ids_above), (first, last), names)
     for plane in range(depth):
-        spread_coarse(spread, plane + 1, 1, pooled[0, plane].astype(F32))
+        spread_coarse(spread, plane + 1, 1, lambda rows: pooled[0, plane, rows].astype(F32))
     for flag, rim, plane in ((first, below, 0), (last, above, depth + 1)):
-        values = rim[0].astype(F32)
-        spread_coarse(spread, plane, 1, at_edge(flag, values, jnp.zeros_like(values)))
+        spread_rim(spread_coarse, spread, plane, 1, flag, lambda rows: rim[0, rows].astype(F32))
     stack_coarse(spread, masks, stack, 1, depth)
     values = apply_weights(stack, weights, depth * CELLS, depth * CELLS)
     for plane in range(depth):
@@ -808,12 +982,16 @@
     scale = segment(scales, 0)
     first, last = edge_flags()
     for plane in range(depth):
-        values = norm_silu(z[0, plane], stats_in, scale)
-        out[0, plane] = values.astype(BF16)
-        spread_coarse(spread, plane + 1, 2, values)
+
+        def make(rows):
+            values = norm_silu(z[0, plane, rows], stats_in, scale)
+            out[0, plane, rows] = values.astype(BF16)
+            return values
+
+        spread_coarse(spread, plane + 1, 2, make)
     for flag, rim, plane in ((first, below, 0), (last, above, depth + 1)):
-        values = norm_silu(rim[0], stats_in, scale)
-        spread_coarse(spread, plane, 2, at_edge(flag, values, jnp.zeros_like(values)))
+        make = lambda rows: norm_silu(rim[0, rows], stats_in, scale)
+        spread_rim(spread_coarse, spread, plane, 2, flag, make)
     stack_coarse(spread, masks, stack, 2, depth)
     values = apply_weights(stack, weights, depth * CELLS, depth * CELLS)
     for plane in range(depth):
@@ -821,16 +999,14 @@
     stats[0, 0:1], stats[0, 1:2] = moments_of(values)
 
 
-def widened(values, low, column):
-    before = jnp.concatenate([values[:RIM], values[: CELLS - RIM]], axis=0)
-    after = jnp.concatenate([values[RIM:], values[CELLS - RIM :]], axis=0)
-    result = []
-    for beside in (before, after):
-        line = 0.75 * values + 0.25 * beside
-        left = jnp.where(column == 0, line, pltpu.roll(line, 1, 0))
-        right = jnp.where(column == HALF_WIDTH - 1, line, pltpu.roll(line, CELLS - 1, 0))
-        result.append((0.75 * line + 0.25 * left, 0.75 * line + 0.25 * right))
-    return result
+def widened(values, beside, column):
+    line = 0.75 * values + 0.25 * beside
+    left = jnp.where(column == 0, line, pltpu.roll(line, 1, 0))
+    right = jnp.where(column == HALF_WIDTH - 1, line, pltpu.roll(line, line.shape[0] - 1, 0))
+    most, least = 0.75 * line, 0.25 * line
+    slots = (0.75 * left + least, most + 0.25 * left, most + 0.25 * right, 0.75 * right + least)
+    plain = [slot.astype(BF16) for slot in slots]
+    return plain, [pltpu.roll(slot, GROUP, 1) for slot in plain]
 
 
 def third_kernel(
@@ -855,6 +1031,7 @@
     stack,
     weights,
     gates,
+    up,
 ):
     depth = z.shape[1]
     planes = 2 * depth
@@ -875,8 +1052,9 @@
         values = norm_silu(rim[0], stats_in, scale).astype(BF16).astype(F32)
         coarse[plane] = at_edge(flag, values, coarse[inner])
     gate_rows = gate_lines(gating)
-    low = lane_is_low((CELLS, width))
-    column = row_column((CELLS, width))
+    block = 2 * HALF_WIDTH
+    low = lane_is_low((block, width))
+    column = row_column((block, width))
     span = gate_rows.shape[1]
     spans = lax.broadcasted_iota(jnp.int32, (span, FINE), 0) // (span // 4)
     lanes = lax.broadcasted_iota(jnp.int32, (span, FINE), 1) // GROUP
@@ -887,22 +1065,34 @@
             fine = index - 1
             center = fine // 2
             other = center - 1 if fine % 2 == 0 else center + 1
-            doubled = 0.75 * coarse[center + 1] + 0.25 * coarse[other + 1]
-            grid = widened(doubled, low, column)
-            pieces = []
-            for group in range(2):
-                for parity in range(2):
-                    even, odd = grid[parity]
-                    if group == 0:
-                        pair = jnp.where(low, even, pltpu.roll(odd, GROUP, 1))
-                    else:
-                        pair = jnp.where(low, pltpu.roll(even, GROUP, 1), odd)
-                    pair = pair.astype(BF16)
-                    pieces.append(pair)
-                    pair = pair.astype(F32)
-                    turned = pltpu.roll(pair, GROUP, 1)
-                    spread_pair(spread, index, (parity * 3 + 1 + group) * FINE, pair, turned, low)
-            ups.append(jnp.concatenate(pieces, axis=1))
+            for rows in row_blocks(block):
+                begin, end = rows.start, rows.stop
+
+                def doubled(first_row, last_row):
+                    part = slice(first_row, last_row)
+                    return 0.75 * coarse[center + 1, part] + 0.25 * coarse[other + 1, part]
+
+                values = doubled(begin, end)
+                if begin == 0:
+                    before = jnp.concatenate([values[:RIM], values[: block - RIM]], axis=0)
+                else:
+                    before = doubled(begin - RIM, end - RIM)
+                if end == CELLS:
+                    after = jnp.concatenate([values[RIM:], values[block - RIM :]], axis=0)
+                else:
+                    after = doubled(begin + RIM, end + RIM)
+                lines = slice(RIM + begin, RIM + end)
+                for parity, beside in enumerate((before, after)):
+                    plain, turned = widened(values, beside, column)
+                    for group in range(2):
+                        one, two = (plain, turned) if group == 0 else (turned, plain)
+                        pick = lambda left, right: jnp.where(low, one[left], two[right])
+                        place = (2 * group + parity) * width
+                        up[index, rows, place : place + width] = pick(1, 2)
+                        place = (parity * 3 + 1 + group) * FINE
+                        spread[index, lines, place : place + width] = pick(0, 1)
+                        spread[index, lines, place + width : place + 2 * width] = pick(2, 3)
+            ups.append(up[index])
             if fine < 0:
                 features = at_edge(first, skip_below[0].astype(F32), 0.0).astype(BF16)
             elif fine == planes:
@@ -921,7 +1111,8 @@
         for place, index in enumerate(indices):
             fine = index - 1
             lines = slice(place * CELLS, (place + 1) * CELLS)
-            spread_fine(spread, index, 3, 0, kept[lines].astype(F32))
+            here = kept[lines]
+            spread_fine(spread, index, 3, 0, lambda rows: here[rows].astype(F32))
             if 0 <= fine < planes:
                 attended[0, fine] = kept[lines]
                 upsampled[0, fine] = ups[place]
@@ -950,12 +1141,16 @@
     scale = segment(scales, 2)
     first, last = edge_flags()
     for plane in range(planes):
-        values = norm_silu(z[0, plane], stats_in, scale)
-        out[0, plane] = values.astype(BF16)
-        spread_fine(spread, plane + 1, 1, 0, values)
+
+        def make(rows):
+            values = norm_silu(z[0, plane, rows], stats_in, scale)
+            out[0, plane, rows] = values.astype(BF16)
+            return values
+
+        spread_fine(spread, plane + 1, 1, 0, make)
     for flag, rim, plane in ((first, below, 0), (last, above, planes + 1)):
-        values = norm_silu(rim[0], stats_in, scale)
-        spread_fine(spread, plane, 1, 0, at_edge(flag, values, jnp.zeros_like(values)))
+        make = lambda rows: norm_silu(rim[0, rows], stats_in, scale)
+        spread_rim(spread_fine, spread, plane, 1, flag, make)
     values = forward_products(spread, masks, stack, weights, 1, depth)
     for block in range(planes):
         fine = 2 * (block % depth) + block // depth
@@ -992,12 +1187,16 @@
     scale = segment(scales, 3)
     first, second, made = 0.0, 0.0, []
     for plane in range(planes):
-        normed = normalize(z[0, plane], stats_in)
-        active = normed * scale[0:1] + scale[1:2]
-        made.append(silu(active))
-        upstream = grad[0, plane].astype(F32) * silu_slope(active)
-        first = first + jnp.sum(upstream, axis=0, keepdims=True)
-        second = second + jnp.sum(upstream * normed, axis=0, keepdims=True)
+        pieces = []
+        for rows in row_blocks(32):
+            normed = normalize(z[0, plane, rows], stats_in)
+            active = normed * scale[0:1] + scale[1:2]
+            sigma = jax.nn.sigmoid(active)
+            pieces.append(active * sigma)
+            upstream = grad[0, plane, rows].astype(F32) * (sigma * (1.0 + active * (1.0 - sigma)))
+            first = first + jnp.sum(upstream, axis=0, keepdims=True)
+            second = second + jnp.sum(upstream * normed, axis=0, keepdims=True)
+        made.append(jnp.concatenate(pieces, axis=0))
     sums[0, 0:1] = first
     sums[0, 1:2] = second
     to_voxels(decoded, made)
@@ -1047,13 +1246,14 @@
         return norm_back(upstream, normed, stats_in, sums_in, scale)
 
     for plane in range(planes):
-        spread_fine(spread, plane + 1, 1, 0, rounded(z[0, plane], grad[0, plane]))
+        make = lambda rows: rounded(z[0, plane, rows], grad[0, plane, rows])
+        spread_fine(spread, plane + 1, 1, 0, make)
     for flag, rim, rim_grad, plane in (
         (first, below, grad_below, 0),
         (last, above, grad_above, planes + 1),
     ):
-        values = rounded(rim[0], rim_grad[0])
-        spread_fine(spread, plane, 1, 0, at_edge(flag, values, jnp.zeros_like(values)))
+        make = lambda rows: rounded(rim[0, rows], rim_grad[0, rows])
+        spread_rim(spread_fine, spread, plane, 1, flag, make)
     unit = identity(FINE)
     for block in range(planes):
         fine = 2 * (block % depth) + block // depth
@@ -1069,29 +1269,32 @@
     first_sum, second_sum = 0.0, 0.0
     for block in range(planes):
         fine = 2 * (block % depth) + block // depth
-        normed = normalize(z_before[0, fine], stats_before)
-        slope = silu_slope(normed * scale_before[0:1] + scale_before[1:2])
-        values = given[block * CELLS : (block + 1) * CELLS] * slope
-        back[0, fine] = values
-        first_sum = first_sum + jnp.sum(values, axis=0, keepdims=True)
-        second_sum = second_sum + jnp.sum(values * normed, axis=0, keepdims=True)
+        for rows in row_blocks(32):
+            normed = normalize(z_before[0, fine, rows], stats_before)
+            slope = silu_slope(normed * scale_before[0:1] + scale_before[1:2])
+            begin = block * CELLS + rows.start
+            values = given[begin : begin + 32] * slope
+            back[0, fine, rows] = values
+            first_sum = first_sum + jnp.sum(values, axis=0, keepdims=True)
+            second_sum = second_sum + jnp.sum(values * normed, axis=0, keepdims=True)
     sums[0, 0:1] = first_sum
     sums[0, 1:2] = second_sum
 
     @pl.when(step == pl.num_programs(0) - 1)
     def _():
-        fine_kernel_grad(kernel_grad, totals, 1, False)
-
-
-def narrowed(values, low, column):
+        fine_kernel_grad(kernel_grad, totals, 1)
+
+
+def narrowed(first, second, low, column):
     lines = []
     for parity in range(2):
-        pair = values[:, parity * 128 : (parity + 1) * 128]
-        turned = pltpu.roll(pair, GROUP, 1)
-        later = jnp.where(column == HALF_WIDTH - 1, turned, pltpu.roll(pair, CELLS - 1, 0))
-        earlier = jnp.where(column == 0, turned, pltpu.roll(pair, 1, 0))
-        mixed = 0.75 * pair + 0.25 * jnp.where(low, later, earlier)
-        lines.append(mixed + pltpu.roll(mixed, GROUP, 1))
+        lanes = slice(parity * 2 * GROUP, (parity + 1) * 2 * GROUP)
+        one, two = first[:, lanes], second[:, lanes]
+        even = jnp.where(low, one, pltpu.roll(two, GROUP, 1))
+        odd = jnp.where(low, pltpu.roll(one, GROUP, 1), two)
+        later = jnp.where(column == HALF_WIDTH - 1, odd, pltpu.roll(even, CELLS - 1, 0))
+        earlier = jnp.where(column == 0, even, pltpu.roll(odd, 1, 0))
+        lines.append(0.75 * (even + odd) + 0.25 * (later + earlier))
     even, odd = lines
     later = jnp.concatenate([even[RIM:], odd[CELLS - RIM :]], axis=0)
     earlier = jnp.concatenate([even[:RIM], odd[: CELLS - RIM]], axis=0)
@@ -1139,10 +1342,10 @@
     gating,
     masks,
     kernel,
+    closing_grad,
     skip_back,
     coarse_back,
-    kernel_grad,
-    gate_grad,
+    packed,
     spread,
     stack,
     weights,
@@ -1171,13 +1374,14 @@
         return norm_back(upstream, normalize(values, stats_in), stats_in, sums_in, scale)
 
     for plane in range(planes):
-        spread_fine(spread, plane + 1, 1, 0, rounded(z[0, plane], grad[0, plane]))
+        make = lambda rows: rounded(z[0, plane, rows], grad[0, plane, rows])
+        spread_fine(spread, plane + 1, 1, 0, make)
     for flag, rim, rim_grad, plane in (
         (first, below, grad_below, 0),
         (last, above, grad_above, planes + 1),
     ):
-        values = rounded(rim[0], rim_grad[0])
-        spread_fine(spread, plane, 1, 0, at_edge(flag, values, jnp.zeros_like(values)))
+        make = lambda rows: rounded(rim[0, rows], rim_grad[0, rows])
+        spread_rim(spread_fine, spread, plane, 1, flag, make)
     unit = identity(FINE)
     width = 2 * GROUP
     order = [2 * (block % depth) + block // depth for block in range(planes)]
@@ -1241,15 +1445,17 @@
         lines = slice(block * CELLS, (block + 1) * CELLS)
         skip_back[0, fine] = skip_part[lines]
         left = jnp.concatenate([given[lines, width:FINE], given[lines, FINE + width : 2 * FINE]], axis=1)
-        left = narrowed(left + through_gate[lines, FINE : 2 * FINE], low, column)
+        left = left + through_gate[lines, FINE : 2 * FINE]
         right = given[lines, 2 * FINE :] + through_gate[lines, 2 * FINE :]
-        right = narrowed(right, low, column)
-        coarse_back[0, fine] = jnp.where(low, left, right)
+        coarse_back[0, fine] = narrowed(left, right, low, column)
 
     @pl.when(step == pl.num_programs(0) - 1)
     def _():
-        fine_kernel_grad(kernel_grad, totals, 3, True)
-        gate_gradient(gate_grad, gate_sums)
+        fine_kernel_grad(packed, totals, 3, closing_grad)
+        first, inner = 2 * closing_grad.shape[0] * GROUP, gating.shape[1]
+        gate_gradient(packed.at[first : first + 2 * inner], gate_sums)
+        rest = packed.shape[0] - first - 2 * inner
+        packed[first + 2 * inner :, :] = jnp.zeros((rest, 2 * GROUP), BF16)
 
 
 def coarse_grad_kernel(fine_back, below, above, z, stats_in, scales, back, sums):
@@ -1285,13 +1491,14 @@
         return norm_back(upstream, normalize(values, stats_in), stats_in, sums_in, scale)
 
     for plane in range(depth):
-        spread_coarse(spread, plane + 1, 2, rounded(z[0, plane], grad[0, plane]))
+        make = lambda rows: rounded(z[0, plane, rows], grad[0, plane, rows])
+        spread_coarse(spread, plane + 1, 2, make)
     for flag, rim, rim_grad, plane in (
         (first, rims[0], grad_rims[0], 0),
         (last, rims[1], grad_rims[1], depth + 1),
     ):
-        values = rounded(rim[0], rim_grad[0])
-        spread_coarse(spread, plane, 2, at_edge(flag, values, jnp.zeros_like(values)))
+        make = lambda rows: rounded(rim[0, rows], rim_grad[0, rows])
+        spread_rim(spread_coarse, spread, plane, 2, flag, make)
     stack_coarse(spread, masks, stack, 2, depth)
 
 
@@ -1364,6 +1571,50 @@
         coarse_kernel_grad(kernel_grad, totals, 2)
 
 
+def widening_with_sums(gathered, summed, counts, *refs):
+    inputs, outputs, scratch, _ = counts
+    ins, refs = refs[:inputs], refs[inputs:]
+    pieces, source, refs = refs[0], refs[1], refs[2:]
+    outs, refs = refs[:outputs], refs[outputs:]
+    total, pieces_out, refs = refs[0], refs[1], refs[2:]
+    own, refs = refs[:scratch], refs[scratch:]
+    step = pl.program_id(0)
+    plan = stats_plan()
+
+    @pl.when(step == 0)
+    def _():
+        greet(plan)
+
+    widening_back_kernel(*ins, *outs, *own)
+
+    @pl.when(step == 0)
+    def _():
+        await_greetings(plan)
+
+    gather = tuple(refs[:2])
+    scatter = (source,) + tuple(refs[2:])
+
+    def done():
+        total[...] = gather[0][...]
+
+    actions = [
+        [
+            lambda: gathered.load_pieces(pieces, gather[0], 1),
+            lambda: gathered.gather_start(gather, 0),
+            lambda: summed.scatter_start(scatter, 0),
+        ],
+        [lambda: summed.scatter_finish(scatter, 0), lambda: summed.scatter_start(scatter, 1)],
+        [lambda: summed.scatter_finish(scatter, 1), lambda: summed.scatter_start(scatter, 2)],
+        [
+            lambda: gathered.gather_finish(gather, 0),
+            done,
+            lambda: summed.scatter_finish(scatter, 2),
+            lambda: summed.store_pieces(scatter[1], pieces_out, 3),
+        ],
+    ]
+    in_steps(step, counts[3], actions)
+
+
 def widening_back_kernel(
     grad,
     grad_below,
@@ -1436,13 +1687,13 @@
     return (weight_next, momentum, smoothed, weight_next.astype(jnp.bfloat16))
 
 
-def update_kernel(grads, one, two, three, four, *refs):
+def update_kernel(first_grads, second_grads, third_grads, one, two, three, four, *refs):
     inputs, outs = refs[:18], refs[18:]
     step = pl.program_id(0)
     taps = inputs[0].shape[0]
     width = 2 * GROUP
 
-    def rows(first, count):
+    def rows(grads, first, count):
         begin = pl.multiple_of(first + step * taps * count, 16)
         return grads[pl.ds(begin, taps * count), :].astype(F32).reshape(taps, count, width)
 
@@ -1453,18 +1704,18 @@
             outs[6 * kind + index][...] = state[kind]
 
     base = 27 * GROUP
-    store(0, rows(0, GROUP), weight_decay, learning_rate)
-    store(1, rows(base, 2 * GROUP), weight_decay, learning_rate)
-    both = rows(4 * base, GROUP)
-    merged = jnp.concatenate([rows(3 * base, GROUP), both[:, :, :GROUP]], axis=2)
+    store(0, rows(first_grads, 0, GROUP), weight_decay, learning_rate)
+    store(1, rows(second_grads, 0, 2 * GROUP), weight_decay, learning_rate)
+    both = rows(third_grads, base, GROUP)
+    merged = jnp.concatenate([rows(third_grads, 0, GROUP), both[:, :, :GROUP]], axis=2)
     store(2, merged, weight_decay, learning_rate)
     store(3, both[:, :, GROUP:], weight_decay, learning_rate)
 
     @pl.when(step == 0)
     def _():
         inner, count = inputs[12].shape
-        first = grads[5 * base : 5 * base + inner, :].astype(F32)
-        second = grads[5 * base + inner : 5 * base + 2 * inner, :].astype(F32)
+        first = third_grads[2 * base : 2 * base + inner, :].astype(F32)
+        second = third_grads[2 * base + inner : 2 * base + 2 * inner, :].astype(F32)
         gate = jnp.concatenate([first, second[:, : count - width]], axis=1)
         store(4, gate, weight_decay, learning_rate)
         lines = [one[...], two[...], three[:, :GROUP], four[:, :GROUP]]
@@ -1474,7 +1725,7 @@
 
 def update(grads, sums, states):
     taps = states[0][0].shape[0]
-    steps = 9
+    steps = 3
     flat = [array for state in states for array in state]
 
     def spec(array):
@@ -1490,10 +1741,10 @@
         update_kernel,
         grid=(steps,),
         out_shape=outs,
-        in_specs=[WHOLE] * 5 + [spec(array) for array in flat],
+        in_specs=[WHOLE] * 7 + [spec(array) for array in flat],
         out_specs=[spec(array) for array in outs],
         compiler_params=params(dimension_semantics=("arbitrary",)),
-    )(grads, *sums, *flat)
+    )(*grads, *sums, *flat)
     return [[results[6 * kind + index] for kind in range(4)] for index in range(len(states))]
 
 
@@ -1535,7 +1786,17 @@
 
 
 def run_with_stats(
-    kernel, patches, inputs, outputs, scratch, stats_at, rims_of, moments, samples, number
+    kernel,
+    patches,
+    inputs,
+    outputs,
+    scratch,
+    stats_at,
+    rims_of,
+    moments,
+    samples,
+    number,
+    beside=None,
 ):
     plan = stats_plan()
     ndep, low, high = plan
@@ -1545,6 +1806,14 @@
     shapes = [array for array, _ in rest] + [shape(8, width)]
     specs = [by_patch(array) if spec is None else spec for array, spec in rest]
     specs.append(constant(shapes[-1]))
+    in_specs = [by_patch(array) if spec is None else spec for array, spec in inputs]
+    operands = [array for array, _ in inputs]
+    if beside is not None:
+        make, hook_operands, hook_shapes, hook_scratch = beside
+        operands += hook_operands
+        in_specs += [WHOLE] * len(hook_operands)
+        shapes += hook_shapes
+        specs += [constant(array) for array in hook_shapes]
     extra = [
         vmem(1, 8, width, dtype=F32),
         vmem(patches, 8, width, dtype=F32),
@@ -1557,20 +1826,42 @@
         specs += [pl.BlockSpec(memory_space=pl.ANY)] * 2
         extra.append(vmem(patches, 2, *rims.shape[2:], dtype=rims.dtype))
         extra.append(pltpu.SemaphoreType.DMA((4,)))
+    if beside is not None:
+        extra += hook_scratch
+        beside = (make, len(hook_operands), len(hook_shapes), len(hook_scratch))
     counts = (len(inputs), len(outputs), len(scratch))
     return pl.pallas_call(
         functools.partial(
-            with_stats, kernel, plan, moments, float(samples), counts, stats_at, rims_of
+            with_stats, kernel, plan, moments, float(samples), counts, stats_at, rims_of, beside
         ),
         grid=(patches,),
         out_shape=shapes,
-        in_specs=[by_patch(array) if spec is None else spec for array, spec in inputs],
+        in_specs=in_specs,
         out_specs=specs,
         scratch_shapes=list(scratch) + extra,
         compiler_params=params(
             dimension_semantics=("arbitrary",), collective_id=number, has_side_effects=True
         ),
-    )(*[array for array, _ in inputs])
+    )(*operands)
+
+
+def run_with_sums(gathered, pieces, summed, grads, number, patches, inputs, outputs, scratch):
+    shapes = [array for array, _ in outputs]
+    specs = [by_patch(array) if spec is None else spec for array, spec in outputs]
+    shapes += [shape(gathered.rows, 2 * GROUP, dtype=BF16), summed.pieces(3)]
+    specs += [constant(array) for array in shapes[-2:]]
+    counts = (len(inputs), len(outputs), len(scratch), patches)
+    return pl.pallas_call(
+        functools.partial(widening_with_sums, gathered, summed, counts),
+        grid=(patches,),
+        out_shape=shapes,
+        in_specs=[by_patch(array) if spec is None else spec for array, spec in inputs] + [WHOLE] * 2,
+        out_specs=specs,
+        scratch_shapes=list(scratch) + gathered.gather_scratch() + summed.scatter_scratch(),
+        compiler_params=params(
+            dimension_semantics=("arbitrary",), collective_id=number, has_side_effects=True
+        ),
+    )(*[array for array, _ in inputs], pieces, grads)
 
 
 def vmem(*sizes, dtype=BF16):
@@ -1712,6 +2003,7 @@
             fine_stack(3),
             vmem(3, 12 * FINE, FINE),
             vmem(3 * FINE, span),
+            vmem(planes + 2, CELLS, 2 * FINE),
         ],
         4,
         0,
@@ -1787,9 +2079,9 @@
         planes * CELLS,
         7,
     )
-    merging_shape = shape(*merging_turned.shape, dtype=BF16)
-    gate_shape = shape(2 * inner, 2 * GROUP, dtype=BF16)
-    skip_back, fine_back, merging_grad, gate_grad = run(
+    decoder_plan = GradSum(2 * merging.shape[0] * GROUP + 2 * inner)
+    decoder_shape = shape(decoder_plan.rows, 2 * GROUP, dtype=BF16)
+    skip_back, fine_back, decoder_grads = run(
         merging_back_kernel,
         patches,
         [
@@ -1809,12 +2101,12 @@
             (gating, WHOLE),
             masked,
             (merging_turned, WHOLE),
+            (closing_grad, WHOLE),
         ],
         [
             (fine, None),
             (shape(patches, planes, CELLS, 2 * GROUP), None),
-            (merging_shape, constant(merging_shape)),
-            (gate_shape, constant(gate_shape)),
+            (decoder_shape, constant(decoder_shape)),
         ],
         [
             fine_spread(1),
@@ -1828,7 +2120,7 @@
         ],
     )
     fine_below, fine_above = exchange_rims([fine_back], 8)
-    back_two, sums_two, back_below, back_above = run_with_stats(
+    back_two, sums_two, decoder_parts, back_below, back_above = run_with_stats(
         coarse_grad_kernel,
         patches,
         [
@@ -1846,9 +2138,16 @@
         False,
         depth * CELLS,
         9,
+        (
+            functools.partial(first_rounds, decoder_plan),
+            [decoder_grads],
+            [decoder_plan.pieces(2)],
+            decoder_plan.scatter_scratch(),
+        ),
     )
-    bottom_shape = shape(*bottom.shape, dtype=BF16)
-    back_one, bottom_grad, sums_one, back_below, back_above = run_with_stats(
+    bottom_plan = GradSum(bottom.shape[0] * bottom.shape[1])
+    bottom_shape = shape(bottom_plan.rows // bottom.shape[1], *bottom.shape[1:], dtype=BF16)
+    back_one, bottom_grad, sums_one, decoder_pieces, back_below, back_above = run_with_stats(
         bottom_back_kernel,
         patches,
         [
@@ -1879,10 +2178,21 @@
         False,
         depth * CELLS,
         10,
+        (
+            functools.partial(middle_rounds, decoder_plan),
+            [decoder_parts],
+            [decoder_plan.pieces(1)],
+            decoder_plan.gather_scratch() + decoder_plan.scatter_scratch(),
+        ),
     )
-    widening_shape = shape(*widening.shape, dtype=BF16)
-    skip_grad, widening_grad = run(
-        widening_back_kernel,
+    widening_plan = GradSum(widening.shape[0] * widening.shape[1])
+    widening_shape = shape(widening_plan.rows // widening.shape[1], *widening.shape[1:], dtype=BF16)
+    skip_grad, widening_grad, decoder_total, bottom_pieces = run_with_sums(
+        decoder_plan,
+        decoder_pieces,
+        bottom_plan,
+        bottom_grad.reshape(-1, 2 * GROUP),
+        12,
         patches,
         [
             (back_one, None),
@@ -1911,18 +2221,12 @@
         ],
     )
 
-    second_half = jnp.concatenate([merging_grad[:, :, 2 * GROUP :], closing_grad], axis=2)
-    parts = [
-        widening_grad.reshape(-1, 2 * GROUP),
-        bottom_grad.reshape(-1, 2 * GROUP),
-        merging_grad[:, :, : 2 * GROUP].reshape(-1, 2 * GROUP),
-        second_half.reshape(-1, 2 * GROUP),
-        gate_grad,
-    ]
-    total = all_reduce_grads(jnp.concatenate(parts, axis=0), 11)
+    bottom_total, widening_total = last_sums(
+        bottom_plan, bottom_pieces, widening_plan, widening_grad.reshape(-1, 2 * GROUP), 11
+    )
     turned = lambda *arrays: [jnp.swapaxes(array, -1, -2) for array in arrays]
     states = update(
-        total,
+        [widening_total, bottom_total, decoder_total],
         [sums_one, sums_two, sums_three, sums_four],
         [
             (widening, widening_velocity, widening_average),

time: 363 us -> 350 us (0.964)
  Pallas kernels: 349 us -> 338 us
    pallas_call x3 -> x2, Pallas kernels: 85.7 us -> 64.3 us  [run(): pl.pallas_call(kernel, grid=(patches,), out_shape=[array for array, _ in...]
    pallas_call x8, Pallas kernels: 194 us -> 202 us  [run_with_stats(): pl.pallas_call(functools.partial(with_stats, kernel, plan, moments, float...]
    pallas_call x1 -> x2, Pallas kernels: 43.9 us -> 49.4 us  [the longest x1 25.1 us: run_with_sums(): pl.pallas_call(functools.partial(widening_with_sums, gathered, summed, co...]
where the time goes in v4:
time: 350 us; the launch traced here: 346 us
  Pallas kernels  338 us (97%)
  local copies, waits for them, and re-layouts  6.46 us (2%)
    pallas_call x8, Pallas kernels, run_with_stats(): pl.pallas_call(functools.partial(with_stats, kernel, plan, moments, float...  202 us
    pallas_call x2, Pallas kernels, run(): pl.pallas_call(kernel, grid=(patches,), out_shape=[array for array, _ in...  64.3 us
    pallas_call x1, Pallas kernels, run_with_sums(): pl.pallas_call(functools.partial(widening_with_sums, gathered, summed, co...  25.1 us
    pallas_call x1, Pallas kernels, last_sums(): pl.pallas_call(functools.partial(last_sums_kernel, gathered, summed), out...  24.3 us
    pallas_call x1, Pallas kernels, update(): pl.pallas_call(update_kernel, grid=(steps,), out_shape=outs, in_specs=[WH...  15.7 us

profile of v4, /device:TPU:0, one launch (start us, length us, event | category | flops | bytes accessed | tf_op | source)
XLA Modules:
  0.0 345.6 jit_solution(9091036293995597458)
XLA Ops:
  0.7 1.5 copy.47.refs_8_.gating
  2.2 6.8 %shard_map.404 = (bf16[4,4,256,256]{3,2,1,0:T(8,128)(2,1)}, bf16[4,4,256,256]{3,2,1,0:T(8,128)(2,1)}, bf16[4,2,256,128]{3,2,1,0:T(8,128)(2,1)}, bf16[4,2,256,128]{3,2,1,0:T(8,128)(2,1)}) custom-call(bf16[4,64,4,1024]{3,2,1,0:T(4,128)(2,1)} %skip.1, bf16[4,64,4,1024]{3,2,1,0:T(4,128)(2,1)} %grad.1, s32[4,4,1024]{2,1,0:T(4,128)} %ids.1), custom_call_target="tpu_custom_call" | custom-call | tf_op jit(solution)/shard_map/pallas_call | solution.py:1772
  9.0 4.0 %shard_map.405 = (bf16[4,256,256]{2,1,0:T(8,128)(2,1)}, bf16[4,256,256]{2,1,0:T(8,128)(2,1)}, bf16[4,256,256]{2,1,0:T(8,128)(2,1)}, bf16[4,256,256]{2,1,0:T(8,12...) custom-call(bf16[4,4,256,256]{3,2,1,0:T(8,128)(2,1)} %get-tuple-elem, ...), custom_call_target="tpu_custom_call" | custom-call | tf_op jit(solution)/shard_map/pallas_call | solution.py:127
  13.0 20.1 %shard_map.406 = (f32[4,2,256,128]{3,2,1,0:T(8,128)}, bf16[9,4,512,256]{3,2,1,0:T(8,128)(2,1)}, f32[8,128]{1,0:T(8,128)}, f32[4,256,128]{2,1,0:T(8,128)}, f32[4,256,128]{2,1,0:T(8,128)}) custom-call(bf16[4,2,256,128]{3,2,1,0:T(8,128)(2,1)} %get-tuple-element.113.refs_2_.refs_0_.refs_9_, bf16[4,256,128]{2,1,0:T(8,128)(2,1)} %get-tuple-element.117.refs_1_, ...), custom_call_target="tpu_custom_call" | custom-call | tf_op jit(solution)/shard_map/pallas_call | solution.py:1833
  33.1 15.5 %shard_map.407 = (f32[4,2,256,128]{3,2,1,0:T(8,128)}, bf16[4,2,256,128]{3,2,1,0:T(8,128)(2,1)}, f32[8,128]{1,0:T(8,128)}, f32[4,256,128]{2,1,0:T(8,128)}, f32[4,256,128]{2,1,0:T(8,128)}) custom-call(f32[4,2,256,128]{3,2,1,0:T(8,128)} %get-tuple-element.121.refs_0_.refs_10_.refs_3_, f32[4,256,128]{2,1,0:T(8,128)} %get-tuple-element.122.refs_1_.refs_4_, ...), custom_call_target="tpu_custom_call" | custom-call | tf_op jit(solution)/shard_map/pallas_call | solution.py:1833
  48.7 54.2 %shard_map.408 = (f32[4,4,256,256]{3,2,1,0:T(8,128)}, bf16[4,4,256,256]{3,2,1,0:T(8,128)(2,1)}, bf16[4,4,256,512]{3,2,1,0:T(8,128)(2,1)}, f32[4,4,256,128]{3,2,1...) custom-call(f32[4,2,256,128]{3,2,1,0:T(8,128)} %get-tuple-element.126.refs_0_.refs_3_, ...), custom_call_target="tpu_custom_call" | custom-call | tf_op jit(solution)/shard_map/pallas_call | solution.py:1833
  102.9 20.6 %shard_map.409 = (f32[4,4,256,256]{3,2,1,0:T(8,128)}, bf16[4,4,256,256]{3,2,1,0:T(8,128)(2,1)}, f32[8,256]{1,0:T(8,128)}, f32[4,256,256]{2,1,0:T(8,128)}, f32[4,256,256]{2,1,0:T(8,128)}) custom-call(f32[4,4,256,256]{3,2,1,0:T(8,128)} %get-tuple-element.132.refs_0_.refs_10_.z, f32[4,256,256]{2,1,0:T(8,128)} %get-tuple-element.133.refs_1_.below, ...), custom_call_target="tpu_custom_call" | custom-call | tf_op jit(solution)/shard_map/pallas_call | solution.py:1833
  123.5 16.6 %shard_map.410 = (bf16[4,64,4,1024]{3,2,1,0:T(4,128)(2,1)}, f32[8,256]{1,0:T(8,128)}) custom-call(f32[4,4,256,256]{3,2,1,0:T(8,128)} %get-tuple-element.136.refs_0_, bf16[4,4,256,256]{3,2,1,0:T(8,128)(2,1)} %get-tuple-element.115.refs_1_.refs_3_, f32[8,256]{1,0:T(8,128)} %get-tuple-element.137.refs_2_.refs_6_, f32[2,384]{1,0:T(2,128)} %refs_15_.1), custom_call_target="tpu_custom_call" | custom-call | tf_op jit(solution)/shard_map/pallas_call | solution.py:1833
  140.2 29.8 %shard_map.411 = (f32[4,4,256,256]{3,2,1,0:T(8,128)}, bf16[27,64,64]{2,1,0:T(8,128)(2,1)}, f32[8,256]{1,0:T(8,128)}, f32[4,256,256]{2,1,0:T(8,128)}, f32[4,256,256]{2,1,0:T(8,128)}) custom-call(f32[4,4,256,256]{3,2,1,0:T(8,128)} %get-tuple-element.136.refs_0_, f32[4,256,256]{2,1,0:T(8,128)} %get-tuple-element.139.refs_1_, ...), custom_call_target="tpu_custom_call" | custom-call | tf_op jit(solution)/shard_map/pallas_call | solution.py:1833
  170.0 57.4 %shard_map.412 = (f32[4,4,256,256]{3,2,1,0:T(8,128)}, f32[4,4,256,128]{3,2,1,0:T(8,128)}, bf16[3584,128]{1,0:T(8,128)(2,1)}) custom-call(f32[4,4,256,256]{3,2,1,0:T(8,128)} %get-tuple-element.145.grad, f32[4,256,256]{2,1,0:T(8,128)} %get-tuple-element.146.grad_below, f32[4,256,256]{2,1,0:T(8,128)} %get-tuple-element.147.grad_above, ...), custom_call_target="tpu_custom_call" | custom-call | tf_op jit(solution)/shard_map/pallas_call | solution.py:1772
  227.5 2.3 shard_map.413
  229.8 18.0 %shard_map.414 = (f32[4,2,256,128]{3,2,1,0:T(8,128)}, f32[8,128]{1,0:T(8,128)}, bf16[448,128]{1,0:T(8,128)(2,1)}, f32[4,256,128]{2,1,0:T(8,128)}, f32[4,256,128]{2,1,0:T(8,128)}) custom-call(f32[4,4,256,128]{3,2,1,0:T(8,128)} %get-tuple-element.153.refs_0_, f32[4,256,128]{2,1,0:T(8,128)} %get-tuple-element.154.refs_1_, ...), custom_call_target="tpu_custom_call" | custom-call | tf_op jit(solution)/shard_map/pallas_call | solution.py:1833
  247.8 27.2 %shard_map.415 = (f32[4,2,256,128]{3,2,1,0:T(8,128)}, bf16[28,128,128]{2,1,0:T(8,128)(2,1)}, f32[8,128]{1,0:T(8,128)}, bf16[1792,128]{1,0:T(8,128)(2,1)}, f32[4,...) custom-call(f32[4,2,256,128]{3,2,1,0:T(8,128)} %get-tuple-element.157.refs_0_, f32[4,256,128]{2,1,0:T(8,128)} %get-tuple-element.158.refs_1_, ...), custom_call_target="tpu_custom_call" | custom-call | tf_op jit(solution)/shard_map/pallas_call | solution.py:1833
  275.1 25.1 %shard_map.416 = (f32[4,64,4,1024]{3,2,1,0:T(4,128)}, bf16[32,64,128]{2,1,0:T(8,128)(2,1)}, bf16[3584,128]{1,0:T(8,128)(2,1)}, bf16[112,128]{1,0:T(8,128)(2,1)}) custom-call(f32[4,2,256,128]{3,2,1,0:T(8,128)} %get-tuple-element.163.refs_0_, f32[4,256,128]{2,1,0:T(8,128)} %get-tuple-element.164.refs_1_, f32[4,256,128]{2,1,0:T(8,128)} %get-tuple-element.165.refs_2_, ...), custom_call_target="tpu_custom_call" | custom-call | tf_op jit(solution)/shard_map/pallas_call | solution.py:1854
  300.2 24.3 %shard_map.417 = (bf16[3584,128]{1,0:T(8,128)(2,1)}, bf16[2048,128]{1,0:T(8,128)(2,1)}) custom-call(bf16[112,128]{1,0:T(8,128)(2,1)} %get-tuple-element.171.pieces, bf16[2048,128]{1,0:T(8,128)(2,1)} %bitcast.22), custom_call_target="tpu_custom_call" | custom-call | tf_op jit(solution)/shard_map/pallas_call | solution.py:474
  324.5 0.0 copy-start.1
  324.5 15.7 %shard_map.418 = (f32[27,64,128]{2,1,0:T(8,128)}, f32[27,128,128]{2,1,0:T(8,128)}, f32[27,64,192]{2,1,0:T(8,128)}, f32[27,64,64]{2,1,0:T(8,128)}, f32[32,194]{1,...) custom-call(bf16[2048,128]{1,0:T(8,128)(2,1)} %get-tuple-element.173, ...), custom_call_target="tpu_custom_call" | custom-call | tf_op jit(solution)/shard_map/pallas_call | solution.py:1740
  340.2 0.0 copy-done.1
  340.2 0.0 copy-start
  340.2 1.3 copy.51
  341.5 1.6 copy-done
  343.1 2.0 copy.52
Async XLA Ops:
  324.5 15.7 %copy-start.1 = (bf16[4,64,4,1024]{3,2,1,0:T(4,128)(2,1)S(1)}, bf16[4,64,4,1024]{3,2,1,0:T(4,128)(2,1)}, u32[]{:S(2)}) copy-start(bf16[4,64,4,1024]{3,2,1,0:T(4,128)(2,1)} %get-tuple-element.226) | copy-start | bytes 6291460
  340.2 2.9 copy-start

commit v5 on v4

--- a/solution.py
+++ b/solution.py
@@ -836,15 +836,13 @@
     ).astype(BF16)
 
 
-def two_parts(values):
+def dot_exact(values, weights):
     high = values.astype(BF16)
-    return high, (values - high.astype(F32)).astype(BF16)
-
-
-def dot_exact(values, weights):
-    high, low = two_parts(values)
-    return jnp.dot(high, weights, preferred_element_type=F32) + jnp.dot(
-        low, weights, preferred_element_type=F32
+    low = (values - high.astype(F32)).astype(BF16)
+    return jnp.dot(
+        jnp.concatenate([high, low], axis=1),
+        jnp.concatenate([weights, weights], axis=0),
+        preferred_element_type=F32,
     )
 
 
@@ -1424,9 +1422,11 @@
     features = jnp.concatenate([skip[0, fine] for fine in order], axis=0)
     asked = jnp.concatenate([query[0, fine] for fine in order], axis=0)
     active = silu(asked)
-    high, rest = two_parts(active * gate_rows[1:2])
-    attention = jax.nn.sigmoid(dot(high, to_lanes) + dot(rest, to_lanes))
-    attention_span = jax.nn.sigmoid(dot(high, to_span) + dot(rest, to_span))
+    logits = dot_exact(
+        active * gate_rows[1:2], jnp.concatenate([to_lanes, to_span], axis=1)
+    )
+    attention = jax.nn.sigmoid(logits[:, :FINE])
+    attention_span = jax.nn.sigmoid(logits[:, FINE:])
     attended_back = jnp.concatenate([given[:, :width], given[:, FINE : FINE + width]], axis=1)
     attention_back = dot_exact(attended_back * features.astype(F32), from_lanes)
     logit_back = attention_back * attention_span * (1.0 - attention_span)

time: 350 us -> 346 us (0.989)
  Pallas kernels: 338 us -> 333 us
    pallas_call x8, Pallas kernels: 202 us -> 199 us  [run_with_stats(): pl.pallas_call(functools.partial(with_stats, kernel, plan, moments, float...]
where the time goes in v5:
time: 346 us; the launch traced here: 341 us
  Pallas kernels  333 us (96%)
  local copies, waits for them, and re-layouts  6.46 us (2%)
    pallas_call x8, Pallas kernels, run_with_stats(): pl.pallas_call(functools.partial(with_stats, kernel, plan, moments, float...  199 us
    pallas_call x2, Pallas kernels, run(): pl.pallas_call(kernel, grid=(patches,), out_shape=[array for array, _ in...  63 us
    pallas_call x1, Pallas kernels, run_with_sums(): pl.pallas_call(functools.partial(widening_with_sums, gathered, summed, co...  25.1 us
    pallas_call x1, Pallas kernels, last_sums(): pl.pallas_call(functools.partial(last_sums_kernel, gathered, summed), out...  24.3 us
    pallas_call x1, Pallas kernels, update(): pl.pallas_call(update_kernel, grid=(steps,), out_shape=outs, in_specs=[WH...  15.7 us

profile of v5, /device:TPU:0, one launch (start us, length us, event | category | flops | bytes accessed | tf_op | source)
XLA Modules:
  0.0 340.8 jit_solution(17508387376341809667)
XLA Ops:
  0.7 1.5 copy.47.refs_8_.gating
  2.2 6.8 %shard_map.404 = (bf16[4,4,256,256]{3,2,1,0:T(8,128)(2,1)}, bf16[4,4,256,256]{3,2,1,0:T(8,128)(2,1)}, bf16[4,2,256,128]{3,2,1,0:T(8,128)(2,1)}, bf16[4,2,256,128]{3,2,1,0:T(8,128)(2,1)}) custom-call(bf16[4,64,4,1024]{3,2,1,0:T(4,128)(2,1)} %skip.1, bf16[4,64,4,1024]{3,2,1,0:T(4,128)(2,1)} %grad.1, s32[4,4,1024]{2,1,0:T(4,128)} %ids.1), custom_call_target="tpu_custom_call" | custom-call | tf_op jit(solution)/shard_map/pallas_call | solution.py:1772
  9.0 4.0 %shard_map.405 = (bf16[4,256,256]{2,1,0:T(8,128)(2,1)}, bf16[4,256,256]{2,1,0:T(8,128)(2,1)}, bf16[4,256,256]{2,1,0:T(8,128)(2,1)}, bf16[4,256,256]{2,1,0:T(8,12...) custom-call(bf16[4,4,256,256]{3,2,1,0:T(8,128)(2,1)} %get-tuple-elem, ...), custom_call_target="tpu_custom_call" | custom-call | tf_op jit(solution)/shard_map/pallas_call | solution.py:127
  13.0 20.1 %shard_map.406 = (f32[4,2,256,128]{3,2,1,0:T(8,128)}, bf16[9,4,512,256]{3,2,1,0:T(8,128)(2,1)}, f32[8,128]{1,0:T(8,128)}, f32[4,256,128]{2,1,0:T(8,128)}, f32[4,256,128]{2,1,0:T(8,128)}) custom-call(bf16[4,2,256,128]{3,2,1,0:T(8,128)(2,1)} %get-tuple-element.113.refs_2_.refs_0_.refs_9_, bf16[4,256,128]{2,1,0:T(8,128)(2,1)} %get-tuple-element.117.refs_1_, ...), custom_call_target="tpu_custom_call" | custom-call | tf_op jit(solution)/shard_map/pallas_call | solution.py:1833
  33.1 15.5 %shard_map.407 = (f32[4,2,256,128]{3,2,1,0:T(8,128)}, bf16[4,2,256,128]{3,2,1,0:T(8,128)(2,1)}, f32[8,128]{1,0:T(8,128)}, f32[4,256,128]{2,1,0:T(8,128)}, f32[4,256,128]{2,1,0:T(8,128)}) custom-call(f32[4,2,256,128]{3,2,1,0:T(8,128)} %get-tuple-element.121.refs_0_.refs_10_.refs_3_, f32[4,256,128]{2,1,0:T(8,128)} %get-tuple-element.122.refs_1_.refs_4_, ...), custom_call_target="tpu_custom_call" | custom-call | tf_op jit(solution)/shard_map/pallas_call | solution.py:1833
  48.7 50.7 %shard_map.408 = (f32[4,4,256,256]{3,2,1,0:T(8,128)}, bf16[4,4,256,256]{3,2,1,0:T(8,128)(2,1)}, bf16[4,4,256,512]{3,2,1,0:T(8,128)(2,1)}, f32[4,4,256,128]{3,2,1...) custom-call(f32[4,2,256,128]{3,2,1,0:T(8,128)} %get-tuple-element.126.refs_0_.refs_3_, ...), custom_call_target="tpu_custom_call" | custom-call | tf_op jit(solution)/shard_map/pallas_call | solution.py:1833
  99.3 20.6 %shard_map.409 = (f32[4,4,256,256]{3,2,1,0:T(8,128)}, bf16[4,4,256,256]{3,2,1,0:T(8,128)(2,1)}, f32[8,256]{1,0:T(8,128)}, f32[4,256,256]{2,1,0:T(8,128)}, f32[4,256,256]{2,1,0:T(8,128)}) custom-call(f32[4,4,256,256]{3,2,1,0:T(8,128)} %get-tuple-element.132.refs_0_.refs_10_.z, f32[4,256,256]{2,1,0:T(8,128)} %get-tuple-element.133.refs_1_.below, ...), custom_call_target="tpu_custom_call" | custom-call | tf_op jit(solution)/shard_map/pallas_call | solution.py:1833
  120.0 16.6 %shard_map.410 = (bf16[4,64,4,1024]{3,2,1,0:T(4,128)(2,1)}, f32[8,256]{1,0:T(8,128)}) custom-call(f32[4,4,256,256]{3,2,1,0:T(8,128)} %get-tuple-element.136.refs_0_, bf16[4,4,256,256]{3,2,1,0:T(8,128)(2,1)} %get-tuple-element.115.refs_1_.refs_3_, f32[8,256]{1,0:T(8,128)} %get-tuple-element.137.refs_2_.refs_6_, f32[2,384]{1,0:T(2,128)} %refs_15_.1), custom_call_target="tpu_custom_call" | custom-call | tf_op jit(solution)/shard_map/pallas_call | solution.py:1833
  136.6 29.8 %shard_map.411 = (f32[4,4,256,256]{3,2,1,0:T(8,128)}, bf16[27,64,64]{2,1,0:T(8,128)(2,1)}, f32[8,256]{1,0:T(8,128)}, f32[4,256,256]{2,1,0:T(8,128)}, f32[4,256,256]{2,1,0:T(8,128)}) custom-call(f32[4,4,256,256]{3,2,1,0:T(8,128)} %get-tuple-element.136.refs_0_, f32[4,256,256]{2,1,0:T(8,128)} %get-tuple-element.139.refs_1_, ...), custom_call_target="tpu_custom_call" | custom-call | tf_op jit(solution)/shard_map/pallas_call | solution.py:1833
  166.5 56.2 %shard_map.412 = (f32[4,4,256,256]{3,2,1,0:T(8,128)}, f32[4,4,256,128]{3,2,1,0:T(8,128)}, bf16[3584,128]{1,0:T(8,128)(2,1)}) custom-call(f32[4,4,256,256]{3,2,1,0:T(8,128)} %get-tuple-element.145.grad, f32[4,256,256]{2,1,0:T(8,128)} %get-tuple-element.146.grad_below, f32[4,256,256]{2,1,0:T(8,128)} %get-tuple-element.147.grad_above, ...), custom_call_target="tpu_custom_call" | custom-call | tf_op jit(solution)/shard_map/pallas_call | solution.py:1772
  222.7 2.3 shard_map.413
  225.0 18.1 %shard_map.414 = (f32[4,2,256,128]{3,2,1,0:T(8,128)}, f32[8,128]{1,0:T(8,128)}, bf16[448,128]{1,0:T(8,128)(2,1)}, f32[4,256,128]{2,1,0:T(8,128)}, f32[4,256,128]{2,1,0:T(8,128)}) custom-call(f32[4,4,256,128]{3,2,1,0:T(8,128)} %get-tuple-element.153.refs_0_, f32[4,256,128]{2,1,0:T(8,128)} %get-tuple-element.154.refs_1_, ...), custom_call_target="tpu_custom_call" | custom-call | tf_op jit(solution)/shard_map/pallas_call | solution.py:1833
  243.0 27.2 %shard_map.415 = (f32[4,2,256,128]{3,2,1,0:T(8,128)}, bf16[28,128,128]{2,1,0:T(8,128)(2,1)}, f32[8,128]{1,0:T(8,128)}, bf16[1792,128]{1,0:T(8,128)(2,1)}, f32[4,...) custom-call(f32[4,2,256,128]{3,2,1,0:T(8,128)} %get-tuple-element.157.refs_0_, f32[4,256,128]{2,1,0:T(8,128)} %get-tuple-element.158.refs_1_, ...), custom_call_target="tpu_custom_call" | custom-call | tf_op jit(solution)/shard_map/pallas_call | solution.py:1833
  270.2 25.1 %shard_map.416 = (f32[4,64,4,1024]{3,2,1,0:T(4,128)}, bf16[32,64,128]{2,1,0:T(8,128)(2,1)}, bf16[3584,128]{1,0:T(8,128)(2,1)}, bf16[112,128]{1,0:T(8,128)(2,1)}) custom-call(f32[4,2,256,128]{3,2,1,0:T(8,128)} %get-tuple-element.163.refs_0_, f32[4,256,128]{2,1,0:T(8,128)} %get-tuple-element.164.refs_1_, f32[4,256,128]{2,1,0:T(8,128)} %get-tuple-element.165.refs_2_, ...), custom_call_target="tpu_custom_call" | custom-call | tf_op jit(solution)/shard_map/pallas_call | solution.py:1854
  295.4 24.3 %shard_map.417 = (bf16[3584,128]{1,0:T(8,128)(2,1)}, bf16[2048,128]{1,0:T(8,128)(2,1)}) custom-call(bf16[112,128]{1,0:T(8,128)(2,1)} %get-tuple-element.171.pieces, bf16[2048,128]{1,0:T(8,128)(2,1)} %bitcast.22), custom_call_target="tpu_custom_call" | custom-call | tf_op jit(solution)/shard_map/pallas_call | solution.py:474
  319.7 0.0 copy-start.1
  319.7 15.7 %shard_map.418 = (f32[27,64,128]{2,1,0:T(8,128)}, f32[27,128,128]{2,1,0:T(8,128)}, f32[27,64,192]{2,1,0:T(8,128)}, f32[27,64,64]{2,1,0:T(8,128)}, f32[32,194]{1,...) custom-call(bf16[2048,128]{1,0:T(8,128)(2,1)} %get-tuple-element.173, ...), custom_call_target="tpu_custom_call" | custom-call | tf_op jit(solution)/shard_map/pallas_call | solution.py:1740
  335.4 0.0 copy-done.1
  335.4 0.0 copy-start
  335.4 1.3 copy.51
  336.7 1.6 copy-done
  338.3 2.0 copy.52
Async XLA Ops:
  319.7 15.7 %copy-start.1 = (bf16[4,64,4,1024]{3,2,1,0:T(4,128)(2,1)S(1)}, bf16[4,64,4,1024]{3,2,1,0:T(4,128)(2,1)}, u32[]{:S(2)}) copy-start(bf16[4,64,4,1024]{3,2,1,0:T(4,128)(2,1)} %get-tuple-element.226) | copy-start | bytes 6291460
  335.4 2.9 copy-start
